TPU v7x, 32 devices: a whole 2x2x4 slice. The times are simulated.
32 devices in a mesh: req: 8 (over z, x), tp: 4 (over y, core).
Axes of the slice: x: 2, y: 2, z: 4, core: 2. Of those that a mesh axis runs over, the one named last changes fastest.
Arguments:
- tokens: bfloat16 [4096, 2560], P('req'), may hold values from -6 to 6
- lengths: int32 [8], P('req'), may hold values from 1 to 512, as said below
- page_slot: int32 [32], replicated, may hold values from 0 to 31, as said below
- trainer_layout: int32 [32], replicated, may hold values from 0 to 31, each once
- trainer_qkv: float32 [2560, 3840], P(('req', 'tp'))
- trainer_gateup: float32 [2560, 13824], P(('req', 'tp')), may hold values from -0.125 to 0.125
- attn_gain: float32 [2560], replicated, may hold values from 0.1 to 1.9
- ffn_gain: float32 [2560], replicated, may hold values from 0.1 to 1.9
- out_proj: bfloat16 [2560, 2560], P('tp'), may hold values from -0.125 to 0.125
- down_proj: bfloat16 [6912, 2560], P('tp'), may hold values from -0.078125 to 0.078125
Outputs:
- layer_out: bfloat16 [4096, 2560], P(('req', 'tp'))
- kv_cache: bfloat16 [32, 128, 1280], P('req', None, 'tp')
Inputs may be any that keep to these rules, and one draw needn't show every extreme that they name: `lengths`: heavy-tailed; some request has exactly 512. `page_slot`: a permutation; pool slot s belongs to request device s // 4; the 4 pages of one request belong to 4 different devices. `trainer_layout`: a permutation; shard s is the trainer shard on the device with index s over req and tp together.
All inputs are finite; a program needn't handle non-finite values.
Results may differ from a plain program's by a relative error of at most 0.0065.
The roundings to bfloat16 on the way count: a program that leaves them out, or rounds other values in their place, can miss the bound.
Values may be sent and summed in bfloat16 or wider, within the bound.
No kernel may reach another device: no remote copies, remote signals or barrier semaphores. Data moves between devices by JAX's collectives and lax.ppermute only.
A program may use at most 192 MiB of HBM per device.

v0:
```python
import jax
import jax.numpy as jnp
from jax import lax
from jax.sharding import PartitionSpec as P

HD = 80
PAGE = 128


eps_norm = 1e-05
theta_base = 10000.0


def normed(values, gain):
    scale = lax.rsqrt(jnp.mean(values * values, axis=-1, keepdims=True) + eps_norm)
    return (values * scale * gain).astype(jnp.bfloat16)


def rotary(field, head_dim):
    half = head_dim // 2
    count = field.shape[0]
    freq = theta_base ** (-jnp.arange(half, dtype=jnp.float32) * 2.0 / head_dim)
    angles = jnp.arange(count, dtype=jnp.float32)[:, None] * freq[None, :]
    cosine = jnp.cos(angles)[:, None, :]
    sine = jnp.sin(angles)[:, None, :]
    first = field[..., :half]
    second = field[..., half:]
    return jnp.concatenate(
        [first * cosine - second * sine, second * cosine + first * sine], axis=-1
    )


def body(
    tokens,
    lengths,
    page_slot,
    trainer_layout,
    trainer_qkv,
    trainer_gateup,
    attn_gain,
    ffn_gain,
    out_proj,
    down_proj,
):
    n_tp = lax.axis_size("tp")
    n_req = lax.axis_size("req")
    devices = n_tp * n_req
    rows_each = trainer_qkv.shape[0]
    seq_len = tokens.shape[0]
    model_dim = tokens.shape[1]
    head_dim = HD
    local_heads = out_proj.shape[0] // head_dim
    group_cols = trainer_qkv.shape[1] // n_tp
    local_kv = (group_cols // head_dim - local_heads) // 2
    group = local_heads // local_kv
    q_cols = local_heads * head_dim
    k_cols = local_kv * head_dim
    ff_local = down_proj.shape[0]
    qkv_half, gu_half = (
        lax.all_to_all(
            trainer_qkv.astype(jnp.bfloat16), "tp", split_axis=1, concat_axis=0, tiled=True
        ),
        lax.all_to_all(
            trainer_gateup.astype(jnp.bfloat16), "tp", split_axis=1, concat_axis=0, tiled=True
        ),
    )
    x_f = tokens.astype(jnp.float32)
    x_norm = normed(x_f, attn_gain)
    inverse = (
        jnp.zeros((devices,), jnp.int32)
        .at[trainer_layout]
        .set(jnp.arange(devices, dtype=jnp.int32))
    )
    qkv_all, gu_all = (
        lax.all_gather(qkv_half, "req", axis=0, tiled=True),
        lax.all_gather(gu_half, "req", axis=0, tiled=True),
    )
    qkv_weight = qkv_all.reshape(devices, rows_each, qkv_all.shape[1])[inverse].reshape(
        model_dim, qkv_all.shape[1]
    )
    gu_weight = gu_all.reshape(devices, rows_each, gu_all.shape[1])[inverse].reshape(
        model_dim, gu_all.shape[1]
    )
    joined = jnp.dot(x_norm, qkv_weight, preferred_element_type=jnp.float32)
    query = rotary(joined[:, :q_cols].reshape(seq_len, local_heads, head_dim), head_dim)
    keys = rotary(
        joined[:, q_cols : q_cols + k_cols].reshape(seq_len, local_kv, head_dim), head_dim
    )
    query16 = query.astype(jnp.bfloat16).reshape(seq_len, local_kv, group, head_dim)
    keys16 = keys.astype(jnp.bfloat16)
    values16 = (
        joined[:, q_cols + k_cols :].reshape(seq_len, local_kv, head_dim).astype(jnp.bfloat16)
    )
    scores = jnp.einsum(
        "qkgd,skd->kgqs", query16, keys16, preferred_element_type=jnp.float32
    ) * head_dim ** (-0.5)
    slots = jnp.arange(seq_len, dtype=jnp.int32)
    length = lengths[0]
    allowed = (slots[None, :] <= slots[:, None]) & (slots[None, :] < length)
    scores = jnp.where(allowed[None, None], scores, -1e30)
    probs = jax.nn.softmax(scores, axis=-1).astype(jnp.bfloat16)
    context = jnp.einsum(
        "kgqs,skd->qkgd", probs, values16, preferred_element_type=jnp.float32
    ).astype(jnp.bfloat16)
    partial_out = jnp.dot(
        context.reshape(seq_len, q_cols), out_proj, preferred_element_type=jnp.float32
    )
    share = seq_len // n_tp
    tp_index = lax.axis_index("tp")
    mixed = lax.psum(partial_out, "tp")
    resid = x_f + mixed
    h_norm = normed(resid, ffn_gain)
    resid_share = lax.dynamic_slice_in_dim(resid, tp_index * share, share, 0)
    projected = jnp.dot(h_norm, gu_weight, preferred_element_type=jnp.float32)
    hidden = (jax.nn.silu(projected[:, :ff_local]) * projected[:, ff_local:]).astype(jnp.bfloat16)
    down = jnp.dot(hidden, down_proj, preferred_element_type=jnp.float32)
    added = lax.psum_scatter(down, "tp", scatter_dimension=0, tiled=True)
    share_slots = tp_index * share + jnp.arange(share, dtype=jnp.int32)
    live_share = (share_slots < length).astype(jnp.float32)
    layer_out = ((resid_share + added) * live_share[:, None]).astype(jnp.bfloat16)
    live_rows = (slots < length)[:, None]
    key_rows = keys16.reshape(seq_len, k_cols)
    value_rows = values16.reshape(seq_len, k_cols)
    cache_rows = jnp.concatenate(
        [
            jnp.where(live_rows, key_rows, jnp.zeros_like(key_rows)),
            jnp.where(live_rows, value_rows, jnp.zeros_like(value_rows)),
        ],
        axis=1,
    )
    pages = cache_rows.reshape(seq_len // PAGE, PAGE, 2 * k_cols)
    pool_size = pages.shape[0]
    owner = lax.axis_index("req")
    targets = owner * pool_size + jnp.arange(pool_size, dtype=jnp.int32)
    picks = (page_slot[:, None] == targets[None, :]).astype(jnp.bfloat16)
    pool = jnp.einsum(
        "np,nsc->psc",
        picks,
        lax.all_gather(pages, "req", axis=0, tiled=True),
        preferred_element_type=jnp.float32,
    )
    kv_cache = pool.astype(jnp.bfloat16)
    return (layer_out, kv_cache)


def solution(mesh):
    return jax.shard_map(
        body,
        mesh=mesh,
        in_specs=(
            P("req", None),
            P("req"),
            P(),
            P(),
            P(("req", "tp"), None),
            P(("req", "tp"), None),
            P(),
            P(),
            P("tp", None),
            P("tp", None),
        ),
        out_specs=(P(("req", "tp"), None), P("req", None, "tp")),
        check_vma=False,
    )
```

profile of v0, /device:TPU:0, one launch (start us, length us, event | category | flops | bytes accessed | tf_op | source)
XLA Modules:
  0.0 732.0 jit_solution(17733383014808575585)
XLA Ops:
  7.2 0.0 copy-start
  7.2 0.0 copy-start.9
  7.2 0.0 all-gather.4.cloned.1.call-start
  7.2 2.3 convert_element_type.60
  9.6 3.0 all_to_all.28
  12.6 1.3 copy.20
  13.9 14.4 %all_to_all.38 = bf16[80,4,960]{2,0,1:T(8,128)(2,1)} all-to-all(bf16[80,4,960]{2,0,1:T(8,128)(2,1)S(1)} %copy.20), channel_id=1, replica_groups=mesh['req'=8,'tp'=4] {'tp'}, dimensions={1} | all-to-all | bytes 1228800 | tf_op jit(solution)/shard_map/all_to_all | solution.py:60
  28.3 0.0 all-gather.4.cloned.1.call-update
  28.3 0.0 all-reduce.2.cloned.1.call-start
  29.0 0.7 scatter_custom_fusion
  29.8 2.3 fusion.2
  32.1 0.4 fusion.35
  32.5 0.9 fusion.26
  33.3 82.1 %all-gather.4.cloned.1.call-done = bf16[2560,960]{1,0:T(8,128)(2,1)} async-done(((bf16[320,960]{1,0:T(8,128)(2,1)}), bf16[2560,960]{1,0:T(8,128)(2,1)}) %all-gather.4.cloned.1.call-update) | async-done | bytes 4915216 | tf_op jit(solution)/shard_map/all_gather | solution.py:75
  115.4 5.7 gather_fusion
  121.2 6.2 fusion.11
  127.3 0.7 select_bitcast_fusion
  128.1 0.1 slice.44
  128.2 1.0 subtract_convert_fusion
  129.2 0.7 multiply_subtract_fusion
  129.9 7.6 %fusion.49 = (f32[2,4,512]{2,1,0:T(4,128)S(1)}, f32[2,4,512,512]{2,3,1,0:T(8,128)}) fusion(pred[512,512]{0,1:T(8,128)(4,1)} %fusion.26, bf16[512,2,4,40]{0,3,2,1:T(8,128)(2,1)} %bitcast.83, bf16[512,2,4,40]{0,3,2,1:T(8,128)(2,1)} %bitcast.82, bf16[512,2,40]{0,2,1:T(8,128)(2,1)} %get-tuple-element.17, bf16[512,2,40]{0,2,1:T(8,128)(2,1)S(1)} %get-tuple-element.16), kind=kOutput, calls=%fused_computation.77 | convolution fusion | flops 345571840 | bytes 9486336 | tf_op jit(solution)/shard_map/sub | solution.py:101
  137.5 4.2 fusion.22
  141.7 4.6 fusion.54
  146.4 0.0 all-reduce.2.cloned.1.call-update
  146.4 0.0 all-gather.6.cloned.1.call-start
  146.5 2.5 convert_element_type.68
  149.0 0.2 copy.39
  149.1 0.0 copy-start.2
  149.1 54.4 %all_to_all.39 = bf16[80,4,3456]{2,0,1:T(8,128)(2,1)} all-to-all(bf16[80,4,3456]{2,0,1:T(8,128)(2,1)S(1)} %bitcast.74), channel_id=1, replica_groups=mesh['req'=8,'tp'=4] {'tp'}, dimensions={1} | all-to-all | bytes 4423680 | tf_op jit(solution)/shard_map/all_to_all | solution.py:63
  203.6 0.0 all-gather.6.cloned.1.call-update
  203.6 0.0 all-gather.8.cloned.1.call-start
  203.7 0.0 copy-done.3
  203.8 0.7 pad_maximum_fusion.7
  204.6 0.0 all-gather.8.cloned.1.call-update
  204.6 0.2 reduce-scatter.2.cloned.1.call-start
  204.8 66.2 %all-reduce.2.cloned.1.call-done = f32[512,2560]{1,0:T(8,128)} async-done(((f32[512,2560]{1,0:T(8,128)}), f32[512,2560]{1,0:T(8,128)}) %all-reduce.2.cloned.1.call-update) | async-done | bytes 5242896 | tf_op jit(solution)/shard_map/psum | solution.py:110
  271.0 0.0 copy-done.2
  271.0 5.5 multiply_reduce_fusion
  276.5 336.6 %all-gather.6.cloned.1.call-done = bf16[2560,3456]{1,0:T(8,128)(2,1)} async-done(((bf16[320,3456]{1,0:T(8,128)(2,1)}), bf16[2560,3456]{1,0:T(8,128)(2,1)}) %all-gather.6.cloned.1.call-update) | async-done | bytes 17694736 | tf_op jit(solution)/shard_map/all_gather | solution.py:76
  613.1 13.7 %gather_fusion.1 = bf16[32,80,3456]{2,1,0:T(8,128)(2,1)} fusion(bf16[32,80,3456]{2,1,0:T(8,128)(2,1)} %bitcast.70, s32[1024]{0:T(1024)S(1)} %pad_clamp_fusion), kind=kCustom, calls=%fused_computation.1 | custom fusion | bytes 35389568 | tf_op jit(solution)/shard_map/gather | solution.py:81
  626.8 15.4 %fusion.10 = f32[512,3456]{1,0:T(8,128)S(1)} fusion(bf16[2560,3456]{1,0:T(8,128)(2,1)} %bitcast.71, f32[512,2560]{1,0:T(8,128)} %get-tuple-element.13, f32[2560]{0:T(1024)S(1)} %copy-done.8, f32[512]{0:T(512)S(1)} %add_rsqrt_fusion), kind=kOutput, calls=%fused_computation.22 | convolution fusion | flops 9063628800 | bytes 30027776 | tf_op jit(solution)/shard_map/dot_general | solution.py:114
  642.2 10.7 %fusion.19 = f32[512,2560]{1,0:T(8,128)} fusion(bf16[1728,2560]{1,0:T(8,128)(2,1)} %param.19, f32[512,3456]{1,0:T(8,128)S(1)} %fusion.10), kind=kOutput, calls=%fused_computation.31 | convolution fusion | flops 4535156736 | bytes 21430272 | tf_op jit(solution)/shard_map/dot_general | solution.py:116
  653.0 0.0 reduce-scatter.2.cloned.1.call-update
  653.0 17.4 %all-gather.8.cloned.1.call-done = bf16[32,128,320]{1,2,0:T(8,128)(2,1)} async-done(((bf16[4,128,320]{1,2,0:T(8,128)(2,1)}), bf16[32,128,320]{1,2,0:T(8,128)(2,1)}) %all-gather.8.cloned.1.call-update) | async-done | bytes 2621456 | tf_op jit(solution)/shard_map/all_gather | solution.py:139
  670.4 3.3 fusion.23
  673.7 0.8 copy.26
  674.4 48.3 %reduce-scatter.2.cloned.1.call-done = f32[128,2560]{1,0:T(8,128)} async-done(((f32[512,2560]{1,0:T(8,128)}), f32[128,2560]{1,0:T(8,128)}) %reduce-scatter.2.cloned.1.call-update) | async-done | bytes 1310736 | tf_op jit(solution)/shard_map/reduce_scatter | solution.py:117
  722.8 2.7 multiply_convert_fusion.2
  (31 shorter events, 0.2 us)
Async XLA Ops:
  7.2 134.6 %copy-start = (bf16[640,2560]{1,0:T(8,128)(2,1)S(1)}, bf16[640,2560]{1,0:T(8,128)(2,1)}, u32[]{:S(2)}) copy-start(bf16[640,2560]{1,0:T(8,128)(2,1)} %param.18) | copy-start | bytes 9830404
  7.2 21.8 %copy-start.9 = (s32[32]{0:T(128)S(1)}, s32[32]{0:T(128)}, u32[]{:S(2)}) copy-start(s32[32]{0:T(128)} %param.13) | copy-start | bytes 388
  7.2 108.2 %all-gather.4.cloned.1.call-start = ((), (), s32[]{:S(2)}) async-start(), calls=%async_computation.3 | async-start | bytes 5898240 | tf_op jit(solution)/shard_map/all_gather | solution.py:75
  28.3 242.7 %all-reduce.2.cloned.1.call-start = ((), (), s32[]{:S(2)}) async-start(), calls=%async_computation.4 | async-start | bytes 10485760 | tf_op jit(solution)/shard_map/psum | solution.py:110
  115.4 5.7 copy-start.7
  129.9 7.6 %copy-start.5 = (bf16[512,160]{0,1:T(8,128)(2,1)S(1)}, bf16[512,160]{0,1:T(8,128)(2,1)}, u32[]{:S(2)}) copy-start(bf16[512,160]{0,1:T(8,128)(2,1)} %get-tuple-element.11) | copy-start | bytes 491524
  146.4 466.7 %all-gather.6.cloned.1.call-start = ((), (), s32[]{:S(2)}) async-start(), calls=%async_computation.5 | async-start | bytes 19906560 | tf_op jit(solution)/shard_map/all_gather | solution.py:76
  148.9 54.7 %copy-start.3 = (bf16[20,4,8,128]{3,2,1,0:T(8,128)(2,1)S(1)}, bf16[20,4,8,128]{3,2,1,0:T(8,128)(2,1)}, u32[]{:S(2)}) copy-start(bf16[20,4,8,128]{3,2,1,0:T(8,128)(2,1)} %get-tuple-element.10) | copy-start | bytes 491524
  149.0 54.8 %copy-start.4 = (bf16[512,2,40]{0,2,1:T(8,128)(2,1)S(1)}, bf16[512,2,40]{0,2,1:T(8,128)(2,1)}, u32[]{:S(2)}) copy-start(bf16[512,2,40]{0,2,1:T(8,128)(2,1)} %get-tuple-element.17) | copy-start | bytes 245764
  149.1 121.9 %copy-start.2 = (bf16[512,2560]{1,0:T(8,128)(2,1)S(1)}, bf16[512,2560]{1,0:T(8,128)(2,1)}, u32[]{:S(2)}) copy-start(bf16[512,2560]{1,0:T(8,128)(2,1)} %param.10) | copy-start | bytes 7864324
  203.6 466.8 %all-gather.8.cloned.1.call-start = ((), (), s32[]{:S(2)}) async-start(), calls=%async_computation.7 | async-start | bytes 2949120 | tf_op jit(solution)/shard_map/all_gather | solution.py:139
  204.6 518.2 %reduce-scatter.2.cloned.1.call-start = ((), (), s32[]{:S(2)}) async-start(), calls=%async_computation.6 | async-start | bytes 6553600 | tf_op jit(solution)/shard_map/reduce_scatter | solution.py:117
  613.1 13.7 %copy-start.8 = (f32[2560]{0:T(1024)S(1)}, f32[2560]{0:T(1024)}, u32[]{:S(2)}) copy-start(f32[2560]{0:T(1024)} %param.17) | copy-start | bytes 30724
  653.0 17.4 %copy-start.6 = (s32[32]{0:T(128)S(1)}, s32[32]{0:T(128)}, u32[]{:S(2)}) copy-start(s32[32]{0:T(128)} %param.12) | copy-start | bytes 388
  653.0 72.5 %copy-start.1 = (bf16[640,2560]{1,0:T(8,128)(2,1)S(1)}, bf16[640,2560]{1,0:T(8,128)(2,1)}, u32[]{:S(2)}) copy-start(bf16[640,2560]{1,0:T(8,128)(2,1)} %param.18) | copy-start | bytes 9830404
Sparse Core Ops, SparseCore 0:
  28.4 86.9 all-gather.3
  146.5 124.4 all-reduce.1
  272.6 340.4 all-gather.5
  615.7 54.6 all-gather.7
  672.7 49.9 reduce-scatter.1
where the time goes:
time: 733 us; the launch traced here: 732 us
  waiting for transfers between devices  551 us (75%)
  blocking collectives  68.8 us (9%)
  matrix products  52 us (7%)
  local copies, waits for them, and re-layouts  25.6 us (3%)
  other arithmetic  19.8 us (3%)
  between operations  14.7 us (2%)
    all_gather x1, waiting for transfers between devices, body(): lax.all_gather(gu_half, 'req', axis=0, tiled=True)  337 us
    all_gather x1, waiting for transfers between devices, body(): lax.all_gather(qkv_half, 'req', axis=0, tiled=True)  82.1 us
    psum x1, waiting for transfers between devices, body(): mixed = lax.psum(partial_out, 'tp')  66.2 us
    all_to_all x1, blocking collectives, body(): lax.all_to_all(trainer_gateup.astype(jnp.bfloat16), 'tp', split_axis=1, c...  54.4 us
    reduce_scatter x1, waiting for transfers between devices, body(): added = lax.psum_scatter(down, 'tp', scatter_dimension=0, tiled=True)  48.3 us
    all_gather x1, waiting for transfers between devices, body(): lax.all_gather(pages, 'req', axis=0, tiled=True)  17.4 us
    dot_general x1, matrix products, body(): projected = jnp.dot(h_norm, gu_weight, preferred_element_type=jnp.float32)  15.4 us
  transfers between devices with their start and end apart: 5, of which 5 were waited for; matrix products, arithmetic and copies ran while one was open for 8% of the time, Pallas kernels for 0%

commit v1 on v0

v1 whole, which is shorter than its diff:
```python
import jax
import jax.numpy as jnp
import numpy as np
from jax import lax
from jax.sharding import PartitionSpec as P

HD = 80
PAGE = 128
BF = jnp.bfloat16
F32 = jnp.float32

eps_norm = 1e-05
theta_base = 10000.0

PAIR = 2
CHUNKS = (320, 320)


def normed(values, gain):
    scale = lax.rsqrt(jnp.mean(values * values, axis=-1, keepdims=True) + eps_norm)
    return (values * scale * gain).astype(BF)


def rotary(field, head_dim):
    half = head_dim // 2
    count = field.shape[0]
    freq = theta_base ** (-jnp.arange(half, dtype=F32) * 2.0 / head_dim)
    angles = jnp.arange(count, dtype=F32)[:, None] * freq[None, :]
    cosine = jnp.cos(angles)[:, None, :]
    sine = jnp.sin(angles)[:, None, :]
    first = field[..., :half]
    second = field[..., half:]
    return jnp.concatenate(
        [first * cosine - second * sine, second * cosine + first * sine], axis=-1
    )


def dot(a, b):
    return jnp.dot(a, b, preferred_element_type=F32)


def body(
    tokens,
    lengths,
    page_slot,
    trainer_layout,
    trainer_qkv,
    trainer_gateup,
    attn_gain,
    ffn_gain,
    out_proj,
    down_proj,
):
    n_tp = lax.axis_size("tp")
    n_req = lax.axis_size("req")
    devices = n_tp * n_req
    req = lax.axis_index("req")
    tp = lax.axis_index("tp")
    rows_each = trainer_qkv.shape[0]
    seq_len, model_dim = tokens.shape
    head_dim = HD
    local_heads = out_proj.shape[0] // head_dim
    group_cols = trainer_qkv.shape[1] // n_tp
    local_kv = (group_cols // head_dim - local_heads) // 2
    group = local_heads // local_kv
    q_cols = local_heads * head_dim
    k_cols = local_kv * head_dim
    ff_local = down_proj.shape[0]
    share = seq_len // n_tp

    def swap(value, req_mask, tp_mask):
        pairs = [(d, d ^ (req_mask * n_tp + tp_mask)) for d in range(devices)]
        return lax.ppermute(value, ("req", "tp"), pairs)

    def pick(stack, index):
        return lax.dynamic_index_in_dim(stack, index, 0, keepdims=False)

    def to_groups(blocks):
        lead, (rows, columns) = blocks.shape[1:-2], blocks.shape[-2:]
        held = jnp.zeros(lead + (n_tp, rows, columns), blocks.dtype)
        for s in range(n_tp):
            mine = pick(blocks, tp ^ s)
            if s:
                mine = swap(mine, 0, s)
            held = lax.dynamic_update_slice_in_dim(
                held, jnp.expand_dims(mine, len(lead)), tp ^ s, len(lead)
            )
        return held.reshape(lead + (n_tp * rows, columns))

    qkv_blocks = trainer_qkv.astype(BF).reshape(rows_each, n_tp, group_cols).transpose(1, 0, 2)
    qkv_own = to_groups(qkv_blocks)

    def gather_rows(block_for):
        out = []
        for g in range(0, n_req, 2):
            block = block_for(g)
            if g:
                block = swap(block, g, 0)
            out.append(block)
            out.append(swap(block, 1, 0))
        return out

    qkv_parts = gather_rows(lambda g: qkv_own)

    order = jnp.arange(n_req, dtype=jnp.int32) ^ req
    shards = (order[:, None] * n_tp + jnp.arange(n_tp, dtype=jnp.int32)[None, :]).reshape(-1)
    blocks_at = trainer_layout[shards]
    columns_at = (
        blocks_at[:, None] * rows_each + jnp.arange(rows_each, dtype=jnp.int32)[None, :]
    ).reshape(-1)
    onehot = (jnp.arange(model_dim, dtype=jnp.int32)[:, None] == columns_at[None, :]).astype(BF)
    tokens_in = dot(tokens, onehot)
    attn_gain_in = attn_gain.reshape(devices, rows_each)[blocks_at].reshape(-1)
    ffn_gain_in = ffn_gain.reshape(devices, rows_each)[blocks_at].reshape(-1)
    out_in = dot(out_proj, onehot).astype(BF)
    x_norm = normed(tokens_in, attn_gain_in)

    half = n_tp // 2
    out_rel = [out_in] + [None] * (n_tp - 1)
    step = 1
    bits = []
    while step < n_tp:
        bits.append(step)
        step *= 2
    have = [0]
    for bit in reversed(bits):
        for s in list(have):
            out_rel[s ^ bit] = swap(out_rel[s], 0, bit)
            have.append(s ^ bit)

    halves = 2
    units = ff_local // halves
    chunks = list(CHUNKS) + [units - sum(CHUNKS)]
    my_class = (req // PAIR) % 2
    gu = trainer_gateup.astype(BF).reshape(rows_each, n_tp, 2, halves, units)
    chunk_weights = []
    start = 0
    for size in chunks:
        part = gu[..., start : start + size].transpose(1, 3, 0, 2, 4)
        part = to_groups(part.reshape(n_tp, halves, rows_each, 2 * size))
        mine = pick(part, my_class)
        other = pick(part, 1 - my_class)
        chunk_weights.append(gather_rows(lambda g: other if g & PAIR else mine))
        start += size

    joined = dot(x_norm, jnp.concatenate(qkv_parts, axis=0))
    query = rotary(joined[:, :q_cols].reshape(seq_len, local_heads, head_dim), head_dim)
    keys = rotary(
        joined[:, q_cols : q_cols + k_cols].reshape(seq_len, local_kv, head_dim), head_dim
    )
    query16 = query.astype(BF).reshape(seq_len, local_kv, group, head_dim)
    keys16 = keys.astype(BF)
    values16 = joined[:, q_cols + k_cols :].reshape(seq_len, local_kv, head_dim).astype(BF)
    scores = jnp.einsum(
        "qkgd,skd->kgqs", query16, keys16, preferred_element_type=F32
    ) * head_dim ** (-0.5)
    slots = jnp.arange(seq_len, dtype=jnp.int32)
    length = lengths[0]
    allowed = (slots[None, :] <= slots[:, None]) & (slots[None, :] < length)
    scores = jnp.where(allowed[None, None], scores, -1e30)
    probs = jax.nn.softmax(scores, axis=-1).astype(BF)
    context = jnp.einsum(
        "kgqs,skd->qkgd", probs, values16, preferred_element_type=F32
    ).astype(BF)

    by_share = context.reshape(n_tp, share, q_cols)
    mixed = 0.0
    for s in range(n_tp):
        piece = pick(by_share, tp ^ s)
        if s:
            piece = swap(piece, 0, s)
        mixed = mixed + dot(piece, out_rel[s])
    resid_in = lax.dynamic_slice_in_dim(tokens_in, tp * share, share, 0) + mixed
    h_share = normed(resid_in, ffn_gain_in)

    coarse = resid_in.astype(BF)
    fine = (resid_in - coarse.astype(F32)).astype(BF)
    back = (((1,), (1,)), ((), ()))
    resid = lax.dot_general(coarse, onehot, back, preferred_element_type=F32) + lax.dot_general(
        fine, onehot, back, preferred_element_type=F32
    )

    cross = n_tp // 2
    rest = n_tp // 2
    own = [None] * n_tp
    theirs = [None] * n_tp
    own[0] = h_share
    own[cross] = swap(h_share, 0, cross)
    theirs[0] = swap(h_share, PAIR, 0)
    cut = share // 2
    theirs[cross] = jnp.concatenate(
        [swap(theirs[0][:cut], 0, cross), swap(own[cross][cut:], PAIR, 0)], axis=0
    )
    for s in range(1, rest):
        for base in (0, cross):
            own[base ^ s] = swap(own[base], 0, s)
            theirs[base ^ s] = swap(theirs[base], 0, s)
    h_own = jnp.concatenate(own, axis=0)
    h_theirs = jnp.concatenate(theirs, axis=0)
    width = model_dim // n_req
    h_theirs = jnp.concatenate(
        [h_theirs[:, (j ^ PAIR) * width : ((j ^ PAIR) + 1) * width] for j in range(n_req)], axis=1
    )
    h_all = jnp.concatenate([h_own, h_theirs], axis=0)

    down_rel = jnp.roll(down_proj.reshape(halves, units, model_dim), -my_class, axis=0)
    down = 0.0
    start = 0
    for size, parts in zip(chunks, chunk_weights):
        projected = dot(h_all, jnp.concatenate(parts, axis=0))
        hidden = (jax.nn.silu(projected[:, :size]) * projected[:, size:]).astype(BF)
        returned = swap(hidden[seq_len:], PAIR, 0)
        down = (
            down
            + dot(hidden[:seq_len], down_rel[0, start : start + size])
            + dot(returned, down_rel[1, start : start + size])
        )
        start += size

    down = down.reshape(n_tp, share, model_dim)
    keep = [down[s] for s in range(n_tp)]
    for bit in bits:
        keep = [
            keep[i] + swap(keep[i + 1].astype(BF), 0, bit).astype(F32)
            for i in range(0, len(keep), 2)
        ]
    added = keep[0]
    share_slots = tp * share + jnp.arange(share, dtype=jnp.int32)
    live_share = (share_slots < length).astype(F32)
    layer_out = ((resid + added) * live_share[:, None]).astype(BF)

    live_rows = (slots < length)[:, None]
    key_rows = keys16.reshape(seq_len, k_cols)
    value_rows = values16.reshape(seq_len, k_cols)
    cache_rows = jnp.concatenate(
        [
            jnp.where(live_rows, key_rows, jnp.zeros_like(key_rows)),
            jnp.where(live_rows, value_rows, jnp.zeros_like(value_rows)),
        ],
        axis=1,
    )
    pages = cache_rows.reshape(seq_len // PAGE, PAGE, 2 * k_cols)
    pool_size = pages.shape[0]
    holders = lax.dynamic_slice_in_dim(page_slot, req * pool_size, pool_size, 0) // pool_size
    arrived = []
    for r in range(n_req):
        sent = pick(pages, jnp.argmax(holders == (req ^ r)))
        arrived.append(swap(sent, r, 0) if r else sent)
    targets = req * pool_size + jnp.arange(pool_size, dtype=jnp.int32)
    source = jnp.argmax(page_slot[None, :] == targets[:, None], axis=1) // pool_size
    kv_cache = jnp.stack(arrived)[source ^ req]
    return (layer_out, kv_cache)


def solution(mesh):
    return jax.shard_map(
        body,
        mesh=mesh,
        in_specs=(
            P("req", None),
            P("req"),
            P(),
            P(),
            P(("req", "tp"), None),
            P(("req", "tp"), None),
            P(),
            P(),
            P("tp", None),
            P("tp", None),
        ),
        out_specs=(P(("req", "tp"), None), P("req", None, "tp")),
        check_vma=False,
    )
```

time: 733 us -> 570 us (0.78); the launches traced: 732 us -> 559 us
  waiting for transfers between devices: 551 us -> 228 us
  local copies, waits for them, and re-layouts: 25.6 us -> 115 us
  blocking collectives: 68.8 us -> 0 us
  starting transfers between devices: 0.39 us -> 68.1 us
  matrix products: 52 us -> 92.7 us
  other arithmetic: 19.8 us -> 38.6 us
    all_gather x3 -> x0, waiting for transfers between devices: 436 us -> none  [the longest x1 337 us: body(): lax.all_gather(gu_half, 'req', axis=0, tiled=True)]
    ppermute x0 -> x67, waiting for transfers between devices: none -> 228 us  [swap(): return lax.ppermute(value, ('req', 'tp'), pairs)]
    all_to_all x2 -> x0, blocking collectives: 68.8 us -> none  [the longest x1 54.4 us: body(): lax.all_to_all(trainer_gateup.astype(jnp.bfloat16), 'tp', split_axis=1, c...]
    ppermute x0 -> x67, starting transfers between devices: none -> 68.1 us  [swap(): return lax.ppermute(value, ('req', 'tp'), pairs)]
    psum x1 -> x0, waiting for transfers between devices: 66.2 us -> none  [body(): mixed = lax.psum(partial_out, 'tp')]
    reduce_scatter x1 -> x0, waiting for transfers between devices: 48.3 us -> none  [body(): added = lax.psum_scatter(down, 'tp', scatter_dimension=0, tiled=True)]
    dot_general x6 -> x19, matrix products: 44.4 us -> 84.8 us  [the longest x16 68.2 us: dot(): return jnp.dot(a, b, preferred_element_type=F32)]
    unnamed x21 -> x125, local copies, waits for them, and re-layouts: 0.82 us -> 28.1 us
  transfers between devices with their start and end apart: 5 -> 67, of which waited for: 5 -> 26; matrix products, arithmetic and copies ran while one was open for 8% -> 41% of each run, Pallas kernels for 0% -> 0%
where the time goes in v1:
time: 570 us; the launch traced here: 559 us
  waiting for transfers between devices  228 us (40%)
  local copies, waits for them, and re-layouts  115 us (20%)
  matrix products  92.7 us (16%)
  starting transfers between devices  68.1 us (12%)
  other arithmetic  38.6 us (7%)
  between operations  17.5 us (3%)
    ppermute x67, waiting for transfers between devices, swap(): return lax.ppermute(value, ('req', 'tp'), pairs)  228 us
    dot_general x16, matrix products, dot(): return jnp.dot(a, b, preferred_element_type=F32)  68.2 us
    ppermute x67, starting transfers between devices, swap(): return lax.ppermute(value, ('req', 'tp'), pairs)  68.1 us
    unnamed x125, local copies, waits for them, and re-layouts  28.1 us
    dynamic_update_slice x16, local copies, waits for them, and re-layouts, to_groups(): lax.dynamic_update_slice_in_dim(held, jnp.expand_dims(mine, len(lead)), t...  14.7 us
  transfers between devices with their start and end apart: 67, of which 26 were waited for; matrix products, arithmetic and copies ran while one was open for 41% of the time, Pallas kernels for 0%

profile of v1, /device:TPU:0, one launch (start us, length us, event | category | flops | bytes accessed | tf_op | source)
XLA Modules:
  0.0 559.5 jit_solution(13190056917180192888)
XLA Ops:
  6.1 4.2 constant_dynamic-slice_fusion.4
  15.4 3.8 convert_element_type.102
  19.3 7.9 %reshape.270 = bf16[80,4,2,2,864]{4,3,2,1,0:T(2,128)(2,1)} reshape(bf16[80,13824]{1,0:T(8,128)(2,1)} %convert_element_type.102) | data formatting | bytes 4423680 | tf_op jit(solution)/shard_map/reshape | solution.py:135
  37.6 4.5 fusion.83
  54.7 4.8 copy_bitcast_fusion
  59.5 3.3 reshape.274
  70.6 11.9 %fusion.14 = bf16[2560,640]{1,0:T(8,128)(2,1)} fusion(bf16[640,2560]{1,0:T(8,128)(2,1)S(1)} %copy-done, s32[2560]{0:T(1024)S(1)} %add.287), kind=kOutput, calls=%fused_computation.25 | convolution fusion | flops 8403353600 | bytes 6563840 | tf_op jit(solution)/shard_map/dot_general | solution.py:39
  82.6 8.9 %multiply_reduce_fusion = (f32[512]{0:T(512)S(1)}, f32[2560,512]{1,0:T(8,128)}) fusion(bf16[512,2560]{1,0:T(8,128)(2,1)S(1)} %copy-done.34, s32[2560]{0:T(1024)S(1)} %add.287), kind=kOutput, calls=%fused_computation.24 | convolution fusion | flops 6726614528 | bytes 7876608 | tf_op jit(solution)/shard_map/dot_general | solution.py:39
  93.3 9.2 %fusion.12 = bf16[2,864,2560]{2,1,0:T(8,128)(2,1)} fusion(s32[]{:T(128)S(6)} %select_n.193, bf16[2,864,2560]{2,1,0:T(8,128)(2,1)} %bitcast.222), kind=kLoop, calls=%fused_computation.17 | loop fusion | flops 4423680 | bytes 17694724 | tf_op jit(solution)/shard_map/jit(_roll_dynamic)/concatenate | solution.py:206
  120.9 4.5 collective-permute-done.47
  139.8 5.8 %collective-permute-done.25 = bf16[2,80,640]{2,1,0:T(8,128)(2,1)S(1)} collective-permute-done((bf16[2,80,640]{2,1,0:T(8,128)(2,1)S(1)}, bf16[2,80,640]{2,1,0:T(8,128)(2,1)S(1)}, u32[]{:S(2)}, u32[]{:S(2)}) %collective-permute-start.25) | collective-permute-done | bytes 204832 | tf_op jit(solution)/shard_map/ppermute | solution.py:73
  160.5 6.3 %collective-permute-done.50 = bf16[320,448]{1,0:T(8,128)(2,1)S(1)} collective-permute-done((bf16[320,448]{1,0:T(8,128)(2,1)S(1)}, bf16[320,448]{1,0:T(8,128)(2,1)S(1)}, u32[]{:S(2)}, u32[]{:S(2)}) %collective-permute-start.50) | collective-permute-done | bytes 286752 | tf_op jit(solution)/shard_map/ppermute | solution.py:73
  169.1 6.5 %collective-permute-done.28 = bf16[320,640]{1,0:T(8,128)(2,1)S(1)} collective-permute-done((bf16[320,640]{1,0:T(8,128)(2,1)S(1)}, bf16[320,640]{1,0:T(8,128)(2,1)S(1)}, u32[]{:S(2)}, u32[]{:S(2)}) %collective-permute-start.28) | collective-permute-done | bytes 409632 | tf_op jit(solution)/shard_map/ppermute | solution.py:73
  178.1 16.2 %collective-permute-done.39 = bf16[320,640]{1,0:T(8,128)(2,1)S(1)} collective-permute-done((bf16[320,640]{1,0:T(8,128)(2,1)S(1)}, bf16[320,640]{1,0:T(8,128)(2,1)S(1)}, u32[]{:S(2)}, u32[]{:S(2)}) %collective-permute-start.39) | collective-permute-done | bytes 409632 | tf_op jit(solution)/shard_map/ppermute | solution.py:73
  199.0 4.7 collective-permute-done.53
  204.9 3.6 collective-permute-done.43
  208.5 5.6 collective-permute-done.55
  214.1 5.9 %collective-permute-start.41 = (bf16[320,640]{1,0:T(8,128)(2,1)S(1)}, bf16[320,640]{1,0:T(8,128)(2,1)S(1)}, u32[]{:S(2)}, u32[]{:S(2)}) collective-permute-start(bf16[320,640]{1,0:T(8,128)(2,1)S(1)} %get-tuple-element.25), channel_id=1, source_target_pairs={{0,16},{1,17},{2,18},{3,19},{4,20},{5,21},{6,22},{7,23},{8,24},{9,... | collective-permute-start | bytes 1228808 | tf_op jit(solution)/shard_map/ppermute | solution.py:73
  220.0 27.9 %collective-permute-done.30 = bf16[320,640]{1,0:T(8,128)(2,1)S(1)} collective-permute-done((bf16[320,640]{1,0:T(8,128)(2,1)S(1)}, bf16[320,640]{1,0:T(8,128)(2,1)S(1)}, u32[]{:S(2)}, u32[]{:S(2)}) %collective-permute-start.30) | collective-permute-done | bytes 409632 | tf_op jit(solution)/shard_map/ppermute | solution.py:73
  252.1 16.0 %collective-permute-done.41 = bf16[320,640]{1,0:T(8,128)(2,1)S(1)} collective-permute-done((bf16[320,640]{1,0:T(8,128)(2,1)S(1)}, bf16[320,640]{1,0:T(8,128)(2,1)S(1)}, u32[]{:S(2)}, u32[]{:S(2)}) %collective-permute-start.41) | collective-permute-done | bytes 409632 | tf_op jit(solution)/shard_map/ppermute | solution.py:73
  271.2 24.8 %collective-permute-done.6 = bf16[320,960]{1,0:T(8,128)(2,1)S(1)} collective-permute-done((bf16[320,960]{1,0:T(8,128)(2,1)}, bf16[320,960]{1,0:T(8,128)(2,1)S(1)}, u32[]{:S(2)}, u32[]{:S(2)}) %collective-permute-start.6) | collective-permute-done | bytes 614432 | tf_op jit(solution)/shard_map/ppermute | solution.py:73
  298.4 10.0 %collective-permute-done.33 = bf16[320,640]{1,0:T(8,128)(2,1)S(1)} collective-permute-done((bf16[320,640]{1,0:T(8,128)(2,1)S(1)}, bf16[320,640]{1,0:T(8,128)(2,1)S(1)}, u32[]{:S(2)}, u32[]{:S(2)}) %collective-permute-start.33) | collective-permute-done | bytes 409632 | tf_op jit(solution)/shard_map/ppermute | solution.py:73
  308.6 22.6 %collective-permute-done.44 = bf16[320,640]{1,0:T(8,128)(2,1)S(1)} collective-permute-done((bf16[320,640]{1,0:T(8,128)(2,1)S(1)}, bf16[320,640]{1,0:T(8,128)(2,1)S(1)}, u32[]{:S(2)}, u32[]{:S(2)}) %collective-permute-start.44) | collective-permute-done | bytes 409632 | tf_op jit(solution)/shard_map/ppermute | solution.py:73
  331.4 13.9 %collective-permute-done.7 = bf16[320,960]{1,0:T(8,128)(2,1)S(1)} collective-permute-done((bf16[320,960]{1,0:T(8,128)(2,1)S(1)}, bf16[320,960]{1,0:T(8,128)(2,1)S(1)}, u32[]{:S(2)}, u32[]{:S(2)}) %collective-permute-start.7) | collective-permute-done | bytes 614432 | tf_op jit(solution)/shard_map/ppermute | solution.py:73
  345.3 8.1 %collective-permute-done.9 = bf16[320,960]{1,0:T(8,128)(2,1)S(1)} collective-permute-done((bf16[320,960]{1,0:T(8,128)(2,1)S(1)}, bf16[320,960]{1,0:T(8,128)(2,1)S(1)}, u32[]{:S(2)}, u32[]{:S(2)}) %collective-permute-start.9) | collective-permute-done | bytes 614432 | tf_op jit(solution)/shard_map/ppermute | solution.py:73
  366.9 9.8 %collective-permute-start.61 = (bf16[128,320]{0,1:T(8,128)(2,1)}, bf16[128,320]{0,1:T(8,128)(2,1)}, u32[]{:S(2)}, u32[]{:S(2)}) collective-permute-start(bf16[128,320]{0,1:T(8,128)(2,1)} %get-tuple-element.62), channel_id=1, source_target_pairs={{0,8},{1,9},{2,10},{3,11},{4,12},{5,13},{6,14},{7,15},{8,0},{9,1},... | collective-permute-start | bytes 245768 | tf_op jit(solution)/shard_map/ppermute | solution.py:73
  379.1 7.8 %fusion.84 = (f32[2,4,512]{2,1,0:T(4,128)S(1)}, f32[2,4,512,512]{2,3,1,0:T(8,128)}) fusion(pred[512,512]{0,1:T(8,128)(4,1)} %fusion.40, bf16[512,2,4,40]{0,3,2,1:T(8,128)(2,1)} %bitcast.234, bf16[512,2,4,40]{0,3,2,1:T(8,128)(2,1)} %bitcast.233, bf16[512,2,40]{0,2,1:T(8,128)(2,1)} %copy-done.12, bf16[512,2,40]{0,2,1:T(8,128)(2,1)} %copy-done.11), kind=kOutput, calls=%fused_computation.258 | convolution fusion | flops 345571840 | bytes 9486336 | tf_op jit(solution)/shard_map/sub | solution.py:161
  386.9 5.1 fusion.38
  394.3 4.3 constant_dynamic-slice_fusion
  399.8 4.0 fusion.54
  410.6 3.4 convolution_add_fusion.2
  418.0 5.3 collective-permute-done.14
  423.3 3.4 multiply_reduce_fusion.1
  433.8 12.0 %collective-permute-done.63 = bf16[128,320]{0,1:T(8,128)(2,1)S(1)} collective-permute-done((bf16[128,320]{0,1:T(8,128)(2,1)S(1)}, bf16[128,320]{0,1:T(8,128)(2,1)S(1)}, u32[]{:S(2)}, u32[]{:S(2)}) %collective-permute-start.63) | collective-permute-done | bytes 81952 | tf_op jit(solution)/shard_map/ppermute | solution.py:73
  445.8 4.6 collective-permute-start.64
  455.4 5.0 collective-permute-done.21
  467.9 4.5 concatenate.54
  476.0 3.6 fusion.91
  479.6 3.6 fusion.90
  485.6 3.9 fusion.29
  495.6 11.8 %collective-permute-done.45 = bf16[512,320]{0,1:T(8,128)(2,1)S(1)} collective-permute-done((bf16[512,320]{0,1:T(8,128)(2,1)S(1)}, bf16[512,320]{0,1:T(8,128)(2,1)S(1)}, u32[]{:S(2)}, u32[]{:S(2)}) %collective-permute-start.45) | collective-permute-done | bytes 327712 | tf_op jit(solution)/shard_map/ppermute | solution.py:73
  507.7 3.9 fusion.26
  511.6 4.8 collective-permute-done.34
  516.5 3.9 fusion.28
  520.4 8.4 %fusion.89 = (bf16[512,2560]{1,0:T(8,128)(2,1)}, f32[512,2560]{1,0:T(8,128)}) fusion(bf16[512,224]{0,1:T(8,128)(2,1)} %collective-permute-done.56, bf16[2,864,2560]{2,1,0:T(8,128)(2,1)S(1)} %bitcast.221, f32[512,2560]{1,0:T(8,128)S(1)} %fusion.39, f32[512,2560]{1,0:T(8,128)} %fusion.26, f32[512,2560]{1,0:T(8,128)S(1)} %fusion.27, f32[512,2560]{1,0:T(8,128)} %fusion.29, ...), kind=kOutput, calls=%fused_computation.259 | convolution fusion | flops 595066880 | bytes 35454976 | tf_op jit(solution)/shard_map/dot_general | solution.py:39
  540.2 5.7 %fusion.1 = f32[128,2560]{1,0:T(8,128)S(1)} fusion(s32[2560]{0:T(1024)S(1)} %copy-done.32, f32[128,2560]{0,1:T(8,128)S(1)} %copy-done.5), kind=kOutput, calls=%fused_computation.6 | convolution fusion | flops 1684602880 | bytes 2631680 | tf_op jit(solution)/shard_map/dot_general | solution.py:179
  545.9 5.8 %fusion.22 = f32[128,2560]{1,0:T(8,128)S(1)} fusion(f32[128,2560]{1,0:T(8,128)S(1)} %fusion.1, s32[2560]{0:T(1024)S(1)} %copy-done.32, f32[128,2560]{0,1:T(8,128)S(1)} %copy-done.6), kind=kOutput, calls=%fused_computation.34 | convolution fusion | flops 1685913600 | bytes 3942400 | tf_op jit(solution)/shard_map/dot_general | solution.py:179
  551.7 5.0 collective-permute-done.59
  (346 shorter events, 171.6 us)
Async XLA Ops:
  10.9 119.9 %collective-permute-start = (bf16[80,960]{1,0:T(8,128)(2,1)}, bf16[80,960]{1,0:T(8,128)(2,1)}, u32[]{:S(2)}, u32[]{:S(2)}) collective-permute-start(bf16[80,960]{1,0:T(8,128)(2,1)} %bitcast.215), channel_id=1, source_target_pairs={{0,1},{1,0},{2,3},{3,2},{4,5},{5,4},{6,7},{7,6},{8,9},{9,8},{10,11... | collective-permute-start | bytes 460808 | tf_op jit(solution)/shard_map/ppermute | solution.py:73
  12.1 121.1 %collective-permute-start.1 = (bf16[80,960]{1,0:T(8,128)(2,1)}, bf16[80,960]{1,0:T(8,128)(2,1)}, u32[]{:S(2)}, u32[]{:S(2)}) collective-permute-start(bf16[80,960]{1,0:T(8,128)(2,1)} %bitcast.214), channel_id=1, source_target_pairs={{0,2},{1,3},{2,0},{3,1},{4,6},{5,7},{6,4},{7,5},{8,10},{9,11},{10,... | collective-permute-start | bytes 460808 | tf_op jit(solution)/shard_map/ppermute | solution.py:73
  15.3 119.8 %collective-permute-start.2 = (bf16[80,960]{1,0:T(8,128)(2,1)}, bf16[80,960]{1,0:T(8,128)(2,1)}, u32[]{:S(2)}, u32[]{:S(2)}) collective-permute-start(bf16[80,960]{1,0:T(8,128)(2,1)} %bitcast.213), channel_id=1, source_target_pairs={{0,3},{1,2},{2,1},{3,0},{4,7},{5,6},{6,5},{7,4},{8,11},{9,10},{10,... | collective-permute-start | bytes 460808 | tf_op jit(solution)/shard_map/ppermute | solution.py:73
  34.9 91.2 %collective-permute-start.48 = (bf16[2,80,448]{2,1,0:T(8,128)(2,1)}, bf16[2,80,448]{2,1,0:T(8,128)(2,1)}, u32[]{:S(2)}, u32[]{:S(2)}) collective-permute-start(bf16[2,80,448]{2,1,0:T(8,128)(2,1)} %get-tuple-element.46), channel_id=1, source_target_pairs={{0,3},{1,2},{2,1},{3,0},{4,7},{5,6},{6,5},{7,4},{8,11},{9,10},{10,... | collective-permute-start | bytes 430088 | tf_op jit(solution)/shard_map/ppermute | solution.py:73
  36.5 82.5 %collective-permute-start.46 = (bf16[2,80,448]{2,1,0:T(8,128)(2,1)}, bf16[2,80,448]{2,1,0:T(8,128)(2,1)}, u32[]{:S(2)}, u32[]{:S(2)}) collective-permute-start(bf16[2,80,448]{2,1,0:T(8,128)(2,1)} %get-tuple-element.48), channel_id=1, source_target_pairs={{0,1},{1,0},{2,3},{3,2},{4,5},{5,4},{6,7},{7,6},{8,9},{9,8},{10,11... | collective-permute-start | bytes 430088 | tf_op jit(solution)/shard_map/ppermute | solution.py:73
  125.4 28.0 %collective-permute-start.37 = (bf16[2,80,640]{2,1,0:T(8,128)(2,1)S(1)}, bf16[2,80,640]{2,1,0:T(8,128)(2,1)S(1)}, u32[]{:S(2)}, u32[]{:S(2)}) collective-permute-start(bf16[2,80,640]{2,1,0:T(8,128)(2,1)S(1)} %copy-done.13), channel_id=1, source_target_pairs={{0,3},{1,2},{2,1},{3,0},{4,7},{5,6},{6,5},{7,4},{8,11},{9,10},{10,... | collective-permute-start | bytes 614408 | tf_op jit(solution)/shard_map/ppermute | solution.py:73
  126.1 26.2 %collective-permute-start.36 = (bf16[2,80,640]{2,1,0:T(8,128)(2,1)S(1)}, bf16[2,80,640]{2,1,0:T(8,128)(2,1)S(1)}, u32[]{:S(2)}, u32[]{:S(2)}) collective-permute-start(bf16[2,80,640]{2,1,0:T(8,128)(2,1)S(1)} %copy-done.14), channel_id=1, source_target_pairs={{0,2},{1,3},{2,0},{3,1},{4,6},{5,7},{6,4},{7,5},{8,10},{9,11},{10,... | collective-permute-start | bytes 614408 | tf_op jit(solution)/shard_map/ppermute | solution.py:73
  130.8 19.1 %collective-permute-start.35 = (bf16[2,80,640]{2,1,0:T(8,128)(2,1)S(1)}, bf16[2,80,640]{2,1,0:T(8,128)(2,1)S(1)}, u32[]{:S(2)}, u32[]{:S(2)}) collective-permute-start(bf16[2,80,640]{2,1,0:T(8,128)(2,1)S(1)} %copy-done.15), channel_id=1, source_target_pairs={{0,1},{1,0},{2,3},{3,2},{4,5},{5,4},{6,7},{7,6},{8,9},{9,8},{10,11... | collective-permute-start | bytes 614408 | tf_op jit(solution)/shard_map/ppermute | solution.py:73
  133.2 15.0 %collective-permute-start.26 = (bf16[2,80,640]{2,1,0:T(8,128)(2,1)S(1)}, bf16[2,80,640]{2,1,0:T(8,128)(2,1)S(1)}, u32[]{:S(2)}, u32[]{:S(2)}) collective-permute-start(bf16[2,80,640]{2,1,0:T(8,128)(2,1)S(1)} %get-tuple-element.40), channel_id=1, source_target_pairs={{0,3},{1,2},{2,1},{3,0},{4,7},{5,6},{6,5},{7,4},{8,11},{9,10},{10,... | collective-permute-start | bytes 614408 | tf_op jit(solution)/shard_map/ppermute | solution.py:73
  145.6 30.4 %collective-permute-start.52 = (bf16[320,448]{1,0:T(8,128)(2,1)S(1)}, bf16[320,448]{1,0:T(8,128)(2,1)S(1)}, u32[]{:S(2)}, u32[]{:S(2)}) collective-permute-start(bf16[320,448]{1,0:T(8,128)(2,1)S(1)} %get-tuple-element.27), channel_id=1, source_target_pairs={{0,16},{1,17},{2,18},{3,19},{4,20},{5,21},{6,22},{7,23},{8,24},{9,... | collective-permute-start | bytes 860168 | tf_op jit(solution)/shard_map/ppermute | solution.py:73
  150.0 16.8 %collective-permute-start.50 = (bf16[320,448]{1,0:T(8,128)(2,1)S(1)}, bf16[320,448]{1,0:T(8,128)(2,1)S(1)}, u32[]{:S(2)}, u32[]{:S(2)}) collective-permute-start(bf16[320,448]{1,0:T(8,128)(2,1)S(1)} %dynamic-slice_bitcast_fusion.4), channel_id=1, source_target_pairs={{0,8},{1,9},{2,10},{3,11},{4,12},{5,13},{6,14},{7,15},{8,0},{9,1},... | collective-permute-start | bytes 860168 | tf_op jit(solution)/shard_map/ppermute | solution.py:73
  152.3 23.3 %collective-permute-start.28 = (bf16[320,640]{1,0:T(8,128)(2,1)S(1)}, bf16[320,640]{1,0:T(8,128)(2,1)S(1)}, u32[]{:S(2)}, u32[]{:S(2)}) collective-permute-start(bf16[320,640]{1,0:T(8,128)(2,1)S(1)} %dynamic-slice_bitcast_fusion.2), channel_id=1, source_target_pairs={{0,8},{1,9},{2,10},{3,11},{4,12},{5,13},{6,14},{7,15},{8,0},{9,1},... | collective-permute-start | bytes 1228808 | tf_op jit(solution)/shard_map/ppermute | solution.py:73
  153.5 14.3 %collective-permute-start.27 = (bf16[320,640]{1,0:T(8,128)(2,1)S(1)}, bf16[320,640]{1,0:T(8,128)(2,1)S(1)}, u32[]{:S(2)}, u32[]{:S(2)}) collective-permute-start(bf16[320,640]{1,0:T(8,128)(2,1)S(1)} %get-tuple-element.23), channel_id=1, source_target_pairs={{0,4},{1,5},{2,6},{3,7},{4,0},{5,1},{6,2},{7,3},{8,12},{9,13},{10,... | collective-permute-start | bytes 1228808 | tf_op jit(solution)/shard_map/ppermute | solution.py:73
  158.9 18.8 %collective-permute-start.38 = (bf16[320,640]{1,0:T(8,128)(2,1)S(1)}, bf16[320,640]{1,0:T(8,128)(2,1)S(1)}, u32[]{:S(2)}, u32[]{:S(2)}) collective-permute-start(bf16[320,640]{1,0:T(8,128)(2,1)S(1)} %get-tuple-element.25), channel_id=1, source_target_pairs={{0,4},{1,5},{2,6},{3,7},{4,0},{5,1},{6,2},{7,3},{8,12},{9,13},{10,... | collective-permute-start | bytes 1228808 | tf_op jit(solution)/shard_map/ppermute | solution.py:73
  166.8 27.6 %collective-permute-start.39 = (bf16[320,640]{1,0:T(8,128)(2,1)S(1)}, bf16[320,640]{1,0:T(8,128)(2,1)S(1)}, u32[]{:S(2)}, u32[]{:S(2)}) collective-permute-start(bf16[320,640]{1,0:T(8,128)(2,1)S(1)} %dynamic-slice_bitcast_fusion), channel_id=1, source_target_pairs={{0,8},{1,9},{2,10},{3,11},{4,12},{5,13},{6,14},{7,15},{8,0},{9,1},... | collective-permute-start | bytes 1228808 | tf_op jit(solution)/shard_map/ppermute | solution.py:73
  167.7 28.7 %collective-permute-start.54 = (bf16[320,448]{1,0:T(8,128)(2,1)S(1)}, bf16[320,448]{1,0:T(8,128)(2,1)S(1)}, u32[]{:S(2)}, u32[]{:S(2)}) collective-permute-start(bf16[320,448]{1,0:T(8,128)(2,1)S(1)} %dynamic-slice_bitcast_fusion.4), channel_id=1, source_target_pairs={{0,24},{1,25},{2,26},{3,27},{4,28},{5,29},{6,30},{7,31},{8,16},{9,... | collective-permute-start | bytes 860168 | tf_op jit(solution)/shard_map/ppermute | solution.py:73
  175.6 20.7 %collective-permute-start.51 = (bf16[320,448]{1,0:T(8,128)(2,1)S(1)}, bf16[320,448]{1,0:T(8,128)(2,1)S(1)}, u32[]{:S(2)}, u32[]{:S(2)}) collective-permute-start(bf16[320,448]{1,0:T(8,128)(2,1)S(1)} %collective-permute-done.50), channel_id=1, source_target_pairs={{0,4},{1,5},{2,6},{3,7},{4,0},{5,1},{6,2},{7,3},{8,12},{9,13},{10,... | collective-permute-start | bytes 860168 | tf_op jit(solution)/shard_map/ppermute | solution.py:73
  176.0 71.9 %collective-permute-start.3 = (bf16[320,960]{1,0:T(8,128)(2,1)}, bf16[320,960]{1,0:T(8,128)(2,1)S(1)}, u32[]{:S(2)}, u32[]{:S(2)}) collective-permute-start(bf16[320,960]{1,0:T(8,128)(2,1)} %bitcast.7), channel_id=1, source_target_pairs={{0,4},{1,5},{2,6},{3,7},{4,0},{5,1},{6,2},{7,3},{8,12},{9,13},{10,... | collective-permute-start | bytes 1843208 | tf_op jit(solution)/shard_map/ppermute | solution.py:73
  177.7 25.9 %collective-permute-start.53 = (bf16[320,448]{1,0:T(8,128)(2,1)S(1)}, bf16[320,448]{1,0:T(8,128)(2,1)S(1)}, u32[]{:S(2)}, u32[]{:S(2)}) collective-permute-start(bf16[320,448]{1,0:T(8,128)(2,1)S(1)} %collective-permute-done.52), channel_id=1, source_target_pairs={{0,4},{1,5},{2,6},{3,7},{4,0},{5,1},{6,2},{7,3},{8,12},{9,13},{10,... | collective-permute-start | bytes 860168 | tf_op jit(solution)/shard_map/ppermute | solution.py:73
  196.3 51.7 %collective-permute-start.4 = (bf16[320,960]{1,0:T(8,128)(2,1)}, bf16[320,960]{1,0:T(8,128)(2,1)S(1)}, u32[]{:S(2)}, u32[]{:S(2)}) collective-permute-start(bf16[320,960]{1,0:T(8,128)(2,1)} %bitcast.7), channel_id=1, source_target_pairs={{0,8},{1,9},{2,10},{3,11},{4,12},{5,13},{6,14},{7,15},{8,0},{9,1},... | collective-permute-start | bytes 1843208 | tf_op jit(solution)/shard_map/ppermute | solution.py:73
  196.4 51.5 %collective-permute-start.30 = (bf16[320,640]{1,0:T(8,128)(2,1)S(1)}, bf16[320,640]{1,0:T(8,128)(2,1)S(1)}, u32[]{:S(2)}, u32[]{:S(2)}) collective-permute-start(bf16[320,640]{1,0:T(8,128)(2,1)S(1)} %get-tuple-element.23), channel_id=1, source_target_pairs={{0,16},{1,17},{2,18},{3,19},{4,20},{5,21},{6,22},{7,23},{8,24},{9,... | collective-permute-start | bytes 1228808 | tf_op jit(solution)/shard_map/ppermute | solution.py:73
  208.5 41.4 %collective-permute-start.29 = (bf16[320,640]{1,0:T(8,128)(2,1)S(1)}, bf16[320,640]{1,0:T(8,128)(2,1)S(1)}, u32[]{:S(2)}, u32[]{:S(2)}) collective-permute-start(bf16[320,640]{1,0:T(8,128)(2,1)S(1)} %collective-permute-done.28), channel_id=1, source_target_pairs={{0,4},{1,5},{2,6},{3,7},{4,0},{5,1},{6,2},{7,3},{8,12},{9,13},{10,... | collective-permute-start | bytes 1228808 | tf_op jit(solution)/shard_map/ppermute | solution.py:73
  214.1 54.0 %collective-permute-start.41 = (bf16[320,640]{1,0:T(8,128)(2,1)S(1)}, bf16[320,640]{1,0:T(8,128)(2,1)S(1)}, u32[]{:S(2)}, u32[]{:S(2)}) collective-permute-start(bf16[320,640]{1,0:T(8,128)(2,1)S(1)} %get-tuple-element.25), channel_id=1, source_target_pairs={{0,16},{1,17},{2,18},{3,19},{4,20},{5,21},{6,22},{7,23},{8,24},{9,... | collective-permute-start | bytes 1228808 | tf_op jit(solution)/shard_map/ppermute | solution.py:73
  247.9 48.1 %collective-permute-start.6 = (bf16[320,960]{1,0:T(8,128)(2,1)}, bf16[320,960]{1,0:T(8,128)(2,1)S(1)}, u32[]{:S(2)}, u32[]{:S(2)}) collective-permute-start(bf16[320,960]{1,0:T(8,128)(2,1)} %bitcast.7), channel_id=1, source_target_pairs={{0,16},{1,17},{2,18},{3,19},{4,20},{5,21},{6,22},{7,23},{8,24},{9,... | collective-permute-start | bytes 1843208 | tf_op jit(solution)/shard_map/ppermute | solution.py:73
  247.9 20.2 %collective-permute-start.31 = (bf16[320,640]{1,0:T(8,128)(2,1)S(1)}, bf16[320,640]{1,0:T(8,128)(2,1)S(1)}, u32[]{:S(2)}, u32[]{:S(2)}) collective-permute-start(bf16[320,640]{1,0:T(8,128)(2,1)S(1)} %collective-permute-done.30), channel_id=1, source_target_pairs={{0,4},{1,5},{2,6},{3,7},{4,0},{5,1},{6,2},{7,3},{8,12},{9,13},{10,... | collective-permute-start | bytes 1228808 | tf_op jit(solution)/shard_map/ppermute | solution.py:73
  248.0 20.8 %collective-permute-start.32 = (bf16[320,640]{1,0:T(8,128)(2,1)S(1)}, bf16[320,640]{1,0:T(8,128)(2,1)S(1)}, u32[]{:S(2)}, u32[]{:S(2)}) collective-permute-start(bf16[320,640]{1,0:T(8,128)(2,1)S(1)} %dynamic-slice_bitcast_fusion.2), channel_id=1, source_target_pairs={{0,24},{1,25},{2,26},{3,27},{4,28},{5,29},{6,30},{7,31},{8,16},{9,... | collective-permute-start | bytes 1228808 | tf_op jit(solution)/shard_map/ppermute | solution.py:73
  249.9 46.1 %collective-permute-start.40 = (bf16[320,640]{1,0:T(8,128)(2,1)S(1)}, bf16[320,640]{1,0:T(8,128)(2,1)S(1)}, u32[]{:S(2)}, u32[]{:S(2)}) collective-permute-start(bf16[320,640]{1,0:T(8,128)(2,1)S(1)} %collective-permute-done.39), channel_id=1, source_target_pairs={{0,4},{1,5},{2,6},{3,7},{4,0},{5,1},{6,2},{7,3},{8,12},{9,13},{10,... | collective-permute-start | bytes 1228808 | tf_op jit(solution)/shard_map/ppermute | solution.py:73
  268.1 30.1 %collective-permute-start.42 = (bf16[320,640]{1,0:T(8,128)(2,1)S(1)}, bf16[320,640]{1,0:T(8,128)(2,1)S(1)}, u32[]{:S(2)}, u32[]{:S(2)}) collective-permute-start(bf16[320,640]{1,0:T(8,128)(2,1)S(1)} %collective-permute-done.41), channel_id=1, source_target_pairs={{0,4},{1,5},{2,6},{3,7},{4,0},{5,1},{6,2},{7,3},{8,12},{9,13},{10,... | collective-permute-start | bytes 1228808 | tf_op jit(solution)/shard_map/ppermute | solution.py:73
  268.2 96.2 %collective-permute-start.13 = (bf16[640,2560]{0,1:T(8,128)(2,1)}, bf16[640,2560]{0,1:T(8,128)(2,1)S(1)}, u32[]{:S(2)}, u32[]{:S(2)}) collective-permute-start(bf16[640,2560]{0,1:T(8,128)(2,1)} %bitcast.22), channel_id=1, source_target_pairs={{0,2},{1,3},{2,0},{3,1},{4,6},{5,7},{6,4},{7,5},{8,10},{9,11},{10,... | collective-permute-start | bytes 9830408 | tf_op jit(solution)/shard_map/ppermute | solution.py:73
  268.8 39.7 %collective-permute-start.8 = (bf16[320,960]{1,0:T(8,128)(2,1)}, bf16[320,960]{1,0:T(8,128)(2,1)S(1)}, u32[]{:S(2)}, u32[]{:S(2)}) collective-permute-start(bf16[320,960]{1,0:T(8,128)(2,1)} %bitcast.7), channel_id=1, source_target_pairs={{0,24},{1,25},{2,26},{3,27},{4,28},{5,29},{6,30},{7,31},{8,16},{9,... | collective-permute-start | bytes 1843208 | tf_op jit(solution)/shard_map/ppermute | solution.py:73
  296.0 35.2 %collective-permute-start.5 = (bf16[320,960]{1,0:T(8,128)(2,1)S(1)}, bf16[320,960]{1,0:T(8,128)(2,1)S(1)}, u32[]{:S(2)}, u32[]{:S(2)}) collective-permute-start(bf16[320,960]{1,0:T(8,128)(2,1)S(1)} %collective-permute-done.4), channel_id=1, source_target_pairs={{0,4},{1,5},{2,6},{3,7},{4,0},{5,1},{6,2},{7,3},{8,12},{9,13},{10,... | collective-permute-start | bytes 1843208 | tf_op jit(solution)/shard_map/ppermute | solution.py:73
  298.2 33.0 %collective-permute-start.44 = (bf16[320,640]{1,0:T(8,128)(2,1)S(1)}, bf16[320,640]{1,0:T(8,128)(2,1)S(1)}, u32[]{:S(2)}, u32[]{:S(2)}) collective-permute-start(bf16[320,640]{1,0:T(8,128)(2,1)S(1)} %collective-permute-done.43), channel_id=1, source_target_pairs={{0,4},{1,5},{2,6},{3,7},{4,0},{5,1},{6,2},{7,3},{8,12},{9,13},{10,... | collective-permute-start | bytes 1228808 | tf_op jit(solution)/shard_map/ppermute | solution.py:73
  308.4 36.9 %collective-permute-start.7 = (bf16[320,960]{1,0:T(8,128)(2,1)S(1)}, bf16[320,960]{1,0:T(8,128)(2,1)S(1)}, u32[]{:S(2)}, u32[]{:S(2)}) collective-permute-start(bf16[320,960]{1,0:T(8,128)(2,1)S(1)} %collective-permute-done.6), channel_id=1, source_target_pairs={{0,4},{1,5},{2,6},{3,7},{4,0},{5,1},{6,2},{7,3},{8,12},{9,13},{10,... | collective-permute-start | bytes 1843208 | tf_op jit(solution)/shard_map/ppermute | solution.py:73
  308.5 101.6 %collective-permute-start.11 = (bf16[640,2560]{0,1:T(8,128)(2,1)}, bf16[640,2560]{0,1:T(8,128)(2,1)}, u32[]{:S(2)}, u32[]{:S(2)}) collective-permute-start(bf16[640,2560]{0,1:T(8,128)(2,1)} %bitcast.22), channel_id=1, source_target_pairs={{0,1},{1,0},{2,3},{3,2},{4,5},{5,4},{6,7},{7,6},{8,9},{9,8},{10,11... | collective-permute-start | bytes 9830408 | tf_op jit(solution)/shard_map/ppermute | solution.py:73
  331.2 22.2 %collective-permute-start.9 = (bf16[320,960]{1,0:T(8,128)(2,1)S(1)}, bf16[320,960]{1,0:T(8,128)(2,1)S(1)}, u32[]{:S(2)}, u32[]{:S(2)}) collective-permute-start(bf16[320,960]{1,0:T(8,128)(2,1)S(1)} %collective-permute-done.8), channel_id=1, source_target_pairs={{0,4},{1,5},{2,6},{3,7},{4,0},{5,1},{6,2},{7,3},{8,12},{9,13},{10,... | collective-permute-start | bytes 1843208 | tf_op jit(solution)/shard_map/ppermute | solution.py:73
  363.1 169.6 %collective-permute-start.65 = (bf16[128,320]{0,1:T(8,128)(2,1)}, bf16[128,320]{0,1:T(8,128)(2,1)}, u32[]{:S(2)}, u32[]{:S(2)}) collective-permute-start(bf16[128,320]{0,1:T(8,128)(2,1)} %get-tuple-element.65), channel_id=1, source_target_pairs={{0,24},{1,25},{2,26},{3,27},{4,28},{5,29},{6,30},{7,31},{8,16},{9,... | collective-permute-start | bytes 245768 | tf_op jit(solution)/shard_map/ppermute | solution.py:73
  364.4 59.0 %collective-permute-start.15 = (bf16[640,2560]{0,1:T(8,128)(2,1)S(1)}, bf16[640,2560]{0,1:T(8,128)(2,1)}, u32[]{:S(2)}, u32[]{:S(2)}) collective-permute-start(bf16[640,2560]{0,1:T(8,128)(2,1)S(1)} %collective-permute-done.13), channel_id=1, source_target_pairs={{0,1},{1,0},{2,3},{3,2},{4,5},{5,4},{6,7},{7,6},{8,9},{9,8},{10,11... | collective-permute-start | bytes 9830408 | tf_op jit(solution)/shard_map/ppermute | solution.py:73
  365.2 43.4 %collective-permute-start.60 = (bf16[128,320]{0,1:T(8,128)(2,1)}, bf16[128,320]{0,1:T(8,128)(2,1)}, u32[]{:S(2)}, u32[]{:S(2)}) collective-permute-start(bf16[128,320]{0,1:T(8,128)(2,1)} %get-tuple-element.61), channel_id=1, source_target_pairs={{0,4},{1,5},{2,6},{3,7},{4,0},{5,1},{6,2},{7,3},{8,12},{9,13},{10,... | collective-permute-start | bytes 245768 | tf_op jit(solution)/shard_map/ppermute | solution.py:73
  366.9 64.0 %collective-permute-start.61 = (bf16[128,320]{0,1:T(8,128)(2,1)}, bf16[128,320]{0,1:T(8,128)(2,1)}, u32[]{:S(2)}, u32[]{:S(2)}) collective-permute-start(bf16[128,320]{0,1:T(8,128)(2,1)} %get-tuple-element.62), channel_id=1, source_target_pairs={{0,8},{1,9},{2,10},{3,11},{4,12},{5,13},{6,14},{7,15},{8,0},{9,1},... | collective-permute-start | bytes 245768 | tf_op jit(solution)/shard_map/ppermute | solution.py:73
  410.1 22.4 %collective-permute-start.62 = (bf16[128,320]{0,1:T(8,128)(2,1)S(1)}, bf16[128,320]{0,1:T(8,128)(2,1)S(1)}, u32[]{:S(2)}, u32[]{:S(2)}) collective-permute-start(bf16[128,320]{0,1:T(8,128)(2,1)S(1)} %copy-done.20), channel_id=1, source_target_pairs={{0,12},{1,13},{2,14},{3,15},{4,8},{5,9},{6,10},{7,11},{8,4},{9,5},... | collective-permute-start | bytes 245768 | tf_op jit(solution)/shard_map/ppermute | solution.py:73
  429.1 21.9 %collective-permute-start.19 = (bf16[128,2560]{0,1:T(8,128)(2,1)S(1)}, bf16[128,2560]{0,1:T(8,128)(2,1)S(1)}, u32[]{:S(2)}, u32[]{:S(2)}) collective-permute-start(bf16[128,2560]{0,1:T(8,128)(2,1)S(1)} %get-tuple-element.29), channel_id=1, source_target_pairs={{0,8},{1,9},{2,10},{3,11},{4,12},{5,13},{6,14},{7,15},{8,0},{9,1},... | collective-permute-start | bytes 1966088 | tf_op jit(solution)/shard_map/ppermute | solution.py:73
  430.2 22.9 %collective-permute-start.17 = (bf16[128,2560]{0,1:T(8,128)(2,1)S(1)}, bf16[128,2560]{0,1:T(8,128)(2,1)S(1)}, u32[]{:S(2)}, u32[]{:S(2)}) collective-permute-start(bf16[128,2560]{0,1:T(8,128)(2,1)S(1)} %get-tuple-element.29), channel_id=1, source_target_pairs={{0,2},{1,3},{2,0},{3,1},{4,6},{5,7},{6,4},{7,5},{8,10},{9,11},{10,... | collective-permute-start | bytes 1966088 | tf_op jit(solution)/shard_map/ppermute | solution.py:73
  431.0 23.4 %collective-permute-start.16 = (bf16[128,2560]{0,1:T(8,128)(2,1)S(1)}, bf16[128,2560]{0,1:T(8,128)(2,1)S(1)}, u32[]{:S(2)}, u32[]{:S(2)}) collective-permute-start(bf16[128,2560]{0,1:T(8,128)(2,1)S(1)} %get-tuple-element.29), channel_id=1, source_target_pairs={{0,1},{1,0},{2,3},{3,2},{4,5},{5,4},{6,7},{7,6},{8,9},{9,8},{10,11... | collective-permute-start | bytes 1966088 | tf_op jit(solution)/shard_map/ppermute | solution.py:73
  445.8 85.3 %collective-permute-start.64 = (bf16[128,320]{0,1:T(8,128)(2,1)}, bf16[128,320]{0,1:T(8,128)(2,1)}, u32[]{:S(2)}, u32[]{:S(2)}) collective-permute-start(bf16[128,320]{0,1:T(8,128)(2,1)} %get-tuple-element.66), channel_id=1, source_target_pairs={{0,20},{1,21},{2,22},{3,23},{4,16},{5,17},{6,18},{7,19},{8,28},{9,... | collective-permute-start | bytes 245768 | tf_op jit(solution)/shard_map/ppermute | solution.py:73
  465.7 68.5 %collective-permute-start.66 = (bf16[128,320]{0,1:T(8,128)(2,1)S(1)}, bf16[128,320]{0,1:T(8,128)(2,1)}, u32[]{:S(2)}, u32[]{:S(2)}) collective-permute-start(bf16[128,320]{0,1:T(8,128)(2,1)S(1)} %copy-done.18), channel_id=1, source_target_pairs={{0,28},{1,29},{2,30},{3,31},{4,24},{5,25},{6,26},{7,27},{8,20},{9,... | collective-permute-start | bytes 245768 | tf_op jit(solution)/shard_map/ppermute | solution.py:73
  492.7 27.7 %collective-permute-start.56 = (bf16[512,224]{0,1:T(8,128)(2,1)S(1)}, bf16[512,224]{0,1:T(8,128)(2,1)}, u32[]{:S(2)}, u32[]{:S(2)}) collective-permute-start(bf16[512,224]{0,1:T(8,128)(2,1)S(1)} %slice.206), channel_id=1, source_target_pairs={{0,8},{1,9},{2,10},{3,11},{4,12},{5,13},{6,14},{7,15},{8,0},{9,1},... | collective-permute-start | bytes 688136 | tf_op jit(solution)/shard_map/ppermute | solution.py:73
  492.7 14.7 %collective-permute-start.45 = (bf16[512,320]{0,1:T(8,128)(2,1)S(1)}, bf16[512,320]{0,1:T(8,128)(2,1)S(1)}, u32[]{:S(2)}, u32[]{:S(2)}) collective-permute-start(bf16[512,320]{0,1:T(8,128)(2,1)S(1)} %slice.199), channel_id=1, source_target_pairs={{0,8},{1,9},{2,10},{3,11},{4,12},{5,13},{6,14},{7,15},{8,0},{9,1},... | collective-permute-start | bytes 983048 | tf_op jit(solution)/shard_map/ppermute | solution.py:73
  540.1 16.7 %collective-permute-start.59 = (bf16[128,2560]{1,0:T(8,128)(2,1)S(1)}, bf16[128,2560]{1,0:T(8,128)(2,1)S(1)}, u32[]{:S(2)}, u32[]{:S(2)}) collective-permute-start(bf16[128,2560]{1,0:T(8,128)(2,1)S(1)} %fusion.31), channel_id=1, source_target_pairs={{0,2},{1,3},{2,0},{3,1},{4,6},{5,7},{6,4},{7,5},{8,10},{9,11},{10,... | collective-permute-start | bytes 1966088 | tf_op jit(solution)/shard_map/ppermute | solution.py:73
  (59 other events, 915.7 us)

commit v2 on v0

v2 whole, which is shorter than its diff:
```python
import jax
import jax.numpy as jnp
from jax import lax
from jax.experimental import pallas as pl
from jax.experimental.pallas import tpu as pltpu
from jax.sharding import PartitionSpec as P

HD = 80
PAGE = 128
BF = jnp.bfloat16
F32 = jnp.float32

eps_norm = 1e-05
theta_base = 10000.0

PAIR = 2
CHUNKS = (512,)


def normed(values, gain):
    scale = lax.rsqrt(jnp.mean(values * values, axis=-1, keepdims=True) + eps_norm)
    return (values * scale * gain).astype(BF)


def dot(a, b):
    return jnp.dot(a, b, preferred_element_type=F32)


def on_device(kernel, place, ins, shapes, vmem_mib, name):
    def run(place_ref, *refs):
        n_in, n_out = len(ins), len(shapes)
        outs, bufs, sems = refs[n_in : n_in + n_out], refs[n_in + n_out : -1], refs[-1]
        kernel(place_ref, *refs[:n_in], *bufs)
        copies = [pltpu.make_async_copy(bufs[i], outs[i], sems.at[i]) for i in range(n_out)]
        for copy in copies:
            copy.start()
        for copy in copies:
            copy.wait()

    return pl.pallas_call(
        run,
        in_specs=[pl.BlockSpec(memory_space=pltpu.SMEM)]
        + [pl.BlockSpec(memory_space=pltpu.VMEM)] * len(ins),
        out_specs=[pl.BlockSpec(memory_space=pltpu.HBM)] * len(shapes),
        out_shape=[jax.ShapeDtypeStruct(shape, BF) for shape in shapes],
        scratch_shapes=[pltpu.VMEM(shape, BF) for shape in shapes]
        + [pltpu.SemaphoreType.DMA((len(shapes),))],
        compiler_params=pltpu.CompilerParams(vmem_limit_bytes=vmem_mib * 2**20),
        name=name,
    )(place, *ins)


def split_qkv(place, shard, n_tp):
    rows, columns = shard.shape
    width = columns // n_tp

    def kernel(place_ref, shard_ref, *bufs):
        tp = place_ref[0]
        for s in range(n_tp):
            for g in range(n_tp):

                @pl.when((tp ^ s) == g)
                def _(s=s, g=g):
                    bufs[s][...] = shard_ref[:, g * width : (g + 1) * width].astype(BF)

    return on_device(kernel, place, [shard], [(rows, width)] * n_tp, 60, "split_qkv")


def split_gateup(place, shard, n_tp, halves, chunks):
    rows, columns = shard.shape
    width = columns // n_tp
    units = width // 2 // halves

    def kernel(place_ref, shard_ref, *bufs):
        tp = place_ref[0]
        for s in range(n_tp):
            begin = pl.multiple_of((tp ^ s) * width, 128)
            group = shard_ref[:, pl.ds(begin, width)].astype(BF)
            for q in range(halves):
                start = q * units
                edge = 0
                for size in chunks:
                    up = width // 2 + start
                    bufs[s % 2][s // 2, q, :, edge : edge + 2 * size] = jnp.concatenate(
                        [group[:, start : start + size], group[:, up : up + size]], axis=1
                    )
                    start += size
                    edge += 2 * size

    shapes = [(n_tp // 2, halves, rows, 2 * units)] * 2
    return on_device(kernel, place, [shard], shapes, 60, "split_gateup")


def pack_far(place, own, near, chunks):
    n_far, halves, rows, _ = own.shape
    n_far -= 1

    def kernel(place_ref, own_ref, near_ref, *bufs):
        edge = 0
        for c, size in enumerate(chunks):
            for f in range(n_far):
                bufs[c][f, 0] = own_ref[f + 1, :, :, edge : edge + 2 * size]
                bufs[c][f, 1] = near_ref[f + 1, :, :, edge : edge + 2 * size]
            edge += 2 * size

    shapes = [(n_far, 2, halves, rows, 2 * size) for size in chunks]
    return on_device(kernel, place, [own, near], shapes, 60, "pack_far")


def join_qkv(place, parts):
    rows, columns = parts[0].shape
    n_tp = len(parts)

    def kernel(place_ref, *refs):
        for s in range(n_tp):
            refs[n_tp][place_ref[0] ^ s] = refs[s][...]

    out = on_device(kernel, place, parts, [(n_tp, rows, columns)], 60, "join_qkv")[0]
    return out.reshape(n_tp * rows, columns)


def join_gateup(place, own, near, far, start):
    n_far, _, halves, rows, columns = far.shape
    n_tp = 2 * n_far + 2

    def kernel(place_ref, own_ref, near_ref, far_ref, *bufs):
        tp, mine = place_ref[0], place_ref[1]
        for k in range(2):
            bufs[k][tp] = own_ref[0, mine ^ k, :, start : start + columns]
            bufs[k][tp ^ 1] = near_ref[0, mine ^ k, :, start : start + columns]
            for f in range(n_far):
                for j in range(2):
                    bufs[k][tp ^ (2 * f + 2 + j)] = far_ref[f, j, mine ^ k]

    shapes = [(n_tp, rows, columns)] * 2
    outs = on_device(kernel, place, [own, near, far], shapes, 60, "join_gateup")
    return [out.reshape(n_tp * rows, columns) for out in outs]


SMEM = pl.BlockSpec(memory_space=pltpu.SMEM)
VMEM = pl.BlockSpec(memory_space=pltpu.VMEM)


def call(kernel, smem, vmem, shapes, scratch, name, mib=48):
    return pl.pallas_call(
        kernel,
        in_specs=[SMEM] * len(smem) + [VMEM] * len(vmem),
        out_specs=[VMEM] * len(shapes),
        out_shape=[jax.ShapeDtypeStruct(*shape) for shape in shapes],
        scratch_shapes=[pltpu.VMEM(*shape) for shape in scratch],
        compiler_params=pltpu.CompilerParams(vmem_limit_bytes=mib * 2**20),
        cost_estimate=pl.CostEstimate(flops=1, transcendentals=0, bytes_accessed=1),
        name=name,
    )(*smem, *vmem)


def permute_columns(values, columns_at):
    rows, width = values.shape
    tile = 256

    def kernel(values_ref, at_ref, out_ref):
        @pl.loop(0, width // tile)
        def _(i):
            at = pl.ds(pl.multiple_of(i * tile, tile), tile)
            source = lax.broadcasted_iota(jnp.int32, (width, tile), 0)
            onehot = (source == at_ref[:, at]).astype(F32).astype(BF)
            out_ref[:, at] = dot(values_ref[...], onehot)

    return call(
        kernel, [], [values, columns_at[None]], [((rows, width), F32)], [], "permute_columns"
    )[0]


def attend(place, lengths, joined, x_last, w_last, tables, out_in, sizes, shares):
    seq_len, columns = joined.shape
    heads, kv_heads, head_dim = sizes
    group = heads // kv_heads
    q_cols, k_cols = heads * head_dim, kv_heads * head_dim
    half = head_dim // 2
    wide = tables[0].shape[1]
    width = w_last[0].shape[0]
    model_dim = out_in.shape[1]
    share = seq_len // len(shares)
    tile = 128

    def kernel(place_ref, length_ref, joined_ref, x_ref, cos_ref, sin_ref, out_in_ref, *refs):
        w_refs = refs[: len(w_last)]
        leaving_ref, staying_ref, cache_ref, qk, v, context = refs[len(w_last) :]
        tp, length = place_ref[0], length_ref[0]
        lane = lax.broadcasted_iota(jnp.int32, (tile, wide), 1)
        first = lax.rem(lane, head_dim) < half
        for t in range(seq_len // tile):
            at = slice(t * tile, (t + 1) * tile)
            rows = joined_ref[at, :]
            for i, w_ref in enumerate(w_refs):
                rows = rows + dot(x_ref[at, i * width : (i + 1) * width], w_ref[...])
            head = rows[:, :wide]
            ahead = pltpu.roll(head, wide - half, 1)
            behind = pltpu.roll(head, half, 1)
            turned = head * cos_ref[at, :] + jnp.where(first, -ahead, behind) * sin_ref[at, :]
            qk[at, :] = turned.astype(BF)
            v[at, :] = rows[:, q_cols + k_cols :].astype(BF)
            slot = t * tile + lax.broadcasted_iota(jnp.int32, (tile, 1), 0)
            live = (slot < length).astype(F32)
            cache_ref[at, :k_cols] = (turned[:, q_cols : q_cols + k_cols] * live).astype(BF)
            cache_ref[at, k_cols:] = (rows[:, q_cols + k_cols :] * live).astype(BF)
        for k in range(kv_heads):
            key_at = q_cols + k * head_dim
            for t in range(seq_len // tile):
                at = slice(t * tile, (t + 1) * tile)
                count = (t + 1) * tile
                q = jnp.concatenate(
                    [
                        qk[at, (k * group + g) * head_dim : (k * group + g + 1) * head_dim]
                        for g in range(group)
                    ],
                    axis=0,
                )
                scores = lax.dot_general(
                    q,
                    qk[:count, key_at : key_at + head_dim],
                    (((1,), (1,)), ((), ())),
                    preferred_element_type=F32,
                ) * head_dim ** (-0.5)
                shape = (tile, count)
                slot = t * tile + lax.broadcasted_iota(jnp.int32, shape, 0)
                key = lax.broadcasted_iota(jnp.int32, shape, 1)
                allowed = (key <= slot) & (key < length)
                scores = scores.reshape(group, tile, count)
                scores = jnp.where(allowed[None], scores, -1e30)
                top = jnp.max(scores, axis=-1, keepdims=True)
                weight = jnp.exp(scores - top)
                probs = (weight / jnp.sum(weight, axis=-1, keepdims=True)).astype(BF)
                mixed = dot(
                    probs.reshape(group * tile, count), v[:count, k * head_dim : (k + 1) * head_dim]
                ).astype(BF)
                for g in range(group):
                    h = k * group + g
                    context[at, h * head_dim : (h + 1) * head_dim] = mixed[
                        g * tile : (g + 1) * tile
                    ]
        for i, s in enumerate(shares):
            block = context[pl.ds(pl.multiple_of((tp ^ s) * share, share), share), :]
            product = dot(block, out_in_ref[...])
            j = i % (len(shares) // 2)
            if i < len(shares) // 2:
                staying_ref[j * share : (j + 1) * share, :] = product
            else:
                leaving_ref[j * share : (j + 1) * share, :] = product.astype(BF)

    return call(
        kernel,
        [place, lengths],
        [joined, x_last, *tables, out_in, *w_last],
        [
            ((seq_len // 2, model_dim), BF),
            ((seq_len // 2, model_dim), F32),
            ((seq_len, 2 * k_cols), BF),
        ],
        [((seq_len, wide), BF), ((seq_len, k_cols), BF), ((seq_len, q_cols), BF)],
        "attend",
    )


def gated(tokens, blocks):
    rows, model_dim = tokens.shape
    each, columns = blocks[0].shape
    size = columns // 2
    tile = 256

    def kernel(tokens_ref, *refs):
        out_ref, weight = refs[-2:]
        for i, ref in enumerate(refs[:-2]):
            weight[i * each : (i + 1) * each, :] = ref[...]

        @pl.loop(0, rows // tile)
        def _(i):
            at = pl.ds(pl.multiple_of(i * tile, tile), tile)
            projected = dot(tokens_ref[at, :], weight[...])
            gate, up = projected[:, :size], projected[:, size:]
            out_ref[at, :] = (gate / (1.0 + jnp.exp(-gate)) * up).astype(BF)

    return call(
        kernel, [], [tokens, *blocks], [((rows, size), BF)], [((model_dim, columns), BF)], "gated"
    )[0]


def down_product(place, kept, returned, weight):
    rows = kept[0].shape[0]
    units, model_dim = weight.shape[0] // 2, weight.shape[1]
    tile = 128

    def kernel(place_ref, *refs):
        ins = refs[: 2 * len(kept)]
        weight_ref, leaving_ref, staying_ref = refs[2 * len(kept) :]

        def product(at):
            total = 0.0
            for k in range(2):
                begin = (place_ref[1] ^ k) * units
                for ref in ins[k * len(kept) : (k + 1) * len(kept)]:
                    size = ref.shape[1]
                    total += dot(ref[at, :], weight_ref[pl.ds(pl.multiple_of(begin, 32), size), :])
                    begin += size
            return total

        @pl.loop(0, rows // 2 // tile)
        def _(i):
            out = pl.ds(pl.multiple_of(i * tile, tile), tile)
            leaving_ref[out, :] = product(
                pl.ds(pl.multiple_of(rows // 2 + i * tile, tile), tile)
            ).astype(BF)
            staying_ref[out, :] = product(out)

    return call(
        kernel,
        [place],
        [*kept, *returned, weight],
        [((rows // 2, model_dim), BF), ((rows // 2, model_dim), F32)],
        [],
        "down_product",
    )


def body(
    tokens,
    lengths,
    page_slot,
    trainer_layout,
    trainer_qkv,
    trainer_gateup,
    attn_gain,
    ffn_gain,
    out_proj,
    down_proj,
):
    n_tp = lax.axis_size("tp")
    n_req = lax.axis_size("req")
    devices = n_tp * n_req
    req = lax.axis_index("req")
    tp = lax.axis_index("tp")
    rows_each = trainer_qkv.shape[0]
    seq_len, model_dim = tokens.shape
    head_dim = HD
    local_heads = out_proj.shape[0] // head_dim
    group_cols = trainer_qkv.shape[1] // n_tp
    local_kv = (group_cols // head_dim - local_heads) // 2
    group = local_heads // local_kv
    q_cols = local_heads * head_dim
    k_cols = local_kv * head_dim
    ff_local = down_proj.shape[0]
    share = seq_len // n_tp

    def swap(value, req_mask, tp_mask):
        pairs = [(d, d ^ (req_mask * n_tp + tp_mask)) for d in range(devices)]
        return lax.ppermute(value, ("req", "tp"), pairs)

    def pick(stack, index):
        return lax.dynamic_index_in_dim(stack, index, 0, keepdims=False)

    def sync(values):
        return lax.optimization_barrier(values)

    halves = 2
    units = ff_local // halves
    chunks = list(CHUNKS) + [units - sum(CHUNKS)]
    bits = [1 << k for k in range(16) if 1 << k < n_tp]
    evens = list(range(2, n_req, 2))
    singles = [r for r in evens if r & (r - 1) == 0]
    doubles = [r for r in evens if r & (r - 1)]
    plain = [r for r in evens if not r & PAIR]
    crossed = [r for r in evens if r & PAIR and r != PAIR]

    def spread_z(held, group):
        for r in group:
            bit = r & -r
            held[r] = swap(held[r ^ bit], bit, 0)

    def spread_class(held, mine, other, group):
        for r in group:
            if r == PAIR:
                held[r] = swap(other, PAIR, 0)
                continue
            rest = r & ~PAIR
            bit = 1 << (rest.bit_length() - 1)
            held[r] = swap(held[r ^ bit] if r != bit else mine, bit, 0)

    place = jnp.stack([tp, (req // PAIR) % 2])
    qkv_split = split_qkv(place, trainer_qkv, n_tp)
    trainer_gateup, qkv_split = sync((trainer_gateup, qkv_split))
    gu_own, gu_odd = split_gateup(place, trainer_gateup, n_tp, halves, chunks)
    gu_near = swap(gu_odd, 0, 1)
    qkv_split = [qkv_split[0]] + [swap(qkv_split[s], 0, s) for s in range(1, n_tp)]
    st = sync(
        dict(
            qkv_split=qkv_split,
            gu_own=gu_own,
            gu_near=gu_near,
            tokens=tokens,
            layout=trainer_layout,
            slots=jnp.arange(seq_len, dtype=jnp.int32),
        )
    )

    tokens, trainer_layout, slots = st["tokens"], st["layout"], st["slots"]
    gu_own, gu_near = st["gu_own"], st["gu_near"]
    qkv_own = join_qkv(place, st["qkv_split"])
    qkv = {0: qkv_own}
    spread_z(qkv, singles)
    qkv[1] = swap(qkv_own, 1, 0)
    far = list(pack_far(place, gu_own, gu_near, chunks))
    for c in range(len(chunks)):
        moved = [swap(far[c][f], 0, 2 * f + 2) for f in range(n_tp // 2 - 1)]
        far[c] = jnp.stack(moved) if len(moved) > 1 else moved[0][None]
    order = jnp.arange(n_req, dtype=jnp.int32) ^ req
    shards = (order[:, None] * n_tp + jnp.arange(n_tp, dtype=jnp.int32)[None, :]).reshape(-1)
    blocks_at = trainer_layout[shards]
    columns_at = (
        blocks_at[:, None] * rows_each + jnp.arange(rows_each, dtype=jnp.int32)[None, :]
    ).reshape(-1)
    columns_back = (
        jnp.argmax(
            blocks_at[None, :] == jnp.arange(devices, dtype=jnp.int32)[:, None], axis=1
        ).astype(jnp.int32)[:, None]
        * rows_each
        + jnp.arange(rows_each, dtype=jnp.int32)[None, :]
    ).reshape(-1)
    tokens_in = permute_columns(tokens, columns_at)
    x_norm = normed(tokens_in, attn_gain.reshape(devices, rows_each)[blocks_at].reshape(-1))
    st = sync(
        dict(
            qkv=qkv,
            far=far,
            gu_own=gu_own,
            gu_near=gu_near,
            x_norm=x_norm,
            tokens_in=tokens_in,
            onehot_at=columns_at,
            out_proj=out_proj,
            page_slot=page_slot,
            ffn_gain=ffn_gain,
        )
    )

    qkv, far, x_norm, tokens_in = st["qkv"], st["far"], st["x_norm"], st["tokens_in"]
    columns_at, page_slot = st["onehot_at"], st["page_slot"]
    blocks = []
    for c in range(len(chunks)):
        blocks.append(
            join_gateup(place, st["gu_own"], st["gu_near"], far[c], 2 * sum(chunks[:c]))
        )
    spread_z(qkv, doubles)
    for r in singles[::-1]:
        qkv[r ^ 1] = swap(qkv[r], 1, 0)
    gu = [dict() for _ in chunks]
    spread_class(gu[0], *blocks[0], plain)
    out_in = permute_columns(st["out_proj"], columns_at).astype(BF)
    half = head_dim // 2
    wide = (q_cols + k_cols + 127) // 128 * 128
    lane = jnp.arange(wide, dtype=jnp.int32) % half
    freq = theta_base ** (-lane.astype(F32) * 2.0 / head_dim)
    angles = slots.astype(F32)[:, None] * freq[None, :]
    tables = (jnp.cos(angles), jnp.sin(angles))
    ffn_gain_in = st["ffn_gain"].reshape(devices, rows_each)[blocks_at].reshape(-1)
    n_pages = seq_len // PAGE
    holders = lax.dynamic_slice_in_dim(page_slot, req * n_pages, n_pages, 0) // n_pages
    relative = jnp.arange(n_req, dtype=jnp.int32) ^ req
    chosen = jnp.argmax(holders[None, :] == relative[:, None], axis=1)
    targets = req * n_pages + jnp.arange(n_pages, dtype=jnp.int32)
    source = jnp.argmax(page_slot[None, :] == targets[:, None], axis=1) // n_pages
    st = sync(
        dict(
            qkv=qkv,
            gu=gu,
            blocks=blocks,
            x_norm=x_norm,
            out_in=out_in,
            ffn_gain_in=ffn_gain_in,
            tables=tables,
            pages=(chosen, source),
        )
    )

    qkv, gu, blocks, x_norm, out_in = (st[k] for k in ("qkv", "gu", "blocks", "x_norm", "out_in"))
    chosen, source = st["pages"]
    spread_class(gu[0], *blocks[0], [PAIR])
    for r in doubles:
        qkv[r ^ 1] = swap(qkv[r], 1, 0)
    width = model_dim // n_req
    first = [0, 1] + [r | j for r in singles for j in (0, 1)]
    last = [r | j for r in doubles for j in (0, 1)]

    def part(rs):
        return dot(
            jnp.concatenate([x_norm[:, r * width : (r + 1) * width] for r in rs], axis=1),
            jnp.concatenate([qkv[r] for r in rs], axis=0),
        )

    joined = part(first)
    st = sync(
        dict(qkv=qkv, gu=gu, blocks=blocks, joined=joined, x_norm=x_norm, tables=st["tables"])
    )

    qkv, gu, blocks, x_norm = (st[k] for k in ("qkv", "gu", "blocks", "x_norm"))
    spread_class(gu[0], *blocks[0], crossed)
    spread_class(gu[1], *blocks[1], [PAIR])
    for c in range(len(chunks)):
        gu[c][0] = blocks[c][0]
        gu[c][1] = swap(blocks[c][0], 1, 0)
    shares = sorted(range(n_tp), key=lambda s: [(s >> k) & 1 for k in range(len(bits))])
    leaving, staying, cache_rows = attend(
        place,
        lengths,
        st["joined"],
        jnp.concatenate([x_norm[:, r * width : (r + 1) * width] for r in last], axis=1),
        [qkv[r] for r in last],
        st["tables"],
        out_in,
        (local_heads, local_kv, head_dim),
        shares,
    )
    st = sync(
        dict(gu=gu, blocks=blocks, leaving=leaving, staying=staying, pages=cache_rows, out=out_in)
    )

    def sum_rest(partial):
        for bit in bits[1:]:
            rows = partial.shape[0] // 2
            arrived = swap(partial[rows:].astype(BF), 0, bit)
            partial = partial[:rows] + arrived.astype(F32)
        return partial

    gu, blocks = st["gu"], st["blocks"]
    mixed = sum_rest(st["staying"] + swap(st["leaving"], 0, bits[0]).astype(F32))
    spread_class(gu[1], *blocks[1], plain)
    for r in plain:
        gu[0][r ^ 1] = swap(gu[0][r], 1, 0)
    resid_in = lax.dynamic_slice_in_dim(tokens_in, tp * share, share, 0) + mixed
    h_share = normed(resid_in, ffn_gain_in)
    box = st["pages"].reshape(n_pages, PAGE, 2 * k_cols)[chosen][:, None]
    st = sync(dict(gu=gu, h_share=h_share, resid_in=resid_in, box=box))

    def reordered(values):
        return jnp.concatenate(
            [values[:, (j ^ PAIR) * width : ((j ^ PAIR) + 1) * width] for j in range(n_req)], axis=1
        )

    def page_step(box, bit):
        box = box.reshape((-1, 2) + box.shape[1:])
        return jnp.concatenate([box[:, 0], swap(box[:, 1], bit, 0)], axis=1)

    gu, h_share, resid_in = st["gu"], st["h_share"], st["resid_in"]
    cross = n_tp // 2
    h_across = swap(h_share, 0, cross)
    h_pair = swap(reordered(h_share), PAIR, 0)
    spread_class(gu[1], None, None, crossed)
    gu[0][PAIR ^ 1] = swap(gu[0][PAIR], 1, 0)
    box = page_step(st["box"], 1)
    coarse = resid_in.astype(BF)
    fine = (resid_in - coarse.astype(F32)).astype(BF)
    terms = permute_columns(jnp.concatenate([coarse, fine], axis=0), columns_back)
    resid = terms[:share] + terms[share:]
    st = sync(dict(gu=gu, h=(h_share, h_across, h_pair), resid=resid, box=box))

    gu, resid, box = st["gu"], st["resid"], st["box"]
    h_share, h_across, h_pair = st["h"]
    cut = share // 2
    h_diag = jnp.concatenate(
        [swap(h_pair[:cut], 0, cross), swap(reordered(h_across[cut:]), PAIR, 0)], axis=0
    )
    for r in crossed:
        gu[0][r ^ 1] = swap(gu[0][r], 1, 0)
    gu[1][PAIR ^ 1] = swap(gu[1][PAIR], 1, 0)
    if n_req > 4:
        box = page_step(box, 2)
    st = sync(dict(gu=gu, own=(h_share, h_across), theirs=(h_pair, h_diag), resid=resid, box=box))

    gu, resid, box = st["gu"], st["resid"], st["box"]

    def whole(parts):
        rows = jnp.concatenate(parts, axis=0)
        for bit in range(1, cross):
            assert bit == 1
            rows = jnp.concatenate([rows, swap(rows, 0, bit)], axis=0)
        return rows

    h_own = whole(st["own"])
    h_theirs = whole(st["theirs"])
    for r in plain + crossed:
        gu[1][r ^ 1] = swap(gu[1][r], 1, 0)
    bit = 4
    while bit < n_req:
        box = page_step(box, bit)
        bit *= 2
    st = sync(
        dict(gu=gu, own=h_own, theirs=h_theirs, resid=resid, box=box)
    )

    h_own, h_theirs, resid, box = (st[k] for k in ("own", "theirs", "resid", "box"))
    weights = [[held[r] for r in range(n_req)] for held in st["gu"]]
    returned = [swap(gated(h_theirs, weight), PAIR, 0) for weight in weights]
    kept = [gated(h_own, weight) for weight in weights]
    leaving, staying = down_product(place, kept, returned, down_proj)
    arrived = swap(leaving, 0, bits[0])
    added = sum_rest(staying + arrived.astype(F32))
    share_slots = tp * share + jnp.arange(share, dtype=jnp.int32)
    live_share = (share_slots < lengths[0]).astype(F32)
    layer_out = ((resid + added) * live_share[:, None]).astype(BF)
    kv_cache = box[0][source ^ req]
    return (layer_out, kv_cache)


def solution(mesh):
    return jax.shard_map(
        body,
        mesh=mesh,
        in_specs=(
            P("req", None),
            P("req"),
            P(),
            P(),
            P(("req", "tp"), None),
            P(("req", "tp"), None),
            P(),
            P(),
            P("tp", None),
            P("tp", None),
        ),
        out_specs=(P(("req", "tp"), None), P("req", None, "tp")),
        check_vma=False,
    )
```

time: 733 us -> 330 us (0.45)
  waiting for transfers between devices: 551 us -> 131 us
  Pallas kernels: 0 us -> 91.9 us
  blocking collectives: 68.8 us -> 0 us
  matrix products: 52 us -> 3.56 us
  starting transfers between devices: 0.39 us -> 41.7 us
  other arithmetic: 19.8 us -> 37.7 us
  between operations: 14.7 us -> 1.93 us
    all_gather x3 -> x0, waiting for transfers between devices: 436 us -> none  [the longest x1 337 us: body(): lax.all_gather(gu_half, 'req', axis=0, tiled=True)]
    ppermute x0 -> x42, waiting for transfers between devices: none -> 131 us  [swap(): return lax.ppermute(value, ('req', 'tp'), pairs)]
    pallas_call x0 -> x15, Pallas kernels: none -> 91.9 us  [the longest x9 74.5 us: call(): pl.pallas_call(kernel, in_specs=[SMEM] * len(smem) + [VMEM] * len(vmem),...]
    all_to_all x2 -> x0, blocking collectives: 68.8 us -> none  [the longest x1 54.4 us: body(): lax.all_to_all(trainer_gateup.astype(jnp.bfloat16), 'tp', split_axis=1, c...]
    psum x1 -> x0, waiting for transfers between devices: 66.2 us -> none  [body(): mixed = lax.psum(partial_out, 'tp')]
    reduce_scatter x1 -> x0, waiting for transfers between devices: 48.3 us -> none  [body(): added = lax.psum_scatter(down, 'tp', scatter_dimension=0, tiled=True)]
    ppermute x0 -> x42, starting transfers between devices: none -> 41.7 us  [swap(): return lax.ppermute(value, ('req', 'tp'), pairs)]
    dot_general x6 -> x1, matrix products: 44.4 us -> 3.56 us  [dot(): return jnp.dot(a, b, preferred_element_type=F32)]
  transfers between devices with their start and end apart: 5 -> 42, of which waited for: 5 -> 20; matrix products, arithmetic and copies ran while one was open for 8% -> 15% of each run, Pallas kernels for 0% -> 21%
where the time goes in v2:
time: 330 us; the launch traced here: 329 us
  waiting for transfers between devices  131 us (40%)
  Pallas kernels  91.9 us (28%)
  starting transfers between devices  41.7 us (13%)
  other arithmetic  37.7 us (11%)
  local copies, waits for them, and re-layouts  21.9 us (7%)
  matrix products  3.56 us (1%)
    ppermute x42, waiting for transfers between devices, swap(): return lax.ppermute(value, ('req', 'tp'), pairs)  131 us
    pallas_call x9, Pallas kernels, call(): pl.pallas_call(kernel, in_specs=[SMEM] * len(smem) + [VMEM] * len(vmem),...  74.5 us
    ppermute x42, starting transfers between devices, swap(): return lax.ppermute(value, ('req', 'tp'), pairs)  41.7 us
    pallas_call x6, Pallas kernels, on_device(): pl.pallas_call(run, in_specs=[pl.BlockSpec(memory_space=pltpu.SMEM)] + [p...  17.4 us
    unnamed x51, local copies, waits for them, and re-layouts  8.69 us
    sin x1, other arithmetic, body(): tables = (jnp.cos(angles), jnp.sin(angles))  7.77 us
  transfers between devices with their start and end apart: 42, of which 20 were waited for; matrix products, arithmetic and copies ran while one was open for 15% of the time, Pallas kernels for 21%

profile of v2, /device:TPU:0, one launch (start us, length us, event | category | flops | bytes accessed | tf_op | source)
XLA Modules:
  0.0 329.5 jit_solution(6973119510543896468)
XLA Ops:
  1.3 2.5 split_qkv.1
  3.8 4.4 %split_gateup.1 = (bf16[2,2,80,1728]{3,2,1,0:T(8,128)(2,1)}, bf16[2,2,80,1728]{3,2,1,0:T(8,128)(2,1)}) custom-call(s32[2]{0:T(128)} %pad_add_fusion.place_ref, f32[80,13824]{1,0:T(8,128)} %refs_0_.2), custom_call_target="tpu_custom_call" | custom-call | tf_op jit(solution)/shard_map/split_gateup/pallas_call | solution.py:40
  8.8 2.9 collective-permute-start.2
  12.1 4.9 %collective-permute-done.2.refs_2_ = bf16[80,960]{1,0:T(8,128)(2,1)S(1)} collective-permute-done((bf16[80,960]{1,0:T(8,128)(2,1)}, bf16[80,960]{1,0:T(8,128)(2,1)S(1)}, u32[]{:S(2)}, u32[]{:S(2)}) %collective-permute-start.2) | collective-permute-done | bytes 153632 | tf_op jit(solution)/shard_map/ppermute | solution.py:356
  17.0 2.4 collective-permute-done.3.refs_3_
  20.1 2.1 join_qkv.1
  25.2 2.6 collective-permute-start.8
  28.0 10.8 %permute_columns.3 = f32[512,2560]{1,0:T(8,128)} custom-call(bf16[512,2560]{1,0:T(8,128)(2,1)S(1)} %copy-done.4, s32[1,2560]{1,0:T(1,128)S(1)} %add.197.at_ref), custom_call_target="tpu_custom_call" | custom-call | flops 1 | bytes 1 | tf_op jit(solution)/shard_map/permute_columns/pallas_call | solution.py:145
  38.8 2.9 multiply_reduce_fusion
  42.4 2.7 pack_far.1
  47.2 4.5 %multiply_convert_fusion = bf16[512,2560]{1,0:T(8,128)(2,1)} fusion(f32[512,2560]{1,0:T(8,128)} %permute_columns.3, f32[2560]{0:T(1024)S(1)} %mul.99, f32[512]{0:T(512)S(1)} %add_rsqrt_fusion), kind=kLoop, calls=%fused_computation.5 | loop fusion | flops 3932160 | bytes 7876608 | tf_op jit(solution)/shard_map/convert_element_type | solution.py:22
  51.7 7.8 %multiply_sine_fusion = (f32[512,896]{1,0:T(8,128)}, f32[512,896]{1,0:T(8,128)S(1)}) fusion(f32[896]{0:T(1024)S(1)} %fusion.9, f32[512]{0:T(512)S(1)} %convert_element_type.54), kind=kLoop, calls=%fused_computation.7 | loop fusion | flops 458752 | bytes 3675648 | tf_op jit(solution)/shard_map/sin | solution.py:463
  59.5 12.9 %collective-permute-done.5 = bf16[2,2,80,704]{3,2,1,0:T(8,128)(2,1)S(1)} collective-permute-done((bf16[2,2,80,704]{3,2,1,0:T(8,128)(2,1)}, bf16[2,2,80,704]{3,2,1,0:T(8,128)(2,1)S(1)}, u32[]{:S(2)}, u32[]{:S(2)}) %collective-permute-start.5) | collective-permute-done | bytes 450592 | tf_op jit(solution)/shard_map/ppermute | solution.py:356
  73.5 3.0 join_gateup.2
  79.1 1.9 copy-done.2
  81.0 12.9 %permute_columns.4 = f32[640,2560]{1,0:T(8,128)} custom-call(bf16[640,2560]{1,0:T(8,128)(2,1)S(1)} %copy-done.2, s32[1,2560]{1,0:T(1,128)S(1)} %broadcast_in_dim.14.at_ref), custom_call_target="tpu_custom_call" | custom-call | flops 1 | bytes 1 | tf_op jit(solution)/shard_map/permute_columns/pallas_call | solution.py:145
  93.9 4.9 %convert_element_type.53.out_in_ref = bf16[640,2560]{1,0:T(8,128)(2,1)} convert(f32[640,2560]{1,0:T(8,128)} %permute_columns.4) | non-fusion elementwise | flops 1638400 | bytes 9830400 | tf_op jit(solution)/shard_map/convert_element_type | solution.py:457
  98.9 2.9 join_gateup.3
  103.0 4.2 %collective-permute-done.9.refs_4_ = bf16[320,1024]{1,0:T(8,128)(2,1)S(1)} collective-permute-done((bf16[320,1024]{1,0:T(8,128)(2,1)}, bf16[320,1024]{1,0:T(8,128)(2,1)S(1)}, u32[]{:S(2)}, u32[]{:S(2)}) %collective-permute-start.9) | collective-permute-done | bytes 655392 | tf_op jit(solution)/shard_map/ppermute | solution.py:356
  114.3 3.6 %fusion = f32[512,960]{0,1:T(8,128)} fusion(bf16[1920,960]{1,0:T(8,128)(2,1)S(1)} %constant_dynamic-update-slice_fusion, bf16[512,2560]{1,0:T(8,128)(2,1)S(1)} %copy-done.9), kind=kOutput, calls=%fused_computation.13 | convolution fusion | flops 1887436800 | bytes 7864320 | tf_op jit(solution)/shard_map/dot_general | solution.py:26
  117.9 4.3 %collective-permute-done.14.refs_1_ = bf16[320,960]{1,0:T(8,128)(2,1)S(1)} collective-permute-done((bf16[320,960]{1,0:T(8,128)(2,1)}, bf16[320,960]{1,0:T(8,128)(2,1)S(1)}, u32[]{:S(2)}, u32[]{:S(2)}) %collective-permute-start.14) | collective-permute-done | bytes 614432 | tf_op jit(solution)/shard_map/ppermute | solution.py:356
  127.4 2.9 copy.33.joined_ref
  132.5 14.8 %attend.1 = (bf16[256,2560]{1,0:T(8,128)(2,1)}, f32[256,2560]{1,0:T(8,128)}, bf16[512,320]{1,0:T(8,128)(2,1)S(1)}) custom-call(s32[2]{0:T(128)S(1)} %copy-done.7, s32[1]{0:T(128)} %copy.53.length_ref, f32[512,960]{1,0:T(8,128)} %copy.33.joined_ref, bf16[512,640]{1,0:T(8,128)(2,1)S(1)} %concatenate.46.x_ref, f32[512,896]{1,0:T(8,128)S(1)} %get-tuple-element.223.cos_ref, ...), custom_call_target="tpu_custom_call" | custom-call | flops 1 | bytes 1 | tf_op jit(solution)/shard_map/attend/pallas_call | solution.py:145
  147.5 4.7 %collective-permute-done.16.refs_6_ = bf16[320,1024]{1,0:T(8,128)(2,1)} collective-permute-done((bf16[320,1024]{1,0:T(8,128)(2,1)}, bf16[320,1024]{1,0:T(8,128)(2,1)}, u32[]{:S(2)}, u32[]{:S(2)}) %collective-permute-start.16) | collective-permute-done | bytes 655392 | tf_op jit(solution)/shard_map/ppermute | solution.py:356
  152.8 2.6 collective-permute-done.21
  155.4 2.1 convert_add_fusion.1
  164.4 11.2 %collective-permute-done.22 = bf16[128,2560]{1,0:T(8,128)(2,1)} collective-permute-done((bf16[128,2560]{1,0:T(8,128)(2,1)}, bf16[128,2560]{1,0:T(8,128)(2,1)}, u32[]{:S(2)}, u32[]{:S(2)}) %collective-permute-start.22) | collective-permute-done | bytes 655392 | tf_op jit(solution)/shard_map/ppermute | solution.py:356
  175.6 2.2 multiply_reduce_fusion.1
  178.0 8.3 %collective-permute-done.20.refs_4_ = bf16[320,704]{1,0:T(8,128)(2,1)S(1)} collective-permute-done((bf16[320,704]{1,0:T(8,128)(2,1)}, bf16[320,704]{1,0:T(8,128)(2,1)S(1)}, u32[]{:S(2)}, u32[]{:S(2)}) %collective-permute-start.20) | collective-permute-done | bytes 450592 | tf_op jit(solution)/shard_map/ppermute | solution.py:356
  190.0 3.3 collective-permute-start.25
  193.2 5.4 %permute_columns.5 = f32[256,2560]{1,0:T(8,128)S(1)} custom-call(bf16[256,2560]{1,0:T(8,128)(2,1)S(1)} %pad_maximum_fusion.2.values_ref, s32[1,2560]{1,0:T(1,128)S(1)} %add.215.at_ref), custom_call_target="tpu_custom_call" | custom-call | flops 1 | bytes 1 | tf_op jit(solution)/shard_map/permute_columns/pallas_call | solution.py:145
  199.9 12.7 %collective-permute-done.25.refs_6_ = bf16[320,704]{1,0:T(8,128)(2,1)S(1)} collective-permute-done((bf16[320,704]{1,0:T(8,128)(2,1)}, bf16[320,704]{1,0:T(8,128)(2,1)S(1)}, u32[]{:S(2)}, u32[]{:S(2)}) %collective-permute-start.25) | collective-permute-done | bytes 450592 | tf_op jit(solution)/shard_map/ppermute | solution.py:356
  212.5 2.1 collective-permute-done.27
  220.2 5.3 %collective-permute-done.28 = bf16[2,2,128,320]{2,3,1,0:T(8,128)(2,1)S(1)} collective-permute-done((bf16[2,2,128,320]{2,3,1,0:T(8,128)(2,1)S(1)}, bf16[2,2,128,320]{2,3,1,0:T(8,128)(2,1)S(1)}, u32[]{:S(2)}, u32[]{:S(2)}) %collective-permute-start.28) | collective-permute-done | bytes 327712 | tf_op jit(solution)/shard_map/ppermute | solution.py:356
  225.5 4.8 %collective-permute-done.32 = bf16[64,2560]{1,0:T(8,128)(2,1)S(1)} collective-permute-done((bf16[64,2560]{1,0:T(8,128)(2,1)S(1)}, bf16[64,2560]{1,0:T(8,128)(2,1)S(1)}, u32[]{:S(2)}, u32[]{:S(2)}) %collective-permute-start.32) | collective-permute-done | bytes 327712 | tf_op jit(solution)/shard_map/ppermute | solution.py:356
  230.4 13.1 %collective-permute-done.30.refs_3_ = bf16[320,704]{1,0:T(8,128)(2,1)S(1)} collective-permute-done((bf16[320,704]{1,0:T(8,128)(2,1)}, bf16[320,704]{1,0:T(8,128)(2,1)S(1)}, u32[]{:S(2)}, u32[]{:S(2)}) %collective-permute-start.30) | collective-permute-done | bytes 450592 | tf_op jit(solution)/shard_map/ppermute | solution.py:356
  247.9 14.0 %collective-permute-done.33 = bf16[1,4,128,320]{2,3,1,0:T(8,128)(2,1)S(1)} collective-permute-done((bf16[1,4,128,320]{2,3,1,0:T(8,128)(2,1)S(1)}, bf16[1,4,128,320]{2,3,1,0:T(8,128)(2,1)S(1)}, u32[]{:S(2)}, u32[]{:S(2)}) %collective-permute-start.33) | collective-permute-done | bytes 327712 | tf_op jit(solution)/shard_map/ppermute | solution.py:356
  266.2 3.1 collective-permute-done.35.refs_7_
  269.3 5.7 %gated.6 = bf16[512,512]{1,0:T(8,128)(2,1)S(1)} custom-call(bf16[512,2560]{1,0:T(8,128)(2,1)} %pad_maximum_fusion.1.tokens_ref, bf16[320,1024]{1,0:T(8,128)(2,1)S(1)} %bitcast.46, bf16[320,1024]{1,0:T(8,128)(2,1)} %collective-permute-done.15.refs_1_, bf16[320,1024]{1,0:T(8,128)(2,1)} %collective-permute-done.13.refs_2_, ...), custom_call_target="tpu_custom_call" | custom-call | flops 1 | bytes 1 | tf_op jit(solution)/shard_map/gated/pallas_call | solution.py:145
  276.6 5.0 %gated.7 = bf16[512,352]{1,0:T(8,128)(2,1)S(1)} custom-call(bf16[512,2560]{1,0:T(8,128)(2,1)} %pad_maximum_fusion.1.tokens_ref, bf16[320,704]{1,0:T(8,128)(2,1)} %bitcast.12.refs_0_, bf16[320,704]{1,0:T(8,128)(2,1)} %collective-permute-done.17.refs_1_, bf16[320,704]{1,0:T(8,128)(2,1)} %collective-permute-done.18.refs_2_, ...), custom_call_target="tpu_custom_call" | custom-call | flops 1 | bytes 1 | tf_op jit(solution)/shard_map/gated/pallas_call | solution.py:145
  282.2 5.0 %gated.5.refs_1_ = bf16[512,352]{1,0:T(8,128)(2,1)S(1)} custom-call(bf16[512,2560]{1,0:T(8,128)(2,1)} %pad_maximum_fusion.tokens_ref, bf16[320,704]{1,0:T(8,128)(2,1)} %bitcast.12.refs_0_, bf16[320,704]{1,0:T(8,128)(2,1)} %collective-permute-done.17.refs_1_, bf16[320,704]{1,0:T(8,128)(2,1)} %collective-permute-done.18.refs_2_, ...), custom_call_target="tpu_custom_call" | custom-call | flops 1 | bytes 1 | tf_op jit(solution)/shard_map/gated/pallas_call | solution.py:145
  287.2 5.7 %gated.4.refs_0_ = bf16[512,512]{1,0:T(8,128)(2,1)S(1)} custom-call(bf16[512,2560]{1,0:T(8,128)(2,1)} %pad_maximum_fusion.tokens_ref, bf16[320,1024]{1,0:T(8,128)(2,1)S(1)} %bitcast.47, bf16[320,1024]{1,0:T(8,128)(2,1)} %collective-permute-done.15.refs_1_, bf16[320,1024]{1,0:T(8,128)(2,1)} %collective-permute-done.13.refs_2_, ...), custom_call_target="tpu_custom_call" | custom-call | flops 1 | bytes 1 | tf_op jit(solution)/shard_map/gated/pallas_call | solution.py:145
  292.8 3.3 %collective-permute-done.39.refs_3_ = bf16[512,352]{1,0:T(8,128)(2,1)S(1)} collective-permute-done((bf16[512,352]{1,0:T(8,128)(2,1)S(1)}, bf16[512,352]{1,0:T(8,128)(2,1)S(1)}, u32[]{:S(2)}, u32[]{:S(2)}) %collective-permute-start.39) | collective-permute-done | bytes 360480 | tf_op jit(solution)/shard_map/ppermute | solution.py:356
  296.2 9.3 %down_product.1 = (bf16[256,2560]{1,0:T(8,128)(2,1)S(1)}, f32[256,2560]{1,0:T(8,128)S(1)}) custom-call(s32[2]{0:T(128)S(1)} %copy-done.7, bf16[512,512]{1,0:T(8,128)(2,1)S(1)} %gated.4.refs_0_, bf16[512,352]{1,0:T(8,128)(2,1)S(1)} %gated.5.refs_1_, bf16[512,512]{1,0:T(8,128)(2,1)S(1)} %collective-permute-done.38.refs_2_, ...), custom_call_target="tpu_custom_call" | custom-call | flops 1 | bytes 1 | tf_op jit(solution)/shard_map/down_product/pallas_call | solution.py:145
  305.5 3.0 collective-permute-done.40
  310.8 2.4 gather_fusion.4
  313.2 13.7 %collective-permute-done.41 = bf16[128,2560]{1,0:T(8,128)(2,1)} collective-permute-done((bf16[128,2560]{1,0:T(8,128)(2,1)}, bf16[128,2560]{1,0:T(8,128)(2,1)}, u32[]{:S(2)}, u32[]{:S(2)}) %collective-permute-start.41) | collective-permute-done | bytes 655392 | tf_op jit(solution)/shard_map/ppermute | solution.py:356
  326.9 2.6 fusion.4
  (178 shorter events, 58.5 us)
Async XLA Ops:
  0.6 18.7 %copy-start = (s32[32]{0:T(128)S(1)}, s32[32]{0:T(128)}, u32[]{:S(2)}) copy-start(s32[32]{0:T(128)} %param.13) | copy-start | bytes 388
  1.3 10.7 %copy-start.16 = (f32[2560]{0:T(1024)S(1)}, f32[2560]{0:T(1024)}, u32[]{:S(2)}) copy-start(f32[2560]{0:T(1024)} %param.16) | copy-start | bytes 30724
  3.8 24.2 %copy-start.4 = (bf16[512,2560]{1,0:T(8,128)(2,1)S(1)}, bf16[512,2560]{1,0:T(8,128)(2,1)}, u32[]{:S(2)}) copy-start(bf16[512,2560]{1,0:T(8,128)(2,1)} %values_ref) | copy-start | bytes 7864324
  8.2 11.1 %collective-permute-start = (bf16[2,2,80,1728]{3,2,1,0:T(8,128)(2,1)}, bf16[2,2,80,1728]{3,2,1,0:T(8,128)(2,1)}, u32[]{:S(2)}, u32[]{:S(2)}) collective-permute-start(bf16[2,2,80,1728]{3,2,1,0:T(8,128)(2,1)} %get-tuple-element.166), channel_id=1, source_target_pairs={{0,1},{1,0},{2,3},{3,2},{4,5},{5,4},{6,7},{7,6},{8,9},{9,8},{10,11... | collective-permute-start | bytes 3317768 | tf_op jit(solution)/shard_map/ppermute | solution.py:356
  8.7 3.3 %collective-permute-start.1 = (bf16[80,960]{1,0:T(8,128)(2,1)}, bf16[80,960]{1,0:T(8,128)(2,1)S(1)}, u32[]{:S(2)}, u32[]{:S(2)}) collective-permute-start(bf16[80,960]{1,0:T(8,128)(2,1)} %get-tuple-element.169), channel_id=1, source_target_pairs={{0,1},{1,0},{2,3},{3,2},{4,5},{5,4},{6,7},{7,6},{8,9},{9,8},{10,11... | collective-permute-start | bytes 460808 | tf_op jit(solution)/shard_map/ppermute | solution.py:356
  8.8 8.1 %collective-permute-start.2 = (bf16[80,960]{1,0:T(8,128)(2,1)}, bf16[80,960]{1,0:T(8,128)(2,1)S(1)}, u32[]{:S(2)}, u32[]{:S(2)}) collective-permute-start(bf16[80,960]{1,0:T(8,128)(2,1)} %get-tuple-element.170), channel_id=1, source_target_pairs={{0,2},{1,3},{2,0},{3,1},{4,6},{5,7},{6,4},{7,5},{8,10},{9,11},{10,... | collective-permute-start | bytes 460808 | tf_op jit(solution)/shard_map/ppermute | solution.py:356
  11.8 7.6 %collective-permute-start.3 = (bf16[80,960]{1,0:T(8,128)(2,1)S(1)}, bf16[80,960]{1,0:T(8,128)(2,1)S(1)}, u32[]{:S(2)}, u32[]{:S(2)}) collective-permute-start(bf16[80,960]{1,0:T(8,128)(2,1)S(1)} %copy-done.20), channel_id=1, source_target_pairs={{0,3},{1,2},{2,1},{3,0},{4,7},{5,6},{6,5},{7,4},{8,11},{9,10},{10,... | collective-permute-start | bytes 460808 | tf_op jit(solution)/shard_map/ppermute | solution.py:356
  22.2 50.2 %collective-permute-start.6 = (bf16[320,960]{1,0:T(8,128)(2,1)}, bf16[320,960]{1,0:T(8,128)(2,1)}, u32[]{:S(2)}, u32[]{:S(2)}) collective-permute-start(bf16[320,960]{1,0:T(8,128)(2,1)} %bitcast.50), channel_id=1, source_target_pairs={{0,4},{1,5},{2,6},{3,7},{4,0},{5,1},{6,2},{7,3},{8,12},{9,13},{10,... | collective-permute-start | bytes 1843208 | tf_op jit(solution)/shard_map/ppermute | solution.py:356
  23.6 48.7 %collective-permute-start.7 = (bf16[320,960]{1,0:T(8,128)(2,1)}, bf16[320,960]{1,0:T(8,128)(2,1)}, u32[]{:S(2)}, u32[]{:S(2)}) collective-permute-start(bf16[320,960]{1,0:T(8,128)(2,1)} %bitcast.51), channel_id=1, source_target_pairs={{0,8},{1,9},{2,10},{3,11},{4,12},{5,13},{6,14},{7,15},{8,0},{9,1},... | collective-permute-start | bytes 1843208 | tf_op jit(solution)/shard_map/ppermute | solution.py:356
  25.2 47.2 %collective-permute-start.8 = (bf16[320,960]{1,0:T(8,128)(2,1)}, bf16[320,960]{1,0:T(8,128)(2,1)}, u32[]{:S(2)}, u32[]{:S(2)}) collective-permute-start(bf16[320,960]{1,0:T(8,128)(2,1)} %bitcast.52), channel_id=1, source_target_pairs={{0,16},{1,17},{2,18},{3,19},{4,20},{5,21},{6,22},{7,23},{8,24},{9,... | collective-permute-start | bytes 1843208 | tf_op jit(solution)/shard_map/ppermute | solution.py:356
  45.1 27.3 %collective-permute-start.4 = (bf16[2,2,80,1024]{3,2,1,0:T(8,128)(2,1)}, bf16[2,2,80,1024]{3,2,1,0:T(8,128)(2,1)S(1)}, u32[]{:S(2)}, u32[]{:S(2)}) collective-permute-start(bf16[2,2,80,1024]{3,2,1,0:T(8,128)(2,1)} %bitcast.62), channel_id=1, source_target_pairs={{0,2},{1,3},{2,0},{3,1},{4,6},{5,7},{6,4},{7,5},{8,10},{9,11},{10,... | collective-permute-start | bytes 1966088 | tf_op jit(solution)/shard_map/ppermute | solution.py:356
  46.6 25.7 %collective-permute-start.5 = (bf16[2,2,80,704]{3,2,1,0:T(8,128)(2,1)}, bf16[2,2,80,704]{3,2,1,0:T(8,128)(2,1)S(1)}, u32[]{:S(2)}, u32[]{:S(2)}) collective-permute-start(bf16[2,2,80,704]{3,2,1,0:T(8,128)(2,1)} %bitcast.63), channel_id=1, source_target_pairs={{0,2},{1,3},{2,0},{3,1},{4,6},{5,7},{6,4},{7,5},{8,10},{9,11},{10,... | collective-permute-start | bytes 1351688 | tf_op jit(solution)/shard_map/ppermute | solution.py:356
  51.7 26.6 %copy-start.18 = (s32[32]{0:T(128)S(1)}, s32[32]{0:T(128)}, u32[]{:S(2)}) copy-start(s32[32]{0:T(128)} %param.12) | copy-start | bytes 388
  72.4 26.5 %copy-start.12 = (bf16[2,2,80,704]{3,2,1,0:T(8,128)(2,1)}, bf16[2,2,80,704]{3,2,1,0:T(8,128)(2,1)S(1)}, u32[]{:S(2)}) copy-start(bf16[2,2,80,704]{3,2,1,0:T(8,128)(2,1)S(1)} %collective-permute-done.5) | copy-start | bytes 1351684
  72.4 30.6 %collective-permute-start.11 = (bf16[320,960]{1,0:T(8,128)(2,1)}, bf16[320,960]{1,0:T(8,128)(2,1)}, u32[]{:S(2)}, u32[]{:S(2)}) collective-permute-start(bf16[320,960]{1,0:T(8,128)(2,1)} %collective-permute-done.8), channel_id=1, source_target_pairs={{0,4},{1,5},{2,6},{3,7},{4,0},{5,1},{6,2},{7,3},{8,12},{9,13},{10,... | collective-permute-start | bytes 1843208 | tf_op jit(solution)/shard_map/ppermute | solution.py:356
  73.0 30.0 %collective-permute-start.12 = (bf16[320,960]{1,0:T(8,128)(2,1)}, bf16[320,960]{1,0:T(8,128)(2,1)}, u32[]{:S(2)}, u32[]{:S(2)}) collective-permute-start(bf16[320,960]{1,0:T(8,128)(2,1)} %collective-permute-done.8), channel_id=1, source_target_pairs={{0,8},{1,9},{2,10},{3,11},{4,12},{5,13},{6,14},{7,15},{8,0},{9,1},... | collective-permute-start | bytes 1843208 | tf_op jit(solution)/shard_map/ppermute | solution.py:356
  76.4 30.8 %collective-permute-start.9 = (bf16[320,1024]{1,0:T(8,128)(2,1)}, bf16[320,1024]{1,0:T(8,128)(2,1)S(1)}, u32[]{:S(2)}, u32[]{:S(2)}) collective-permute-start(bf16[320,1024]{1,0:T(8,128)(2,1)} %bitcast.44), channel_id=1, source_target_pairs={{0,16},{1,17},{2,18},{3,19},{4,20},{5,21},{6,22},{7,23},{8,24},{9,... | collective-permute-start | bytes 1966088 | tf_op jit(solution)/shard_map/ppermute | solution.py:356
  76.8 26.2 %collective-permute-start.10 = (bf16[320,960]{1,0:T(8,128)(2,1)}, bf16[320,960]{1,0:T(8,128)(2,1)}, u32[]{:S(2)}, u32[]{:S(2)}) collective-permute-start(bf16[320,960]{1,0:T(8,128)(2,1)} %collective-permute-done.7), channel_id=1, source_target_pairs={{0,4},{1,5},{2,6},{3,7},{4,0},{5,1},{6,2},{7,3},{8,12},{9,13},{10,... | collective-permute-start | bytes 1843208 | tf_op jit(solution)/shard_map/ppermute | solution.py:356
  107.2 15.8 %collective-permute-start.13 = (bf16[320,1024]{1,0:T(8,128)(2,1)}, bf16[320,1024]{1,0:T(8,128)(2,1)}, u32[]{:S(2)}, u32[]{:S(2)}) collective-permute-start(bf16[320,1024]{1,0:T(8,128)(2,1)} %bitcast.61), channel_id=1, source_target_pairs={{0,8},{1,9},{2,10},{3,11},{4,12},{5,13},{6,14},{7,15},{8,0},{9,1},... | collective-permute-start | bytes 1966088 | tf_op jit(solution)/shard_map/ppermute | solution.py:356
  107.3 14.9 %collective-permute-start.14 = (bf16[320,960]{1,0:T(8,128)(2,1)}, bf16[320,960]{1,0:T(8,128)(2,1)S(1)}, u32[]{:S(2)}, u32[]{:S(2)}) collective-permute-start(bf16[320,960]{1,0:T(8,128)(2,1)} %collective-permute-done.12.refs_0_), channel_id=1, source_target_pairs={{0,4},{1,5},{2,6},{3,7},{4,0},{5,1},{6,2},{7,3},{8,12},{9,13},{10,... | collective-permute-start | bytes 1843208 | tf_op jit(solution)/shard_map/ppermute | solution.py:356
  123.0 24.4 %collective-permute-start.15 = (bf16[320,1024]{1,0:T(8,128)(2,1)S(1)}, bf16[320,1024]{1,0:T(8,128)(2,1)}, u32[]{:S(2)}, u32[]{:S(2)}) collective-permute-start(bf16[320,1024]{1,0:T(8,128)(2,1)S(1)} %bitcast.45), channel_id=1, source_target_pairs={{0,4},{1,5},{2,6},{3,7},{4,0},{5,1},{6,2},{7,3},{8,12},{9,13},{10,... | collective-permute-start | bytes 1966088 | tf_op jit(solution)/shard_map/ppermute | solution.py:356
  123.7 28.4 %collective-permute-start.16 = (bf16[320,1024]{1,0:T(8,128)(2,1)}, bf16[320,1024]{1,0:T(8,128)(2,1)}, u32[]{:S(2)}, u32[]{:S(2)}) collective-permute-start(bf16[320,1024]{1,0:T(8,128)(2,1)} %collective-permute-done.13.refs_2_), channel_id=1, source_target_pairs={{0,16},{1,17},{2,18},{3,19},{4,20},{5,21},{6,22},{7,23},{8,24},{9,... | collective-permute-start | bytes 1966088 | tf_op jit(solution)/shard_map/ppermute | solution.py:356
  125.3 22.2 %collective-permute-start.17 = (bf16[320,704]{1,0:T(8,128)(2,1)}, bf16[320,704]{1,0:T(8,128)(2,1)}, u32[]{:S(2)}, u32[]{:S(2)}) collective-permute-start(bf16[320,704]{1,0:T(8,128)(2,1)} %bitcast.12.refs_0_), channel_id=1, source_target_pairs={{0,4},{1,5},{2,6},{3,7},{4,0},{5,1},{6,2},{7,3},{8,12},{9,13},{10,... | collective-permute-start | bytes 1351688 | tf_op jit(solution)/shard_map/ppermute | solution.py:356
  125.8 21.6 %collective-permute-start.18 = (bf16[320,704]{1,0:T(8,128)(2,1)}, bf16[320,704]{1,0:T(8,128)(2,1)}, u32[]{:S(2)}, u32[]{:S(2)}) collective-permute-start(bf16[320,704]{1,0:T(8,128)(2,1)} %bitcast.13), channel_id=1, source_target_pairs={{0,8},{1,9},{2,10},{3,11},{4,12},{5,13},{6,14},{7,15},{8,0},{9,1},... | collective-permute-start | bytes 1351688 | tf_op jit(solution)/shard_map/ppermute | solution.py:356
  152.2 3.2 collective-permute-start.21
  158.5 17.1 %collective-permute-start.22 = (bf16[128,2560]{1,0:T(8,128)(2,1)}, bf16[128,2560]{1,0:T(8,128)(2,1)}, u32[]{:S(2)}, u32[]{:S(2)}) collective-permute-start(bf16[128,2560]{1,0:T(8,128)(2,1)} %slice.167), channel_id=1, source_target_pairs={{0,2},{1,3},{2,0},{3,1},{4,6},{5,7},{6,4},{7,5},{8,10},{9,11},{10,... | collective-permute-start | bytes 1966088 | tf_op jit(solution)/shard_map/ppermute | solution.py:356
  161.8 24.6 %collective-permute-start.19 = (bf16[320,1024]{1,0:T(8,128)(2,1)S(1)}, bf16[320,1024]{1,0:T(8,128)(2,1)S(1)}, u32[]{:S(2)}, u32[]{:S(2)}) collective-permute-start(bf16[320,1024]{1,0:T(8,128)(2,1)S(1)} %collective-permute-done.9.refs_4_), channel_id=1, source_target_pairs={{0,4},{1,5},{2,6},{3,7},{4,0},{5,1},{6,2},{7,3},{8,12},{9,13},{10,... | collective-permute-start | bytes 1966088 | tf_op jit(solution)/shard_map/ppermute | solution.py:356
  163.6 22.8 %collective-permute-start.20 = (bf16[320,704]{1,0:T(8,128)(2,1)}, bf16[320,704]{1,0:T(8,128)(2,1)S(1)}, u32[]{:S(2)}, u32[]{:S(2)}) collective-permute-start(bf16[320,704]{1,0:T(8,128)(2,1)} %bitcast.12.refs_0_), channel_id=1, source_target_pairs={{0,16},{1,17},{2,18},{3,19},{4,20},{5,21},{6,22},{7,23},{8,24},{9,... | collective-permute-start | bytes 1351688 | tf_op jit(solution)/shard_map/ppermute | solution.py:356
  186.4 28.2 %collective-permute-start.26 = (bf16[128,2560]{1,0:T(8,128)(2,1)S(1)}, bf16[128,2560]{1,0:T(8,128)(2,1)S(1)}, u32[]{:S(2)}, u32[]{:S(2)}) collective-permute-start(bf16[128,2560]{1,0:T(8,128)(2,1)S(1)} %multiply_convert_fusion.1), channel_id=1, source_target_pairs={{0,2},{1,3},{2,0},{3,1},{4,6},{5,7},{6,4},{7,5},{8,10},{9,11},{10,... | collective-permute-start | bytes 1966088 | tf_op jit(solution)/shard_map/ppermute | solution.py:356
  187.7 27.0 %collective-permute-start.27 = (bf16[128,2560]{1,0:T(8,128)(2,1)S(1)}, bf16[128,2560]{1,0:T(8,128)(2,1)S(1)}, u32[]{:S(2)}, u32[]{:S(2)}) collective-permute-start(bf16[128,2560]{1,0:T(8,128)(2,1)S(1)} %pad_maximum_fusion.6), channel_id=1, source_target_pairs={{0,8},{1,9},{2,10},{3,11},{4,12},{5,13},{6,14},{7,15},{8,0},{9,1},... | collective-permute-start | bytes 1966088 | tf_op jit(solution)/shard_map/ppermute | solution.py:356
  187.8 12.0 %collective-permute-start.23 = (bf16[4,1,128,320]{2,3,0,1:T(8,128)(2,1)S(1)}, bf16[4,1,128,320]{2,3,0,1:T(8,128)(2,1)S(1)}, u32[]{:S(2)}, u32[]{:S(2)}) collective-permute-start(bf16[4,1,128,320]{2,3,0,1:T(8,128)(2,1)S(1)} %get-tuple-element.337), channel_id=1, source_target_pairs={{0,4},{1,5},{2,6},{3,7},{4,0},{5,1},{6,2},{7,3},{8,12},{9,13},{10,... | collective-permute-start | bytes 983048 | tf_op jit(solution)/shard_map/ppermute | solution.py:356
  188.3 26.3 %collective-permute-start.24 = (bf16[320,1024]{1,0:T(8,128)(2,1)}, bf16[320,1024]{1,0:T(8,128)(2,1)S(1)}, u32[]{:S(2)}, u32[]{:S(2)}) collective-permute-start(bf16[320,1024]{1,0:T(8,128)(2,1)} %collective-permute-done.13.refs_2_), channel_id=1, source_target_pairs={{0,4},{1,5},{2,6},{3,7},{4,0},{5,1},{6,2},{7,3},{8,12},{9,13},{10,... | collective-permute-start | bytes 1966088 | tf_op jit(solution)/shard_map/ppermute | solution.py:356
  190.0 22.6 %collective-permute-start.25 = (bf16[320,704]{1,0:T(8,128)(2,1)}, bf16[320,704]{1,0:T(8,128)(2,1)S(1)}, u32[]{:S(2)}, u32[]{:S(2)}) collective-permute-start(bf16[320,704]{1,0:T(8,128)(2,1)} %collective-permute-done.18.refs_2_), channel_id=1, source_target_pairs={{0,16},{1,17},{2,18},{3,19},{4,20},{5,21},{6,22},{7,23},{8,24},{9,... | collective-permute-start | bytes 1351688 | tf_op jit(solution)/shard_map/ppermute | solution.py:356
  214.8 10.7 %collective-permute-start.28 = (bf16[2,2,128,320]{2,3,1,0:T(8,128)(2,1)S(1)}, bf16[2,2,128,320]{2,3,1,0:T(8,128)(2,1)S(1)}, u32[]{:S(2)}, u32[]{:S(2)}) collective-permute-start(bf16[2,2,128,320]{2,3,1,0:T(8,128)(2,1)S(1)} %bitcast.60), channel_id=1, source_target_pairs={{0,8},{1,9},{2,10},{3,11},{4,12},{5,13},{6,14},{7,15},{8,0},{9,1},... | collective-permute-start | bytes 983048 | tf_op jit(solution)/shard_map/ppermute | solution.py:356
  216.3 14.1 %collective-permute-start.32 = (bf16[64,2560]{1,0:T(8,128)(2,1)S(1)}, bf16[64,2560]{1,0:T(8,128)(2,1)S(1)}, u32[]{:S(2)}, u32[]{:S(2)}) collective-permute-start(bf16[64,2560]{1,0:T(8,128)(2,1)S(1)} %pad_maximum_fusion.10), channel_id=1, source_target_pairs={{0,8},{1,9},{2,10},{3,11},{4,12},{5,13},{6,14},{7,15},{8,0},{9,1},... | collective-permute-start | bytes 983048 | tf_op jit(solution)/shard_map/ppermute | solution.py:356
  217.0 13.3 %collective-permute-start.31 = (bf16[64,2560]{1,0:T(8,128)(2,1)S(1)}, bf16[64,2560]{1,0:T(8,128)(2,1)S(1)}, u32[]{:S(2)}, u32[]{:S(2)}) collective-permute-start(bf16[64,2560]{1,0:T(8,128)(2,1)S(1)} %slice.115), channel_id=1, source_target_pairs={{0,2},{1,3},{2,0},{3,1},{4,6},{5,7},{6,4},{7,5},{8,10},{9,11},{10,... | collective-permute-start | bytes 983048 | tf_op jit(solution)/shard_map/ppermute | solution.py:356
  218.1 25.4 %collective-permute-start.29 = (bf16[320,1024]{1,0:T(8,128)(2,1)}, bf16[320,1024]{1,0:T(8,128)(2,1)S(1)}, u32[]{:S(2)}, u32[]{:S(2)}) collective-permute-start(bf16[320,1024]{1,0:T(8,128)(2,1)} %collective-permute-done.16.refs_6_), channel_id=1, source_target_pairs={{0,4},{1,5},{2,6},{3,7},{4,0},{5,1},{6,2},{7,3},{8,12},{9,13},{10,... | collective-permute-start | bytes 1966088 | tf_op jit(solution)/shard_map/ppermute | solution.py:356
  218.5 24.9 %collective-permute-start.30 = (bf16[320,704]{1,0:T(8,128)(2,1)}, bf16[320,704]{1,0:T(8,128)(2,1)S(1)}, u32[]{:S(2)}, u32[]{:S(2)}) collective-permute-start(bf16[320,704]{1,0:T(8,128)(2,1)} %collective-permute-done.18.refs_2_), channel_id=1, source_target_pairs={{0,4},{1,5},{2,6},{3,7},{4,0},{5,1},{6,2},{7,3},{8,12},{9,13},{10,... | collective-permute-start | bytes 1351688 | tf_op jit(solution)/shard_map/ppermute | solution.py:356
  243.5 19.3 %collective-permute-start.37 = (bf16[256,2560]{1,0:T(8,128)(2,1)S(1)}, bf16[256,2560]{1,0:T(8,128)(2,1)S(1)}, u32[]{:S(2)}, u32[]{:S(2)}) collective-permute-start(bf16[256,2560]{1,0:T(8,128)(2,1)S(1)} %pad_maximum_fusion.4), channel_id=1, source_target_pairs={{0,1},{1,0},{2,3},{3,2},{4,5},{5,4},{6,7},{7,6},{8,9},{9,8},{10,11... | collective-permute-start | bytes 3932168 | tf_op jit(solution)/shard_map/ppermute | solution.py:356
  243.7 20.8 %collective-permute-start.36 = (bf16[256,2560]{1,0:T(8,128)(2,1)S(1)}, bf16[256,2560]{1,0:T(8,128)(2,1)S(1)}, u32[]{:S(2)}, u32[]{:S(2)}) collective-permute-start(bf16[256,2560]{1,0:T(8,128)(2,1)S(1)} %pad_maximum_fusion.3), channel_id=1, source_target_pairs={{0,1},{1,0},{2,3},{3,2},{4,5},{5,4},{6,7},{7,6},{8,9},{9,8},{10,11... | collective-permute-start | bytes 3932168 | tf_op jit(solution)/shard_map/ppermute | solution.py:356
  244.3 17.6 %collective-permute-start.33 = (bf16[1,4,128,320]{2,3,1,0:T(8,128)(2,1)S(1)}, bf16[1,4,128,320]{2,3,1,0:T(8,128)(2,1)S(1)}, u32[]{:S(2)}, u32[]{:S(2)}) collective-permute-start(bf16[1,4,128,320]{2,3,1,0:T(8,128)(2,1)S(1)} %get-tuple-element.325), channel_id=1, source_target_pairs={{0,16},{1,17},{2,18},{3,19},{4,20},{5,21},{6,22},{7,23},{8,24},{9,... | collective-permute-start | bytes 983048 | tf_op jit(solution)/shard_map/ppermute | solution.py:356
  245.9 20.3 %collective-permute-start.34 = (bf16[320,704]{1,0:T(8,128)(2,1)S(1)}, bf16[320,704]{1,0:T(8,128)(2,1)S(1)}, u32[]{:S(2)}, u32[]{:S(2)}) collective-permute-start(bf16[320,704]{1,0:T(8,128)(2,1)S(1)} %collective-permute-done.20.refs_4_), channel_id=1, source_target_pairs={{0,4},{1,5},{2,6},{3,7},{4,0},{5,1},{6,2},{7,3},{8,12},{9,13},{10,... | collective-permute-start | bytes 1351688 | tf_op jit(solution)/shard_map/ppermute | solution.py:356
  246.4 22.9 %collective-permute-start.35 = (bf16[320,704]{1,0:T(8,128)(2,1)S(1)}, bf16[320,704]{1,0:T(8,128)(2,1)S(1)}, u32[]{:S(2)}, u32[]{:S(2)}) collective-permute-start(bf16[320,704]{1,0:T(8,128)(2,1)S(1)} %collective-permute-done.25.refs_6_), channel_id=1, source_target_pairs={{0,4},{1,5},{2,6},{3,7},{4,0},{5,1},{6,2},{7,3},{8,12},{9,13},{10,... | collective-permute-start | bytes 1351688 | tf_op jit(solution)/shard_map/ppermute | solution.py:356
  275.0 21.2 %collective-permute-start.38 = (bf16[512,512]{1,0:T(8,128)(2,1)S(1)}, bf16[512,512]{1,0:T(8,128)(2,1)S(1)}, u32[]{:S(2)}, u32[]{:S(2)}) collective-permute-start(bf16[512,512]{1,0:T(8,128)(2,1)S(1)} %gated.6), channel_id=1, source_target_pairs={{0,8},{1,9},{2,10},{3,11},{4,12},{5,13},{6,14},{7,15},{8,0},{9,1},... | collective-permute-start | bytes 1572872 | tf_op jit(solution)/shard_map/ppermute | solution.py:356
  281.6 14.6 %collective-permute-start.39 = (bf16[512,352]{1,0:T(8,128)(2,1)S(1)}, bf16[512,352]{1,0:T(8,128)(2,1)S(1)}, u32[]{:S(2)}, u32[]{:S(2)}) collective-permute-start(bf16[512,352]{1,0:T(8,128)(2,1)S(1)} %gated.7), channel_id=1, source_target_pairs={{0,8},{1,9},{2,10},{3,11},{4,12},{5,13},{6,14},{7,15},{8,0},{9,1},... | collective-permute-start | bytes 1081352 | tf_op jit(solution)/shard_map/ppermute | solution.py:356
  305.4 3.1 collective-permute-start.40
  308.9 20.6 %copy-start.1 = (s32[32]{0:T(128)S(1)}, s32[32]{0:T(128)}, u32[]{:S(2)}) copy-start(s32[32]{0:T(128)} %param.13) | copy-start | bytes 388
  309.8 17.1 %collective-permute-start.41 = (bf16[128,2560]{1,0:T(8,128)(2,1)}, bf16[128,2560]{1,0:T(8,128)(2,1)}, u32[]{:S(2)}, u32[]{:S(2)}) collective-permute-start(bf16[128,2560]{1,0:T(8,128)(2,1)} %slice.166), channel_id=1, source_target_pairs={{0,2},{1,3},{2,0},{3,1},{4,6},{5,7},{6,4},{7,5},{8,10},{9,11},{10,... | collective-permute-start | bytes 1966088 | tf_op jit(solution)/shard_map/ppermute | solution.py:356
  (16 other events, 71.0 us)

commit v3 on v2

--- a/solution.py
+++ b/solution.py
@@ -46,6 +46,7 @@
         scratch_shapes=[pltpu.VMEM(shape, BF) for shape in shapes]
         + [pltpu.SemaphoreType.DMA((len(shapes),))],
         compiler_params=pltpu.CompilerParams(vmem_limit_bytes=vmem_mib * 2**20),
+        cost_estimate=pl.CostEstimate(flops=1, transcendentals=0, bytes_accessed=1),
         name=name,
     )(place, *ins)
 
@@ -154,21 +155,46 @@
     )(*smem, *vmem)
 
 
-def permute_columns(values, columns_at):
+def permute_columns(values, columns_at, gain=None, dtype=F32):
     rows, width = values.shape
     tile = 256
 
-    def kernel(values_ref, at_ref, out_ref):
+    def kernel(values_ref, at_ref, *refs):
+        out_ref = refs[0] if gain is None else refs[1]
+
         @pl.loop(0, width // tile)
         def _(i):
             at = pl.ds(pl.multiple_of(i * tile, tile), tile)
             source = lax.broadcasted_iota(jnp.int32, (width, tile), 0)
             onehot = (source == at_ref[:, at]).astype(F32).astype(BF)
-            out_ref[:, at] = dot(values_ref[...], onehot)
-
-    return call(
-        kernel, [], [values, columns_at[None]], [((rows, width), F32)], [], "permute_columns"
-    )[0]
+            out_ref[:, at] = dot(values_ref[...], onehot).astype(dtype)
+
+        if gain is not None:
+
+            @pl.loop(0, rows // 128)
+            def _(i):
+                at = pl.ds(pl.multiple_of(i * 128, 128), 128)
+                refs[2][at, :] = normed(out_ref[at, :], refs[0][...])
+
+    ins = [values, columns_at[None]] + ([] if gain is None else [gain[None]])
+    shapes = [((rows, width), dtype)] + ([] if gain is None else [((rows, width), BF)])
+    outs = call(kernel, [], ins, shapes, [], "permute_columns")
+    return outs[0] if gain is None else outs
+
+
+def hold(value, *others):
+    def kernel(*refs):
+        pass
+
+    return pl.pallas_call(
+        kernel,
+        in_specs=[pl.BlockSpec(memory_space=pl.ANY)] * (1 + len(others)),
+        out_specs=pl.BlockSpec(memory_space=pl.ANY),
+        out_shape=jax.ShapeDtypeStruct(value.shape, value.dtype),
+        input_output_aliases={0: 0},
+        cost_estimate=pl.CostEstimate(flops=10**11, transcendentals=0, bytes_accessed=10**8),
+        name="hold",
+    )(value, *others)
 
 
 def attend(place, lengths, joined, x_last, w_last, tables, out_in, sizes, shares):
@@ -177,7 +203,7 @@
     group = heads // kv_heads
     q_cols, k_cols = heads * head_dim, kv_heads * head_dim
     half = head_dim // 2
-    wide = tables[0].shape[1]
+    wide = (q_cols + k_cols + 127) // 128 * 128
     width = w_last[0].shape[0]
     model_dim = out_in.shape[1]
     share = seq_len // len(shares)
@@ -197,7 +223,11 @@
             head = rows[:, :wide]
             ahead = pltpu.roll(head, wide - half, 1)
             behind = pltpu.roll(head, half, 1)
-            turned = head * cos_ref[at, :] + jnp.where(first, -ahead, behind) * sin_ref[at, :]
+            cosine, sine = (
+                jnp.concatenate([ref[at, :]] * (wide // half + 1), axis=1)[:, :wide]
+                for ref in (cos_ref, sin_ref)
+            )
+            turned = head * cosine + jnp.where(first, -ahead, behind) * sine
             qk[at, :] = turned.astype(BF)
             v[at, :] = rows[:, q_cols + k_cols :].astype(BF)
             slot = t * tile + lax.broadcasted_iota(jnp.int32, (tile, 1), 0)
@@ -262,64 +292,86 @@
     )
 
 
-def gated(tokens, blocks):
-    rows, model_dim = tokens.shape
+def assemble(blocks):
     each, columns = blocks[0].shape
-    size = columns // 2
+    count = len(blocks)
+
+    def kernel(*refs):
+        for i in range(count):
+            refs[count][i * each : (i + 1) * each, :] = refs[i][...]
+
+    return call(kernel, [], blocks, [((count * each, columns), BF)], [], "assemble", 24)[0]
+
+
+def rows_product(pieces, weight, first=0, count=None, base=None, dtype=F32):
+    rows, columns = count or pieces[0].shape[0], weight.shape[1]
+    tile = 128
+
+    def kernel(*refs):
+        weight_ref = refs[len(pieces)]
+
+        @pl.loop(0, rows // tile)
+        def _(i):
+            source = pl.ds(pl.multiple_of(first + i * tile, tile), tile)
+            total = 0.0 if base is None else refs[len(pieces) + 1][source, :]
+            begin = 0
+            for ref in refs[: len(pieces)]:
+                end = begin + ref.shape[1]
+                total = total + dot(ref[source, :], weight_ref[begin:end, :])
+                begin = end
+            refs[-1][pl.ds(pl.multiple_of(i * tile, tile), tile), :] = total.astype(dtype)
+
+    ins = [*pieces, weight] + ([] if base is None else [base])
+    return call(kernel, [], ins, [((rows, columns), dtype)], [], "rows_product", 24)[0]
+
+
+def add_share(staying, arrived, extra):
+    rows, columns = staying.shape
+    half = rows // 2
+
+    def kernel(staying_ref, arrived_ref, extra_ref, keep_ref, send_ref):
+        keep_ref[...] = (
+            staying_ref[:half, :] + arrived_ref[:half, :].astype(F32) + extra_ref[...]
+        )
+        send_ref[...] = (staying_ref[half:, :] + arrived_ref[half:, :].astype(F32)).astype(BF)
+
+    return call(
+        kernel,
+        [],
+        [staying, arrived, extra],
+        [((half, columns), F32), ((half, columns), BF)],
+        [],
+        "add_share",
+        24,
+    )
+
+
+def class_rows(place, weight):
+    rows, columns = weight.shape
+    half = rows // 2
+
+    def kernel(place_ref, weight_ref, *outs):
+        for k in range(2):
+            begin = pl.multiple_of((place_ref[1] ^ k) * half, 16)
+            outs[k][...] = weight_ref[pl.ds(begin, half), :]
+
+    return call(kernel, [place], [weight], [((half, columns), BF)] * 2, [], "class_rows")
+
+
+def gated(tokens, weight):
+    rows = tokens.shape[0]
+    size = weight.shape[1] // 2
     tile = 256
 
-    def kernel(tokens_ref, *refs):
-        out_ref, weight = refs[-2:]
-        for i, ref in enumerate(refs[:-2]):
-            weight[i * each : (i + 1) * each, :] = ref[...]
-
+    def kernel(tokens_ref, weight_ref, out_ref):
         @pl.loop(0, rows // tile)
         def _(i):
             at = pl.ds(pl.multiple_of(i * tile, tile), tile)
-            projected = dot(tokens_ref[at, :], weight[...])
+            projected = dot(tokens_ref[at, :], weight_ref[...])
             gate, up = projected[:, :size], projected[:, size:]
             out_ref[at, :] = (gate / (1.0 + jnp.exp(-gate)) * up).astype(BF)
 
-    return call(
-        kernel, [], [tokens, *blocks], [((rows, size), BF)], [((model_dim, columns), BF)], "gated"
-    )[0]
-
-
-def down_product(place, kept, returned, weight):
-    rows = kept[0].shape[0]
-    units, model_dim = weight.shape[0] // 2, weight.shape[1]
-    tile = 128
-
-    def kernel(place_ref, *refs):
-        ins = refs[: 2 * len(kept)]
-        weight_ref, leaving_ref, staying_ref = refs[2 * len(kept) :]
-
-        def product(at):
-            total = 0.0
-            for k in range(2):
-                begin = (place_ref[1] ^ k) * units
-                for ref in ins[k * len(kept) : (k + 1) * len(kept)]:
-                    size = ref.shape[1]
-                    total += dot(ref[at, :], weight_ref[pl.ds(pl.multiple_of(begin, 32), size), :])
-                    begin += size
-            return total
-
-        @pl.loop(0, rows // 2 // tile)
-        def _(i):
-            out = pl.ds(pl.multiple_of(i * tile, tile), tile)
-            leaving_ref[out, :] = product(
-                pl.ds(pl.multiple_of(rows // 2 + i * tile, tile), tile)
-            ).astype(BF)
-            staying_ref[out, :] = product(out)
-
-    return call(
-        kernel,
-        [place],
-        [*kept, *returned, weight],
-        [((rows // 2, model_dim), BF), ((rows // 2, model_dim), F32)],
-        [],
-        "down_product",
-    )
+    return call(kernel, [], [tokens, weight], [((rows, size), BF)], [], "gated", 24)[0]
 
 
 def body(
@@ -366,6 +418,7 @@
     chunks = list(CHUNKS) + [units - sum(CHUNKS)]
     bits = [1 << k for k in range(16) if 1 << k < n_tp]
     evens = list(range(2, n_req, 2))
+    zbits = [1 << k for k in range(1, 16) if 1 << k < n_req]
     singles = [r for r in evens if r & (r - 1) == 0]
     doubles = [r for r in evens if r & (r - 1)]
     plain = [r for r in evens if not r & PAIR]
@@ -387,28 +440,32 @@
 
     place = jnp.stack([tp, (req // PAIR) % 2])
     qkv_split = split_qkv(place, trainer_qkv, n_tp)
+    half = head_dim // 2
+    freq = theta_base ** (-jnp.arange(half, dtype=F32) * 2.0 / head_dim)
+    angles = jnp.arange(seq_len, dtype=F32)[:, None] * freq[None, :]
+    tables = (jnp.cos(angles), jnp.sin(angles))
     trainer_gateup, qkv_split = sync((trainer_gateup, qkv_split))
     gu_own, gu_odd = split_gateup(place, trainer_gateup, n_tp, halves, chunks)
-    gu_near = swap(gu_odd, 0, 1)
     qkv_split = [qkv_split[0]] + [swap(qkv_split[s], 0, s) for s in range(1, n_tp)]
     st = sync(
         dict(
             qkv_split=qkv_split,
             gu_own=gu_own,
-            gu_near=gu_near,
+            gu_odd=gu_odd,
             tokens=tokens,
             layout=trainer_layout,
-            slots=jnp.arange(seq_len, dtype=jnp.int32),
+            tables=tables,
         )
     )
 
-    tokens, trainer_layout, slots = st["tokens"], st["layout"], st["slots"]
-    gu_own, gu_near = st["gu_own"], st["gu_near"]
+    tokens, trainer_layout, tables = st["tokens"], st["layout"], st["tables"]
+    gu_own, gu_near = st["gu_own"], swap(st["gu_odd"], 0, 1)
     qkv_own = join_qkv(place, st["qkv_split"])
     qkv = {0: qkv_own}
     spread_z(qkv, singles)
     qkv[1] = swap(qkv_own, 1, 0)
     far = list(pack_far(place, gu_own, gu_near, chunks))
+    tokens, far = sync((tokens, far))
     for c in range(len(chunks)):
         moved = [swap(far[c][f], 0, 2 * f + 2) for f in range(n_tp // 2 - 1)]
         far[c] = jnp.stack(moved) if len(moved) > 1 else moved[0][None]
@@ -425,8 +482,8 @@
         * rows_each
         + jnp.arange(rows_each, dtype=jnp.int32)[None, :]
     ).reshape(-1)
-    tokens_in = permute_columns(tokens, columns_at)
-    x_norm = normed(tokens_in, attn_gain.reshape(devices, rows_each)[blocks_at].reshape(-1))
+    gain_in = attn_gain.reshape(devices, rows_each)[blocks_at].reshape(-1)
+    tokens_in, x_norm = permute_columns(tokens, columns_at, gain_in)
     st = sync(
         dict(
             qkv=qkv,
@@ -437,6 +494,7 @@
             tokens_in=tokens_in,
             onehot_at=columns_at,
             out_proj=out_proj,
+            down_proj=down_proj,
             page_slot=page_slot,
             ffn_gain=ffn_gain,
         )
@@ -454,20 +512,20 @@
         qkv[r ^ 1] = swap(qkv[r], 1, 0)
     gu = [dict() for _ in chunks]
     spread_class(gu[0], *blocks[0], plain)
-    out_in = permute_columns(st["out_proj"], columns_at).astype(BF)
-    half = head_dim // 2
-    wide = (q_cols + k_cols + 127) // 128 * 128
-    lane = jnp.arange(wide, dtype=jnp.int32) % half
-    freq = theta_base ** (-lane.astype(F32) * 2.0 / head_dim)
-    angles = slots.astype(F32)[:, None] * freq[None, :]
-    tables = (jnp.cos(angles), jnp.sin(angles))
+    out_in = permute_columns(st["out_proj"], columns_at, dtype=BF)
+    down_rel = class_rows(place, st["down_proj"])
     ffn_gain_in = st["ffn_gain"].reshape(devices, rows_each)[blocks_at].reshape(-1)
     n_pages = seq_len // PAGE
     holders = lax.dynamic_slice_in_dim(page_slot, req * n_pages, n_pages, 0) // n_pages
-    relative = jnp.arange(n_req, dtype=jnp.int32) ^ req
+    page_bits = [bit for bit in zbits if bit != PAIR] + [1, PAIR]
+    at_slot = [
+        sum(bit for k, bit in enumerate(page_bits) if (i >> k) & 1) for i in range(n_req)
+    ]
+    relative = jnp.asarray(at_slot, jnp.int32) ^ req
     chosen = jnp.argmax(holders[None, :] == relative[:, None], axis=1)
     targets = req * n_pages + jnp.arange(n_pages, dtype=jnp.int32)
     source = jnp.argmax(page_slot[None, :] == targets[:, None], axis=1) // n_pages
+    source = jnp.argmax(relative[None, :] == source[:, None], axis=1)
     st = sync(
         dict(
             qkv=qkv,
@@ -475,17 +533,21 @@
             blocks=blocks,
             x_norm=x_norm,
             out_in=out_in,
+            down_rel=down_rel,
             ffn_gain_in=ffn_gain_in,
-            tables=tables,
             pages=(chosen, source),
         )
     )
 
     qkv, gu, blocks, x_norm, out_in = (st[k] for k in ("qkv", "gu", "blocks", "x_norm", "out_in"))
     chosen, source = st["pages"]
+    down_rel, ffn_gain_in = st["down_rel"], st["ffn_gain_in"]
     spread_class(gu[0], *blocks[0], [PAIR])
+    spread_class(gu[1], *blocks[1], plain)
     for r in doubles:
         qkv[r ^ 1] = swap(qkv[r], 1, 0)
+    gu[1][0] = blocks[1][0]
+    gu[1][1] = swap(blocks[1][0], 1, 0)
     width = model_dim // n_req
     first = [0, 1] + [r | j for r in singles for j in (0, 1)]
     last = [r | j for r in doubles for j in (0, 1)]
@@ -497,16 +559,15 @@
         )
 
     joined = part(first)
-    st = sync(
-        dict(qkv=qkv, gu=gu, blocks=blocks, joined=joined, x_norm=x_norm, tables=st["tables"])
-    )
+    st = sync(dict(qkv=qkv, gu=gu, blocks=blocks, joined=joined, x_norm=x_norm))
 
     qkv, gu, blocks, x_norm = (st[k] for k in ("qkv", "gu", "blocks", "x_norm"))
     spread_class(gu[0], *blocks[0], crossed)
     spread_class(gu[1], *blocks[1], [PAIR])
-    for c in range(len(chunks)):
-        gu[c][0] = blocks[c][0]
-        gu[c][1] = swap(blocks[c][0], 1, 0)
+    gu[0][0] = blocks[0][0]
+    gu[0][1] = swap(blocks[0][0], 1, 0)
+    for r in plain:
+        gu[0][r ^ 1] = swap(gu[0][r], 1, 0)
     shares = sorted(range(n_tp), key=lambda s: [(s >> k) & 1 for k in range(len(bits))])
     leaving, staying, cache_rows = attend(
         place,
@@ -514,7 +575,7 @@
         st["joined"],
         jnp.concatenate([x_norm[:, r * width : (r + 1) * width] for r in last], axis=1),
         [qkv[r] for r in last],
-        st["tables"],
+        tables,
         out_in,
         (local_heads, local_kv, head_dim),
         shares,
@@ -523,22 +584,15 @@
         dict(gu=gu, blocks=blocks, leaving=leaving, staying=staying, pages=cache_rows, out=out_in)
     )
 
-    def sum_rest(partial):
-        for bit in bits[1:]:
-            rows = partial.shape[0] // 2
-            arrived = swap(partial[rows:].astype(BF), 0, bit)
-            partial = partial[:rows] + arrived.astype(F32)
-        return partial
-
     gu, blocks = st["gu"], st["blocks"]
-    mixed = sum_rest(st["staying"] + swap(st["leaving"], 0, bits[0]).astype(F32))
-    spread_class(gu[1], *blocks[1], plain)
+    tokens_share = lax.dynamic_slice_in_dim(tokens_in, tp * share, share, 0)
+    keep, send = add_share(st["staying"], swap(st["leaving"], 0, bits[0]), tokens_share)
+    resid_in = keep + swap(send, 0, bits[1]).astype(F32)
+    spread_class(gu[1], None, None, crossed)
+    gu[0][PAIR ^ 1] = swap(gu[0][PAIR], 1, 0)
     for r in plain:
-        gu[0][r ^ 1] = swap(gu[0][r], 1, 0)
-    resid_in = lax.dynamic_slice_in_dim(tokens_in, tp * share, share, 0) + mixed
+        gu[1][r ^ 1] = swap(gu[1][r], 1, 0)
     h_share = normed(resid_in, ffn_gain_in)
-    box = st["pages"].reshape(n_pages, PAGE, 2 * k_cols)[chosen][:, None]
-    st = sync(dict(gu=gu, h_share=h_share, resid_in=resid_in, box=box))
 
     def reordered(values):
         return jnp.concatenate(
@@ -549,64 +603,81 @@
         box = box.reshape((-1, 2) + box.shape[1:])
         return jnp.concatenate([box[:, 0], swap(box[:, 1], bit, 0)], axis=1)
 
-    gu, h_share, resid_in = st["gu"], st["h_share"], st["resid_in"]
+    late = crossed[0]
+    gu[1][late] = hold(gu[1][late], gu[0][PAIR ^ 1], *[gu[1][r ^ 1] for r in plain])
+    st = sync(dict(gu=gu, h=(h_share, reordered(h_share)), resid_in=resid_in, pages=st["pages"]))
+
+    gu, resid_in = st["gu"], st["resid_in"]
+    h_share, h_leaving = st["h"]
     cross = n_tp // 2
     h_across = swap(h_share, 0, cross)
-    h_pair = swap(reordered(h_share), PAIR, 0)
-    spread_class(gu[1], None, None, crossed)
-    gu[0][PAIR ^ 1] = swap(gu[0][PAIR], 1, 0)
-    box = page_step(st["box"], 1)
+    h_pair = swap(h_leaving, PAIR, 0)
+    for r in crossed:
+        gu[0][r ^ 1] = swap(gu[0][r], 1, 0)
     coarse = resid_in.astype(BF)
     fine = (resid_in - coarse.astype(F32)).astype(BF)
     terms = permute_columns(jnp.concatenate([coarse, fine], axis=0), columns_back)
-    resid = terms[:share] + terms[share:]
-    st = sync(dict(gu=gu, h=(h_share, h_across, h_pair), resid=resid, box=box))
-
-    gu, resid, box = st["gu"], st["resid"], st["box"]
-    h_share, h_across, h_pair = st["h"]
     cut = share // 2
-    h_diag = jnp.concatenate(
-        [swap(h_pair[:cut], 0, cross), swap(reordered(h_across[cut:]), PAIR, 0)], axis=0
-    )
-    for r in crossed:
-        gu[0][r ^ 1] = swap(gu[0][r], 1, 0)
+    st = sync(
+        dict(
+            gu=gu,
+            own=(h_share, h_across),
+            theirs=h_pair,
+            halves=(h_pair[:cut], reordered(h_across[cut:])),
+            terms=terms,
+            box=st["pages"].reshape(n_pages, PAGE, 2 * k_cols)[chosen][:, None],
+        )
+    )
+
+    gu, box = st["gu"], st["box"]
+    over_y, over_pair = st["halves"]
+    h_diag = [swap(over_y, 0, cross), swap(over_pair, PAIR, 0)]
     gu[1][PAIR ^ 1] = swap(gu[1][PAIR], 1, 0)
-    if n_req > 4:
-        box = page_step(box, 2)
-    st = sync(dict(gu=gu, own=(h_share, h_across), theirs=(h_pair, h_diag), resid=resid, box=box))
-
-    gu, resid, box = st["gu"], st["resid"], st["box"]
-
-    def whole(parts):
-        rows = jnp.concatenate(parts, axis=0)
-        for bit in range(1, cross):
-            assert bit == 1
+    for bit in page_bits[:-2]:
+        box = page_step(box, bit)
+    resid = st["terms"][:share] + st["terms"][share:]
+    own = jnp.concatenate(st["own"], axis=0)
+    theirs = jnp.concatenate([st["theirs"]] + h_diag, axis=0)
+    st = sync(dict(gu=gu, h=(own, theirs), resid=resid, box=box))
+
+    def whole(rows):
+        for bit in bits[:-1]:
             rows = jnp.concatenate([rows, swap(rows, 0, bit)], axis=0)
         return rows
 
-    h_own = whole(st["own"])
-    h_theirs = whole(st["theirs"])
-    for r in plain + crossed:
+    gu, box = st["gu"], st["box"]
+    h_own, h_theirs = (whole(rows) for rows in st["h"])
+    for r in crossed:
         gu[1][r ^ 1] = swap(gu[1][r], 1, 0)
-    bit = 4
-    while bit < n_req:
-        box = page_step(box, bit)
-        bit *= 2
+    weight = assemble([gu[0][r] for r in range(n_req)])
+    theirs = gated(h_theirs, weight)
+    kept = [gated(h_own, weight)]
     st = sync(
-        dict(gu=gu, own=h_own, theirs=h_theirs, resid=resid, box=box)
-    )
-
-    h_own, h_theirs, resid, box = (st[k] for k in ("own", "theirs", "resid", "box"))
-    weights = [[held[r] for r in range(n_req)] for held in st["gu"]]
-    returned = [swap(gated(h_theirs, weight), PAIR, 0) for weight in weights]
-    kept = [gated(h_own, weight) for weight in weights]
-    leaving, staying = down_product(place, kept, returned, down_proj)
+        dict(gu=gu[1], h=(h_own, h_theirs), hidden=(kept, theirs), resid=st["resid"], box=box)
+    )
+
+    resid, box = st["resid"], st["box"]
+    h_own, h_theirs = st["h"]
+    kept, theirs = st["hidden"]
+    returned = [swap(theirs, PAIR, 0)]
+    weight = assemble([st["gu"][r] for r in range(n_req)])
+    theirs = gated(h_theirs, weight)
+    box = page_step(box, page_bits[-2])
+    h_own, theirs = sync((h_own, theirs))
+    returned.append(swap(theirs, PAIR, 0))
+    kept.append(gated(h_own, weight))
+    product = rows_product(kept, down_rel[0])
+    returned, box, product = sync((returned, box, product))
+    rows = seq_len // 2
+    leaving = rows_product(returned, down_rel[1], rows, rows, product, BF)
     arrived = swap(leaving, 0, bits[0])
-    added = sum_rest(staying + arrived.astype(F32))
+    staying = rows_product(returned, down_rel[1], 0, rows, product)
+    keep, send = add_share(staying, arrived, resid)
+    box = page_step(box, page_bits[-1])
     share_slots = tp * share + jnp.arange(share, dtype=jnp.int32)
     live_share = (share_slots < lengths[0]).astype(F32)
-    layer_out = ((resid + added) * live_share[:, None]).astype(BF)
-    kv_cache = box[0][source ^ req]
+    layer_out = ((keep + swap(send, 0, bits[1]).astype(F32)) * live_share[:, None]).astype(BF)
+    kv_cache = box[0][source]
     return (layer_out, kv_cache)
 
 

time: 330 us -> 276 us (0.84)
  waiting for transfers between devices: 131 us -> 88.4 us
  other arithmetic: 37.7 us -> 12.2 us
  local copies, waits for them, and re-layouts: 21.9 us -> 31.6 us
    ppermute x42, waiting for transfers between devices: 131 us -> 88.4 us  [swap(): return lax.ppermute(value, ('req', 'tp'), pairs)]
    unnamed x51 -> x89, local copies, waits for them, and re-layouts: 8.69 us -> 15.5 us
    sin x1, other arithmetic: 7.77 us -> 0.98 us  [body(): tables = (jnp.cos(angles), jnp.sin(angles))]
    convert_element_type x3 -> x1, other arithmetic: 7.54 us -> 1.02 us  [body(): ((keep + swap(send, 0, bits[1]).astype(F32)) * live_share[:, None]).astyp...]
    reduce_sum x2 -> x1, other arithmetic: 5.14 us -> 1.38 us  [normed(): jnp.mean(values * values, axis=-1, keepdims=True) + eps_norm]
    convert_element_type x2 -> x1, other arithmetic: 4.65 us -> 1.03 us  [normed(): return (values * scale * gain).astype(BF)]
    add x3 -> x1, other arithmetic: 3.63 us -> 0.14 us  [body(): resid = st['terms'][:share] + st['terms'][share:]]
    pallas_call x9 -> x16, Pallas kernels: 74.5 us -> 76.3 us  [call(): pl.pallas_call(kernel, in_specs=[SMEM] * len(smem) + [VMEM] * len(vmem),...]
  transfers between devices with their start and end apart: 42 -> 42, of which waited for: 20 -> 19; matrix products, arithmetic and copies ran while one was open for 15% -> 11% of each run, Pallas kernels for 21% -> 32%
where the time goes in v3:
time: 276 us; the launch traced here: 275 us
  Pallas kernels  93.7 us (34%)
  waiting for transfers between devices  88.4 us (32%)
  starting transfers between devices  43.4 us (16%)
  local copies, waits for them, and re-layouts  31.6 us (11%)
  other arithmetic  12.2 us (4%)
  matrix products  3.51 us (1%)
    ppermute x42, waiting for transfers between devices, swap(): return lax.ppermute(value, ('req', 'tp'), pairs)  88.4 us
    pallas_call x16, Pallas kernels, call(): pl.pallas_call(kernel, in_specs=[SMEM] * len(smem) + [VMEM] * len(vmem),...  76.3 us
    ppermute x42, starting transfers between devices, swap(): return lax.ppermute(value, ('req', 'tp'), pairs)  43.4 us
    pallas_call x6, Pallas kernels, on_device(): pl.pallas_call(run, in_specs=[pl.BlockSpec(memory_space=pltpu.SMEM)] + [p...  17.5 us
    unnamed x89, local copies, waits for them, and re-layouts  15.5 us
  transfers between devices with their start and end apart: 42, of which 19 were waited for; matrix products, arithmetic and copies ran while one was open for 11% of the time, Pallas kernels for 32%

profile of v3, /device:TPU:0, one launch (start us, length us, event | category | flops | bytes accessed | tf_op | source)
XLA Modules:
  0.0 275.0 jit_solution(5700534693801859132)
XLA Ops:
  1.3 2.5 split_qkv.1
  4.3 2.6 collective-permute-start.1
  7.0 4.3 %split_gateup.1 = (bf16[2,2,80,1728]{3,2,1,0:T(8,128)(2,1)}, bf16[2,2,80,1728]{3,2,1,0:T(8,128)(2,1)}) custom-call(s32[2]{0:T(128)} %pad_add_fusion.place_ref, f32[80,13824]{1,0:T(8,128)} %refs_0_.2), custom_call_target="tpu_custom_call" | custom-call | flops 1 | bytes 1 | tf_op jit(solution)/shard_map/split_gateup/pallas_call | solution.py:40
  12.3 2.9 %collective-permute-done.2.refs_3_ = bf16[80,960]{1,0:T(8,128)(2,1)} collective-permute-done((bf16[80,960]{1,0:T(8,128)(2,1)}, bf16[80,960]{1,0:T(8,128)(2,1)}, u32[]{:S(2)}, u32[]{:S(2)}) %collective-permute-start.2) | collective-permute-done | bytes 153632 | tf_op jit(solution)/shard_map/ppermute | solution.py:408
  15.6 2.2 join_qkv.1
  17.8 2.9 %collective-permute-start.8 = (bf16[320,960]{1,0:T(8,128)(2,1)}, bf16[320,960]{1,0:T(8,128)(2,1)}, u32[]{:S(2)}, u32[]{:S(2)}) collective-permute-start(bf16[320,960]{1,0:T(8,128)(2,1)} %bitcast.54), channel_id=1, source_target_pairs={{0,16},{1,17},{2,18},{3,19},{4,20},{5,21},{6,22},{7,23},{8,24},{9,... | collective-permute-start | bytes 1843208 | tf_op jit(solution)/shard_map/ppermute | solution.py:408
  20.7 1.6 collective-permute-start.7
  24.5 2.7 pack_far.1
  27.2 1.6 collective-permute-start.4
  30.3 11.8 %permute_columns.3 = (f32[512,2560]{1,0:T(8,128)}, bf16[512,2560]{1,0:T(8,128)(2,1)S(1)}) custom-call(bf16[512,2560]{1,0:T(8,128)(2,1)S(1)} %copy-done.4, s32[1,2560]{1,0:T(1,128)S(1)} %add.164.at_ref, f32[1,2560]{1,0:T(1,128)S(1)} %broadcast_in_dim_reshape.2.refs_0_), custom_call_target="tpu_custom_call" | custom-call | flops 1 | bytes 1 | tf_op jit(solution)/shard_map/permute_columns/pallas_call | solution.py:146
  43.5 6.8 %collective-permute-done.8 = bf16[320,960]{1,0:T(8,128)(2,1)} collective-permute-done((bf16[320,960]{1,0:T(8,128)(2,1)}, bf16[320,960]{1,0:T(8,128)(2,1)}, u32[]{:S(2)}, u32[]{:S(2)}) %collective-permute-start.8) | collective-permute-done | bytes 614432 | tf_op jit(solution)/shard_map/ppermute | solution.py:408
  50.5 3.7 %collective-permute-done.5 = bf16[2,2,80,704]{3,2,1,0:T(8,128)(2,1)} collective-permute-done((bf16[2,2,80,704]{3,2,1,0:T(8,128)(2,1)}, bf16[2,2,80,704]{3,2,1,0:T(8,128)(2,1)}, u32[]{:S(2)}, u32[]{:S(2)}) %collective-permute-start.5) | collective-permute-done | bytes 450592 | tf_op jit(solution)/shard_map/ppermute | solution.py:408
  55.2 2.9 %join_gateup.2 = (bf16[4,80,1024]{2,1,0:T(8,128)(2,1)}, bf16[4,80,1024]{2,1,0:T(8,128)(2,1)}) custom-call(s32[2]{0:T(128)} %pad_add_fusion.place_ref, bf16[2,2,80,1728]{3,2,1,0:T(8,128)(2,1)} %get-tuple-element.208.refs_0_, bf16[2,2,80,1728]{3,2,1,0:T(8,128)(2,1)} %collective-permute-done.3.refs_1_, bf16[1,2,2,80,1024]{4,3,2,1,0:T(8,128)(2,1)} %bitcast.3.refs_2_), custom_call_target="tpu_custom_call" | custom-call | flops 1 | bytes 1 | tf_op jit(solution)/shard_map/join_gateup/pallas_call | solution.py:40
  60.8 2.8 %join_gateup.3 = (bf16[4,80,704]{2,1,0:T(8,128)(2,1)}, bf16[4,80,704]{2,1,0:T(8,128)(2,1)}) custom-call(s32[2]{0:T(128)} %pad_add_fusion.place_ref, bf16[2,2,80,1728]{3,2,1,0:T(8,128)(2,1)} %get-tuple-element.208.refs_0_, bf16[2,2,80,1728]{3,2,1,0:T(8,128)(2,1)} %collective-permute-done.3.refs_1_, bf16[1,2,2,80,704]{4,3,2,1,0:T(8,128)(2,1)} %bitcast.5.refs_2_), custom_call_target="tpu_custom_call" | custom-call | flops 1 | bytes 1 | tf_op jit(solution)/shard_map/join_gateup/pallas_call | solution.py:40
  63.6 6.2 %class_rows.1 = (bf16[864,2560]{1,0:T(8,128)(2,1)S(1)}, bf16[864,2560]{1,0:T(8,128)(2,1)}) custom-call(s32[2]{0:T(128)S(1)} %copy-done.23, bf16[1728,2560]{1,0:T(8,128)(2,1)} %weight_ref), custom_call_target="tpu_custom_call" | custom-call | flops 1 | bytes 1 | tf_op jit(solution)/shard_map/class_rows/pallas_call | solution.py:146
  69.8 2.1 copy-done.3
  72.0 12.2 %permute_columns.4.out_in_ref = bf16[640,2560]{1,0:T(8,128)(2,1)S(1)} custom-call(bf16[640,2560]{1,0:T(8,128)(2,1)} %values_ref.1, s32[1,2560]{1,0:T(1,128)S(1)} %broadcast_in_dim.14.at_ref), custom_call_target="tpu_custom_call" | custom-call | flops 1 | bytes 1 | tf_op jit(solution)/shard_map/permute_columns/pallas_call | solution.py:146
  84.2 1.7 copy-done.2
  88.0 2.6 collective-permute-start.15
  91.2 1.6 collective-permute-start.13
  99.2 3.5 %fusion = f32[512,960]{0,1:T(8,128)} fusion(bf16[1920,960]{1,0:T(8,128)(2,1)S(1)} %constant_dynamic-update-slice_fusion, bf16[512,2560]{1,0:T(8,128)(2,1)S(1)} %copy-done.22), kind=kOutput, calls=%fused_computation.5 | convolution fusion | flops 1887436800 | bytes 7864320 | tf_op jit(solution)/shard_map/dot_general | solution.py:26
  102.7 8.4 %collective-permute-done.15.refs_4_ = bf16[320,704]{1,0:T(8,128)(2,1)S(1)} collective-permute-done((bf16[320,704]{1,0:T(8,128)(2,1)S(1)}, bf16[320,704]{1,0:T(8,128)(2,1)S(1)}, u32[]{:S(2)}, u32[]{:S(2)}) %collective-permute-start.15) | collective-permute-done | bytes 450592 | tf_op jit(solution)/shard_map/ppermute | solution.py:408
  111.9 3.2 %collective-permute-done.16.refs_1_ = bf16[320,960]{1,0:T(8,128)(2,1)S(1)} collective-permute-done((bf16[320,960]{1,0:T(8,128)(2,1)S(1)}, bf16[320,960]{1,0:T(8,128)(2,1)S(1)}, u32[]{:S(2)}, u32[]{:S(2)}) %collective-permute-start.16) | collective-permute-done | bytes 614432 | tf_op jit(solution)/shard_map/ppermute | solution.py:408
  118.3 1.8 collective-permute-start.20
  120.8 2.9 %copy.35.joined_ref = f32[512,960]{1,0:T(8,128)} copy(f32[512,960]{0,1:T(8,128)} %fusion) | data formatting | bytes 3932160 | tf_op jit(solution)/shard_map/optimization_barrier | solution.py:414
  123.7 16.3 %attend.1 = (bf16[256,2560]{1,0:T(8,128)(2,1)}, f32[256,2560]{1,0:T(8,128)}, bf16[512,320]{1,0:T(8,128)(2,1)S(1)}) custom-call(s32[2]{0:T(128)S(1)} %copy-done.23, s32[1]{0:T(128)} %copy.58.length_ref, f32[512,960]{1,0:T(8,128)} %copy.35.joined_ref, bf16[512,640]{1,0:T(8,128)(2,1)S(1)} %concatenate.41.x_ref, f32[512,40]{1,0:T(8,128)S(1)} %get-tuple-element.253.cos_ref, ...), custom_call_target="tpu_custom_call" | custom-call | flops 1 | bytes 1 | tf_op jit(solution)/shard_map/attend/pallas_call | solution.py:146
  140.8 3.5 %collective-permute-done.19.refs_6_ = bf16[320,1024]{1,0:T(8,128)(2,1)} collective-permute-done((bf16[320,1024]{1,0:T(8,128)(2,1)}, bf16[320,1024]{1,0:T(8,128)(2,1)}, u32[]{:S(2)}, u32[]{:S(2)}) %collective-permute-start.19) | collective-permute-done | bytes 655392 | tf_op jit(solution)/shard_map/ppermute | solution.py:408
  149.0 2.5 add_share.2
  154.1 17.1 %collective-permute-done.23.refs_0_ = bf16[320,704]{1,0:T(8,128)(2,1)S(1)} collective-permute-done((bf16[320,704]{1,0:T(8,128)(2,1)}, bf16[320,704]{1,0:T(8,128)(2,1)S(1)}, u32[]{:S(2)}, u32[]{:S(2)}) %collective-permute-start.23) | collective-permute-done | bytes 450592 | tf_op jit(solution)/shard_map/ppermute | solution.py:408
  182.1 5.1 %permute_columns.5 = f32[256,2560]{1,0:T(8,128)S(1)} custom-call(bf16[256,2560]{1,0:T(8,128)(2,1)S(1)} %pad_maximum_fusion.values_ref, s32[1,2560]{1,0:T(1,128)S(1)} %add.177.at_ref), custom_call_target="tpu_custom_call" | custom-call | flops 1 | bytes 1 | tf_op jit(solution)/shard_map/permute_columns/pallas_call | solution.py:146
  187.2 1.9 copy.36
  189.1 2.4 gather_fusion.3
  191.5 4.1 %collective-permute-done.27 = bf16[128,2560]{1,0:T(8,128)(2,1)} collective-permute-done((bf16[128,2560]{1,0:T(8,128)(2,1)}, bf16[128,2560]{1,0:T(8,128)(2,1)}, u32[]{:S(2)}, u32[]{:S(2)}) %collective-permute-start.27) | collective-permute-done | bytes 655392 | tf_op jit(solution)/shard_map/ppermute | solution.py:408
  197.8 2.7 collective-permute-start.29
  205.2 8.9 %collective-permute-done.29 = bf16[4,1,128,320]{2,3,0,1:T(8,128)(2,1)S(1)} collective-permute-done((bf16[4,1,128,320]{2,3,0,1:T(8,128)(2,1)S(1)}, bf16[4,1,128,320]{2,3,0,1:T(8,128)(2,1)S(1)}, u32[]{:S(2)}, u32[]{:S(2)}) %collective-permute-start.29) | collective-permute-done | bytes 327712 | tf_op jit(solution)/shard_map/ppermute | solution.py:408
  218.3 2.4 assemble.2.weight_ref
  221.8 3.0 %gated.5 = bf16[512,512]{1,0:T(8,128)(2,1)S(1)} custom-call(bf16[512,2560]{1,0:T(8,128)(2,1)S(1)} %constant_dynamic-update-slice_fusion.8.tokens_ref, bf16[2560,1024]{1,0:T(8,128)(2,1)S(1)} %assemble.2.weight_ref), custom_call_target="tpu_custom_call" | custom-call | flops 1 | bytes 1 | tf_op jit(solution)/shard_map/gated/pallas_call | solution.py:146
  224.9 3.0 %gated.4.refs_0_ = bf16[512,512]{1,0:T(8,128)(2,1)S(1)} custom-call(bf16[512,2560]{1,0:T(8,128)(2,1)S(1)} %constant_dynamic-update-slice_fusion.6.tokens_ref, bf16[2560,1024]{1,0:T(8,128)(2,1)S(1)} %assemble.2.weight_ref), custom_call_target="tpu_custom_call" | custom-call | flops 1 | bytes 1 | tf_op jit(solution)/shard_map/gated/pallas_call | solution.py:146
  228.0 2.6 collective-permute-done.33.refs_7_
  233.0 2.6 gated.6
  235.6 2.1 collective-permute-start.37
  237.7 2.6 gated.7.refs_1_
  240.4 3.4 %rows_product.3.refs_3_ = f32[512,2560]{1,0:T(8,128)S(1)} custom-call(bf16[512,512]{1,0:T(8,128)(2,1)S(1)} %gated.4.refs_0_, bf16[512,352]{1,0:T(8,128)(2,1)S(1)} %gated.7.refs_1_, bf16[864,2560]{1,0:T(8,128)(2,1)S(1)} %bitcast.48), custom_call_target="tpu_custom_call" | custom-call | flops 1 | bytes 1 | tf_op jit(solution)/shard_map/rows_product/pallas_call | solution.py:146
  243.9 8.1 %collective-permute-done.37.refs_1_ = bf16[512,352]{1,0:T(8,128)(2,1)S(1)} collective-permute-done((bf16[512,352]{1,0:T(8,128)(2,1)S(1)}, bf16[512,352]{1,0:T(8,128)(2,1)S(1)}, u32[]{:S(2)}, u32[]{:S(2)}) %collective-permute-start.37) | collective-permute-done | bytes 360480 | tf_op jit(solution)/shard_map/ppermute | solution.py:408
  252.0 1.7 rows_product.5
  253.9 1.7 rows_product.4.staying_ref
  258.5 8.8 %collective-permute-done.41 = bf16[1,4,128,320]{2,3,1,0:T(8,128)(2,1)S(1)} collective-permute-done((bf16[1,4,128,320]{2,3,1,0:T(8,128)(2,1)S(1)}, bf16[1,4,128,320]{2,3,1,0:T(8,128)(2,1)S(1)}, u32[]{:S(2)}, u32[]{:S(2)}) %collective-permute-start.41) | collective-permute-done | bytes 327712 | tf_op jit(solution)/shard_map/ppermute | solution.py:408
  268.7 5.3 %collective-permute-done.40 = bf16[128,2560]{1,0:T(8,128)(2,1)S(1)} collective-permute-done((bf16[128,2560]{1,0:T(8,128)(2,1)S(1)}, bf16[128,2560]{1,0:T(8,128)(2,1)S(1)}, u32[]{:S(2)}, u32[]{:S(2)}) %collective-permute-start.40) | collective-permute-done | bytes 655392 | tf_op jit(solution)/shard_map/ppermute | solution.py:408
  (217 shorter events, 63.3 us)
Async XLA Ops:
  0.6 23.2 %copy-start = (s32[32]{0:T(128)S(1)}, s32[32]{0:T(128)}, u32[]{:S(2)}) copy-start(s32[32]{0:T(128)} %param.14) | copy-start | bytes 388
  3.8 8.5 %collective-permute-start = (bf16[80,960]{1,0:T(8,128)(2,1)}, bf16[80,960]{1,0:T(8,128)(2,1)S(1)}, u32[]{:S(2)}, u32[]{:S(2)}) collective-permute-start(bf16[80,960]{1,0:T(8,128)(2,1)} %get-tuple-element.190), channel_id=1, source_target_pairs={{0,1},{1,0},{2,3},{3,2},{4,5},{5,4},{6,7},{7,6},{8,9},{9,8},{10,11... | collective-permute-start | bytes 460808 | tf_op jit(solution)/shard_map/ppermute | solution.py:408
  4.3 8.0 %collective-permute-start.1 = (bf16[80,960]{1,0:T(8,128)(2,1)}, bf16[80,960]{1,0:T(8,128)(2,1)S(1)}, u32[]{:S(2)}, u32[]{:S(2)}) collective-permute-start(bf16[80,960]{1,0:T(8,128)(2,1)} %get-tuple-element.191), channel_id=1, source_target_pairs={{0,2},{1,3},{2,0},{3,1},{4,6},{5,7},{6,4},{7,5},{8,10},{9,11},{10,... | collective-permute-start | bytes 460808 | tf_op jit(solution)/shard_map/ppermute | solution.py:408
  6.9 8.4 %collective-permute-start.2 = (bf16[80,960]{1,0:T(8,128)(2,1)}, bf16[80,960]{1,0:T(8,128)(2,1)}, u32[]{:S(2)}, u32[]{:S(2)}) collective-permute-start(bf16[80,960]{1,0:T(8,128)(2,1)} %get-tuple-element.192), channel_id=1, source_target_pairs={{0,3},{1,2},{2,1},{3,0},{4,7},{5,6},{6,5},{7,4},{8,11},{9,10},{10,... | collective-permute-start | bytes 460808 | tf_op jit(solution)/shard_map/ppermute | solution.py:408
  15.2 9.3 %collective-permute-start.3 = (bf16[2,2,80,1728]{3,2,1,0:T(8,128)(2,1)}, bf16[2,2,80,1728]{3,2,1,0:T(8,128)(2,1)}, u32[]{:S(2)}, u32[]{:S(2)}) collective-permute-start(bf16[2,2,80,1728]{3,2,1,0:T(8,128)(2,1)} %get-tuple-element.195), channel_id=1, source_target_pairs={{0,1},{1,0},{2,3},{3,2},{4,5},{5,4},{6,7},{7,6},{8,9},{9,8},{10,11... | collective-permute-start | bytes 3317768 | tf_op jit(solution)/shard_map/ppermute | solution.py:408
  15.6 14.6 %copy-start.4 = (bf16[512,2560]{1,0:T(8,128)(2,1)S(1)}, bf16[512,2560]{1,0:T(8,128)(2,1)}, u32[]{:S(2)}) copy-start(bf16[512,2560]{1,0:T(8,128)(2,1)} %values_ref) | copy-start | bytes 7864324
  17.8 32.5 %collective-permute-start.8 = (bf16[320,960]{1,0:T(8,128)(2,1)}, bf16[320,960]{1,0:T(8,128)(2,1)}, u32[]{:S(2)}, u32[]{:S(2)}) collective-permute-start(bf16[320,960]{1,0:T(8,128)(2,1)} %bitcast.54), channel_id=1, source_target_pairs={{0,16},{1,17},{2,18},{3,19},{4,20},{5,21},{6,22},{7,23},{8,24},{9,... | collective-permute-start | bytes 1843208 | tf_op jit(solution)/shard_map/ppermute | solution.py:408
  20.7 29.8 %collective-permute-start.7 = (bf16[320,960]{1,0:T(8,128)(2,1)}, bf16[320,960]{1,0:T(8,128)(2,1)}, u32[]{:S(2)}, u32[]{:S(2)}) collective-permute-start(bf16[320,960]{1,0:T(8,128)(2,1)} %bitcast.55), channel_id=1, source_target_pairs={{0,8},{1,9},{2,10},{3,11},{4,12},{5,13},{6,14},{7,15},{8,0},{9,1},... | collective-permute-start | bytes 1843208 | tf_op jit(solution)/shard_map/ppermute | solution.py:408
  22.3 28.2 %collective-permute-start.6 = (bf16[320,960]{1,0:T(8,128)(2,1)}, bf16[320,960]{1,0:T(8,128)(2,1)}, u32[]{:S(2)}, u32[]{:S(2)}) collective-permute-start(bf16[320,960]{1,0:T(8,128)(2,1)} %bitcast.56), channel_id=1, source_target_pairs={{0,4},{1,5},{2,6},{3,7},{4,0},{5,1},{6,2},{7,3},{8,12},{9,13},{10,... | collective-permute-start | bytes 1843208 | tf_op jit(solution)/shard_map/ppermute | solution.py:408
  27.2 26.9 %collective-permute-start.4 = (bf16[2,2,80,1024]{3,2,1,0:T(8,128)(2,1)}, bf16[2,2,80,1024]{3,2,1,0:T(8,128)(2,1)}, u32[]{:S(2)}, u32[]{:S(2)}) collective-permute-start(bf16[2,2,80,1024]{3,2,1,0:T(8,128)(2,1)} %bitcast.63), channel_id=1, source_target_pairs={{0,2},{1,3},{2,0},{3,1},{4,6},{5,7},{6,4},{7,5},{8,10},{9,11},{10,... | collective-permute-start | bytes 1966088 | tf_op jit(solution)/shard_map/ppermute | solution.py:408
  28.8 25.4 %collective-permute-start.5 = (bf16[2,2,80,704]{3,2,1,0:T(8,128)(2,1)}, bf16[2,2,80,704]{3,2,1,0:T(8,128)(2,1)}, u32[]{:S(2)}, u32[]{:S(2)}) collective-permute-start(bf16[2,2,80,704]{3,2,1,0:T(8,128)(2,1)} %bitcast.64), channel_id=1, source_target_pairs={{0,2},{1,3},{2,0},{3,1},{4,6},{5,7},{6,4},{7,5},{8,10},{9,11},{10,... | collective-permute-start | bytes 1351688 | tf_op jit(solution)/shard_map/ppermute | solution.py:408
  43.5 16.5 %copy-start.33 = (s32[32]{0:T(128)S(1)}, s32[32]{0:T(128)}, u32[]{:S(2)}) copy-start(s32[32]{0:T(128)} %param.13) | copy-start | bytes 388
  54.2 33.8 %collective-permute-start.12 = (bf16[320,960]{1,0:T(8,128)(2,1)}, bf16[320,960]{1,0:T(8,128)(2,1)S(1)}, u32[]{:S(2)}, u32[]{:S(2)}) collective-permute-start(bf16[320,960]{1,0:T(8,128)(2,1)} %collective-permute-done.8), channel_id=1, source_target_pairs={{0,8},{1,9},{2,10},{3,11},{4,12},{5,13},{6,14},{7,15},{8,0},{9,1},... | collective-permute-start | bytes 1843208 | tf_op jit(solution)/shard_map/ppermute | solution.py:408
  54.6 33.4 %collective-permute-start.11 = (bf16[320,960]{1,0:T(8,128)(2,1)}, bf16[320,960]{1,0:T(8,128)(2,1)S(1)}, u32[]{:S(2)}, u32[]{:S(2)}) collective-permute-start(bf16[320,960]{1,0:T(8,128)(2,1)} %collective-permute-done.8), channel_id=1, source_target_pairs={{0,4},{1,5},{2,6},{3,7},{4,0},{5,1},{6,2},{7,3},{8,12},{9,13},{10,... | collective-permute-start | bytes 1843208 | tf_op jit(solution)/shard_map/ppermute | solution.py:408
  58.1 29.9 %collective-permute-start.9 = (bf16[320,1024]{1,0:T(8,128)(2,1)}, bf16[320,1024]{1,0:T(8,128)(2,1)}, u32[]{:S(2)}, u32[]{:S(2)}) collective-permute-start(bf16[320,1024]{1,0:T(8,128)(2,1)} %bitcast.10.refs_0_), channel_id=1, source_target_pairs={{0,16},{1,17},{2,18},{3,19},{4,20},{5,21},{6,22},{7,23},{8,24},{9,... | collective-permute-start | bytes 1966088 | tf_op jit(solution)/shard_map/ppermute | solution.py:408
  58.9 29.1 %collective-permute-start.10 = (bf16[320,960]{1,0:T(8,128)(2,1)}, bf16[320,960]{1,0:T(8,128)(2,1)}, u32[]{:S(2)}, u32[]{:S(2)}) collective-permute-start(bf16[320,960]{1,0:T(8,128)(2,1)} %collective-permute-done.7), channel_id=1, source_target_pairs={{0,4},{1,5},{2,6},{3,7},{4,0},{5,1},{6,2},{7,3},{8,12},{9,13},{10,... | collective-permute-start | bytes 1843208 | tf_op jit(solution)/shard_map/ppermute | solution.py:408
  71.9 16.1 %copy-start.10 = (bf16[4,80,704]{2,1,0:T(8,128)(2,1)S(1)}, bf16[4,80,704]{2,1,0:T(8,128)(2,1)}, u32[]{:S(2)}) copy-start(bf16[4,80,704]{2,1,0:T(8,128)(2,1)} %get-tuple-element.214) | copy-start | bytes 1351684
  72.0 22.3 %copy-start.25 = (bf16[4,80,960]{2,1,0:T(8,128)(2,1)S(1)}, bf16[4,80,960]{2,1,0:T(8,128)(2,1)}, u32[]{:S(2)}) copy-start(bf16[4,80,960]{2,1,0:T(8,128)(2,1)} %join_qkv.1) | copy-start | bytes 1843204
  88.0 23.0 %collective-permute-start.15 = (bf16[320,704]{1,0:T(8,128)(2,1)S(1)}, bf16[320,704]{1,0:T(8,128)(2,1)S(1)}, u32[]{:S(2)}, u32[]{:S(2)}) collective-permute-start(bf16[320,704]{1,0:T(8,128)(2,1)S(1)} %bitcast.49), channel_id=1, source_target_pairs={{0,16},{1,17},{2,18},{3,19},{4,20},{5,21},{6,22},{7,23},{8,24},{9,... | collective-permute-start | bytes 1351688 | tf_op jit(solution)/shard_map/ppermute | solution.py:408
  90.7 20.4 %collective-permute-start.14 = (bf16[320,704]{1,0:T(8,128)(2,1)S(1)}, bf16[320,704]{1,0:T(8,128)(2,1)S(1)}, u32[]{:S(2)}, u32[]{:S(2)}) collective-permute-start(bf16[320,704]{1,0:T(8,128)(2,1)S(1)} %bitcast.50), channel_id=1, source_target_pairs={{0,4},{1,5},{2,6},{3,7},{4,0},{5,1},{6,2},{7,3},{8,12},{9,13},{10,... | collective-permute-start | bytes 1351688 | tf_op jit(solution)/shard_map/ppermute | solution.py:408
  91.2 24.1 %collective-permute-start.13 = (bf16[320,1024]{1,0:T(8,128)(2,1)}, bf16[320,1024]{1,0:T(8,128)(2,1)}, u32[]{:S(2)}, u32[]{:S(2)}) collective-permute-start(bf16[320,1024]{1,0:T(8,128)(2,1)} %bitcast.62), channel_id=1, source_target_pairs={{0,8},{1,9},{2,10},{3,11},{4,12},{5,13},{6,14},{7,15},{8,0},{9,1},... | collective-permute-start | bytes 1966088 | tf_op jit(solution)/shard_map/ppermute | solution.py:408
  92.8 22.3 %collective-permute-start.16 = (bf16[320,960]{1,0:T(8,128)(2,1)S(1)}, bf16[320,960]{1,0:T(8,128)(2,1)S(1)}, u32[]{:S(2)}, u32[]{:S(2)}) collective-permute-start(bf16[320,960]{1,0:T(8,128)(2,1)S(1)} %collective-permute-done.12.refs_0_), channel_id=1, source_target_pairs={{0,4},{1,5},{2,6},{3,7},{4,0},{5,1},{6,2},{7,3},{8,12},{9,13},{10,... | collective-permute-start | bytes 1843208 | tf_op jit(solution)/shard_map/ppermute | solution.py:408
  115.3 25.5 %collective-permute-start.17 = (bf16[320,1024]{1,0:T(8,128)(2,1)}, bf16[320,1024]{1,0:T(8,128)(2,1)}, u32[]{:S(2)}, u32[]{:S(2)}) collective-permute-start(bf16[320,1024]{1,0:T(8,128)(2,1)} %bitcast.10.refs_0_), channel_id=1, source_target_pairs={{0,4},{1,5},{2,6},{3,7},{4,0},{5,1},{6,2},{7,3},{8,12},{9,13},{10,... | collective-permute-start | bytes 1966088 | tf_op jit(solution)/shard_map/ppermute | solution.py:408
  116.9 27.4 %collective-permute-start.19 = (bf16[320,1024]{1,0:T(8,128)(2,1)}, bf16[320,1024]{1,0:T(8,128)(2,1)}, u32[]{:S(2)}, u32[]{:S(2)}) collective-permute-start(bf16[320,1024]{1,0:T(8,128)(2,1)} %collective-permute-done.13.refs_2_), channel_id=1, source_target_pairs={{0,16},{1,17},{2,18},{3,19},{4,20},{5,21},{6,22},{7,23},{8,24},{9,... | collective-permute-start | bytes 1966088 | tf_op jit(solution)/shard_map/ppermute | solution.py:408
  117.7 26.6 %collective-permute-start.18 = (bf16[320,1024]{1,0:T(8,128)(2,1)}, bf16[320,1024]{1,0:T(8,128)(2,1)}, u32[]{:S(2)}, u32[]{:S(2)}) collective-permute-start(bf16[320,1024]{1,0:T(8,128)(2,1)} %collective-permute-done.9.refs_4_), channel_id=1, source_target_pairs={{0,4},{1,5},{2,6},{3,7},{4,0},{5,1},{6,2},{7,3},{8,12},{9,13},{10,... | collective-permute-start | bytes 1966088 | tf_op jit(solution)/shard_map/ppermute | solution.py:408
  118.3 22.5 %collective-permute-start.20 = (bf16[320,704]{1,0:T(8,128)(2,1)}, bf16[320,704]{1,0:T(8,128)(2,1)S(1)}, u32[]{:S(2)}, u32[]{:S(2)}) collective-permute-start(bf16[320,704]{1,0:T(8,128)(2,1)} %bitcast.13), channel_id=1, source_target_pairs={{0,8},{1,9},{2,10},{3,11},{4,12},{5,13},{6,14},{7,15},{8,0},{9,1},... | collective-permute-start | bytes 1351688 | tf_op jit(solution)/shard_map/ppermute | solution.py:408
  144.3 4.7 %collective-permute-start.24 = (bf16[256,2560]{1,0:T(8,128)(2,1)}, bf16[256,2560]{1,0:T(8,128)(2,1)}, u32[]{:S(2)}, u32[]{:S(2)}) collective-permute-start(bf16[256,2560]{1,0:T(8,128)(2,1)} %get-tuple-element.272), channel_id=1, source_target_pairs={{0,1},{1,0},{2,3},{3,2},{4,5},{5,4},{6,7},{7,6},{8,9},{9,8},{10,11... | collective-permute-start | bytes 3932168 | tf_op jit(solution)/shard_map/ppermute | solution.py:408
  145.2 27.8 %collective-permute-start.21 = (bf16[320,1024]{1,0:T(8,128)(2,1)}, bf16[320,1024]{1,0:T(8,128)(2,1)S(1)}, u32[]{:S(2)}, u32[]{:S(2)}) collective-permute-start(bf16[320,1024]{1,0:T(8,128)(2,1)} %collective-permute-done.13.refs_2_), channel_id=1, source_target_pairs={{0,4},{1,5},{2,6},{3,7},{4,0},{5,1},{6,2},{7,3},{8,12},{9,13},{10,... | collective-permute-start | bytes 1966088 | tf_op jit(solution)/shard_map/ppermute | solution.py:408
  146.5 24.7 %collective-permute-start.23 = (bf16[320,704]{1,0:T(8,128)(2,1)}, bf16[320,704]{1,0:T(8,128)(2,1)S(1)}, u32[]{:S(2)}, u32[]{:S(2)}) collective-permute-start(bf16[320,704]{1,0:T(8,128)(2,1)} %copy-done.16), channel_id=1, source_target_pairs={{0,16},{1,17},{2,18},{3,19},{4,20},{5,21},{6,22},{7,23},{8,24},{9,... | collective-permute-start | bytes 1351688 | tf_op jit(solution)/shard_map/ppermute | solution.py:408
  147.1 25.9 %collective-permute-start.22 = (bf16[320,704]{1,0:T(8,128)(2,1)}, bf16[320,704]{1,0:T(8,128)(2,1)}, u32[]{:S(2)}, u32[]{:S(2)}) collective-permute-start(bf16[320,704]{1,0:T(8,128)(2,1)} %copy-done.12), channel_id=1, source_target_pairs={{0,4},{1,5},{2,6},{3,7},{4,0},{5,1},{6,2},{7,3},{8,12},{9,13},{10,... | collective-permute-start | bytes 1351688 | tf_op jit(solution)/shard_map/ppermute | solution.py:408
  152.6 22.1 %copy-start.7 = (f32[128,2560]{1,0:T(8,128)S(1)}, f32[128,2560]{1,0:T(8,128)}, u32[]{:S(2)}) copy-start(f32[128,2560]{1,0:T(8,128)} %copy-done.6) | copy-start | bytes 3932164
  152.6 21.2 %collective-permute-start.25 = (bf16[128,2560]{1,0:T(8,128)(2,1)}, bf16[128,2560]{1,0:T(8,128)(2,1)S(1)}, u32[]{:S(2)}, u32[]{:S(2)}) collective-permute-start(bf16[128,2560]{1,0:T(8,128)(2,1)} %get-tuple-element.275), channel_id=1, source_target_pairs={{0,2},{1,3},{2,0},{3,1},{4,6},{5,7},{6,4},{7,5},{8,10},{9,11},{10,... | collective-permute-start | bytes 1966088 | tf_op jit(solution)/shard_map/ppermute | solution.py:408
  179.2 16.4 %collective-permute-start.27 = (bf16[128,2560]{1,0:T(8,128)(2,1)}, bf16[128,2560]{1,0:T(8,128)(2,1)}, u32[]{:S(2)}, u32[]{:S(2)}) collective-permute-start(bf16[128,2560]{1,0:T(8,128)(2,1)} %pad_maximum_fusion.3), channel_id=1, source_target_pairs={{0,8},{1,9},{2,10},{3,11},{4,12},{5,13},{6,14},{7,15},{8,0},{9,1},... | collective-permute-start | bytes 1966088 | tf_op jit(solution)/shard_map/ppermute | solution.py:408
  179.5 18.2 %collective-permute-start.26 = (bf16[320,1024]{1,0:T(8,128)(2,1)}, bf16[320,1024]{1,0:T(8,128)(2,1)S(1)}, u32[]{:S(2)}, u32[]{:S(2)}) collective-permute-start(bf16[320,1024]{1,0:T(8,128)(2,1)} %collective-permute-done.19.refs_6_), channel_id=1, source_target_pairs={{0,4},{1,5},{2,6},{3,7},{4,0},{5,1},{6,2},{7,3},{8,12},{9,13},{10,... | collective-permute-start | bytes 1966088 | tf_op jit(solution)/shard_map/ppermute | solution.py:408
  180.3 16.3 %collective-permute-start.28 = (bf16[128,2560]{1,0:T(8,128)(2,1)}, bf16[128,2560]{1,0:T(8,128)(2,1)}, u32[]{:S(2)}, u32[]{:S(2)}) collective-permute-start(bf16[128,2560]{1,0:T(8,128)(2,1)} %multiply_convert_fusion.1), channel_id=1, source_target_pairs={{0,2},{1,3},{2,0},{3,1},{4,6},{5,7},{6,4},{7,5},{8,10},{9,11},{10,... | collective-permute-start | bytes 1966088 | tf_op jit(solution)/shard_map/ppermute | solution.py:408
  197.8 16.3 %collective-permute-start.29 = (bf16[4,1,128,320]{2,3,0,1:T(8,128)(2,1)S(1)}, bf16[4,1,128,320]{2,3,0,1:T(8,128)(2,1)S(1)}, u32[]{:S(2)}, u32[]{:S(2)}) collective-permute-start(bf16[4,1,128,320]{2,3,0,1:T(8,128)(2,1)S(1)} %get-tuple-element.371), channel_id=1, source_target_pairs={{0,16},{1,17},{2,18},{3,19},{4,20},{5,21},{6,22},{7,23},{8,24},{9,... | collective-permute-start | bytes 983048 | tf_op jit(solution)/shard_map/ppermute | solution.py:408
  200.5 13.6 %collective-permute-start.31 = (bf16[64,2560]{1,0:T(8,128)(2,1)S(1)}, bf16[64,2560]{1,0:T(8,128)(2,1)S(1)}, u32[]{:S(2)}, u32[]{:S(2)}) collective-permute-start(bf16[64,2560]{1,0:T(8,128)(2,1)S(1)} %slice.120), channel_id=1, source_target_pairs={{0,2},{1,3},{2,0},{3,1},{4,6},{5,7},{6,4},{7,5},{8,10},{9,11},{10,... | collective-permute-start | bytes 983048 | tf_op jit(solution)/shard_map/ppermute | solution.py:408
  202.0 13.5 %collective-permute-start.32 = (bf16[64,2560]{1,0:T(8,128)(2,1)S(1)}, bf16[64,2560]{1,0:T(8,128)(2,1)S(1)}, u32[]{:S(2)}, u32[]{:S(2)}) collective-permute-start(bf16[64,2560]{1,0:T(8,128)(2,1)S(1)} %pad_maximum_fusion.6), channel_id=1, source_target_pairs={{0,8},{1,9},{2,10},{3,11},{4,12},{5,13},{6,14},{7,15},{8,0},{9,1},... | collective-permute-start | bytes 983048 | tf_op jit(solution)/shard_map/ppermute | solution.py:408
  202.3 14.4 %collective-permute-start.30 = (bf16[320,704]{1,0:T(8,128)(2,1)S(1)}, bf16[320,704]{1,0:T(8,128)(2,1)S(1)}, u32[]{:S(2)}, u32[]{:S(2)}) collective-permute-start(bf16[320,704]{1,0:T(8,128)(2,1)S(1)} %copy-done.17), channel_id=1, source_target_pairs={{0,4},{1,5},{2,6},{3,7},{4,0},{5,1},{6,2},{7,3},{8,12},{9,13},{10,... | collective-permute-start | bytes 1351688 | tf_op jit(solution)/shard_map/ppermute | solution.py:408
  216.8 4.1 %collective-permute-start.35 = (bf16[256,2560]{1,0:T(8,128)(2,1)S(1)}, bf16[256,2560]{1,0:T(8,128)(2,1)S(1)}, u32[]{:S(2)}, u32[]{:S(2)}) collective-permute-start(bf16[256,2560]{1,0:T(8,128)(2,1)S(1)} %pad_maximum_fusion.2), channel_id=1, source_target_pairs={{0,1},{1,0},{2,3},{3,2},{4,5},{5,4},{6,7},{7,6},{8,9},{9,8},{10,11... | collective-permute-start | bytes 3932168 | tf_op jit(solution)/shard_map/ppermute | solution.py:408
  216.8 4.9 %collective-permute-start.34 = (bf16[256,2560]{1,0:T(8,128)(2,1)S(1)}, bf16[256,2560]{1,0:T(8,128)(2,1)S(1)}, u32[]{:S(2)}, u32[]{:S(2)}) collective-permute-start(bf16[256,2560]{1,0:T(8,128)(2,1)S(1)} %pad_maximum_fusion.1), channel_id=1, source_target_pairs={{0,1},{1,0},{2,3},{3,2},{4,5},{5,4},{6,7},{7,6},{8,9},{9,8},{10,11... | collective-permute-start | bytes 3932168 | tf_op jit(solution)/shard_map/ppermute | solution.py:408
  217.3 13.2 %collective-permute-start.33 = (bf16[320,704]{1,0:T(8,128)(2,1)S(1)}, bf16[320,704]{1,0:T(8,128)(2,1)S(1)}, u32[]{:S(2)}, u32[]{:S(2)}) collective-permute-start(bf16[320,704]{1,0:T(8,128)(2,1)S(1)} %copy-done.19), channel_id=1, source_target_pairs={{0,4},{1,5},{2,6},{3,7},{4,0},{5,1},{6,2},{7,3},{8,12},{9,13},{10,... | collective-permute-start | bytes 1351688 | tf_op jit(solution)/shard_map/ppermute | solution.py:408
  230.5 21.5 %collective-permute-start.36 = (bf16[512,512]{1,0:T(8,128)(2,1)S(1)}, bf16[512,512]{1,0:T(8,128)(2,1)S(1)}, u32[]{:S(2)}, u32[]{:S(2)}) collective-permute-start(bf16[512,512]{1,0:T(8,128)(2,1)S(1)} %gated.5), channel_id=1, source_target_pairs={{0,8},{1,9},{2,10},{3,11},{4,12},{5,13},{6,14},{7,15},{8,0},{9,1},... | collective-permute-start | bytes 1572872 | tf_op jit(solution)/shard_map/ppermute | solution.py:408
  230.6 13.2 %collective-permute-start.38 = (bf16[2,2,128,320]{2,3,1,0:T(8,128)(2,1)S(1)}, bf16[2,2,128,320]{2,3,1,0:T(8,128)(2,1)S(1)}, u32[]{:S(2)}, u32[]{:S(2)}) collective-permute-start(bf16[2,2,128,320]{2,3,1,0:T(8,128)(2,1)S(1)} %bitcast.61), channel_id=1, source_target_pairs={{0,4},{1,5},{2,6},{3,7},{4,0},{5,1},{6,2},{7,3},{8,12},{9,13},{10,... | collective-permute-start | bytes 983048 | tf_op jit(solution)/shard_map/ppermute | solution.py:408
  235.6 16.4 %collective-permute-start.37 = (bf16[512,352]{1,0:T(8,128)(2,1)S(1)}, bf16[512,352]{1,0:T(8,128)(2,1)S(1)}, u32[]{:S(2)}, u32[]{:S(2)}) collective-permute-start(bf16[512,352]{1,0:T(8,128)(2,1)S(1)} %gated.6), channel_id=1, source_target_pairs={{0,8},{1,9},{2,10},{3,11},{4,12},{5,13},{6,14},{7,15},{8,0},{9,1},... | collective-permute-start | bytes 1081352 | tf_op jit(solution)/shard_map/ppermute | solution.py:408
  253.8 3.1 %collective-permute-start.39 = (bf16[256,2560]{1,0:T(8,128)(2,1)S(1)}, bf16[256,2560]{1,0:T(8,128)(2,1)S(1)}, u32[]{:S(2)}, u32[]{:S(2)}) collective-permute-start(bf16[256,2560]{1,0:T(8,128)(2,1)S(1)} %rows_product.5), channel_id=1, source_target_pairs={{0,1},{1,0},{2,3},{3,2},{4,5},{5,4},{6,7},{7,6},{8,9},{9,8},{10,11... | collective-permute-start | bytes 3932168 | tf_op jit(solution)/shard_map/ppermute | solution.py:408
  257.1 16.8 %collective-permute-start.40 = (bf16[128,2560]{1,0:T(8,128)(2,1)S(1)}, bf16[128,2560]{1,0:T(8,128)(2,1)S(1)}, u32[]{:S(2)}, u32[]{:S(2)}) collective-permute-start(bf16[128,2560]{1,0:T(8,128)(2,1)S(1)} %get-tuple-element.359), channel_id=1, source_target_pairs={{0,2},{1,3},{2,0},{3,1},{4,6},{5,7},{6,4},{7,5},{8,10},{9,11},{10,... | collective-permute-start | bytes 1966088 | tf_op jit(solution)/shard_map/ppermute | solution.py:408
  257.7 9.5 %collective-permute-start.41 = (bf16[1,4,128,320]{2,3,1,0:T(8,128)(2,1)S(1)}, bf16[1,4,128,320]{2,3,1,0:T(8,128)(2,1)S(1)}, u32[]{:S(2)}, u32[]{:S(2)}) collective-permute-start(bf16[1,4,128,320]{2,3,1,0:T(8,128)(2,1)S(1)} %get-tuple-element.367), channel_id=1, source_target_pairs={{0,8},{1,9},{2,10},{3,11},{4,12},{5,13},{6,14},{7,15},{8,0},{9,1},... | collective-permute-start | bytes 983048 | tf_op jit(solution)/shard_map/ppermute | solution.py:408
  (34 other events, 190.5 us)

commit v4 on v3

--- a/solution.py
+++ b/solution.py
@@ -142,7 +142,7 @@
 VMEM = pl.BlockSpec(memory_space=pltpu.VMEM)
 
 
-def call(kernel, smem, vmem, shapes, scratch, name, mib=48):
+def call(kernel, smem, vmem, shapes, scratch, name, mib=48, flops=1):
     return pl.pallas_call(
         kernel,
         in_specs=[SMEM] * len(smem) + [VMEM] * len(vmem),
@@ -150,7 +150,7 @@
         out_shape=[jax.ShapeDtypeStruct(*shape) for shape in shapes],
         scratch_shapes=[pltpu.VMEM(*shape) for shape in scratch],
         compiler_params=pltpu.CompilerParams(vmem_limit_bytes=mib * 2**20),
-        cost_estimate=pl.CostEstimate(flops=1, transcendentals=0, bytes_accessed=1),
+        cost_estimate=pl.CostEstimate(flops=flops, transcendentals=0, bytes_accessed=1),
         name=name,
     )(*smem, *vmem)
 
@@ -197,7 +197,7 @@
     )(value, *others)
 
 
-def attend(place, lengths, joined, x_last, w_last, tables, out_in, sizes, shares):
+def attend(place, lengths, chosen, joined, x_last, w_last, tables, out_in, sizes, shares):
     seq_len, columns = joined.shape
     heads, kv_heads, head_dim = sizes
     group = heads // kv_heads
@@ -207,11 +207,14 @@
     width = w_last[0].shape[0]
     model_dim = out_in.shape[1]
     share = seq_len // len(shares)
+    slots = chosen.shape[0] // 2
     tile = 128
 
-    def kernel(place_ref, length_ref, joined_ref, x_ref, cos_ref, sin_ref, out_in_ref, *refs):
+    def kernel(
+        place_ref, length_ref, chosen_ref, joined_ref, x_ref, cos_ref, sin_ref, out_in_ref, *refs
+    ):
         w_refs = refs[: len(w_last)]
-        leaving_ref, staying_ref, cache_ref, qk, v, context = refs[len(w_last) :]
+        leaving_ref, staying_ref, *boxes, cache_ref, qk, v, context = refs[len(w_last) :]
         tp, length = place_ref[0], length_ref[0]
         lane = lax.broadcasted_iota(jnp.int32, (tile, wide), 1)
         first = lax.rem(lane, head_dim) < half
@@ -234,6 +237,9 @@
             live = (slot < length).astype(F32)
             cache_ref[at, :k_cols] = (turned[:, q_cols : q_cols + k_cols] * live).astype(BF)
             cache_ref[at, k_cols:] = (rows[:, q_cols + k_cols :] * live).astype(BF)
+        for i in range(chosen.shape[0]):
+            page = cache_ref[pl.ds(pl.multiple_of(chosen_ref[i] * PAGE, PAGE), PAGE), :]
+            boxes[i // slots][i % slots * PAGE : (i % slots + 1) * PAGE, :] = page
         for k in range(kv_heads):
             key_at = q_cols + k * head_dim
             for t in range(seq_len // tile):
@@ -280,14 +286,14 @@
 
     return call(
         kernel,
-        [place, lengths],
+        [place, lengths, chosen],
         [joined, x_last, *tables, out_in, *w_last],
         [
             ((seq_len // 2, model_dim), BF),
             ((seq_len // 2, model_dim), F32),
-            ((seq_len, 2 * k_cols), BF),
-        ],
-        [((seq_len, wide), BF), ((seq_len, k_cols), BF), ((seq_len, q_cols), BF)],
+        ]
+        + [((slots * PAGE, 2 * k_cols), BF)] * 2,
+        [((seq_len, 2 * k_cols), BF), ((seq_len, wide), BF), ((seq_len, k_cols), BF), ((seq_len, q_cols), BF)],
         "attend",
     )
 
@@ -303,26 +309,27 @@
     return call(kernel, [], blocks, [((count * each, columns), BF)], [], "assemble", 24)[0]
 
 
-def rows_product(pieces, weight, first=0, count=None, base=None, dtype=F32):
-    rows, columns = count or pieces[0].shape[0], weight.shape[1]
+def rows_product(pieces, weight, at, count, base=None, dtype=F32):
+    columns = weight.shape[1]
     tile = 128
 
     def kernel(*refs):
         weight_ref = refs[len(pieces)]
 
-        @pl.loop(0, rows // tile)
+        @pl.loop(0, count // tile)
         def _(i):
-            source = pl.ds(pl.multiple_of(first + i * tile, tile), tile)
-            total = 0.0 if base is None else refs[len(pieces) + 1][source, :]
-            begin = 0
-            for ref in refs[: len(pieces)]:
-                end = begin + ref.shape[1]
+            out = pl.ds(pl.multiple_of(i * tile, tile), tile)
+            total = 0.0 if base is None else refs[len(pieces) + 1][out, :]
+            begin = at
+            for (piece, first), ref in zip(pieces, refs):
+                end = begin + piece.shape[1]
+                source = pl.ds(pl.multiple_of(first + i * tile, tile), tile)
                 total = total + dot(ref[source, :], weight_ref[begin:end, :])
                 begin = end
-            refs[-1][pl.ds(pl.multiple_of(i * tile, tile), tile), :] = total.astype(dtype)
-
-    ins = [*pieces, weight] + ([] if base is None else [base])
-    return call(kernel, [], ins, [((rows, columns), dtype)], [], "rows_product", 24)[0]
+            refs[-1][out, :] = total.astype(dtype)
+
+    ins = [piece for piece, _ in pieces] + [weight] + ([] if base is None else [base])
+    return call(kernel, [], ins, [((count, columns), dtype)], [], "rows_product", 24)[0]
 
 
 def add_share(staying, arrived, extra):
@@ -346,6 +353,40 @@
     )
 
 
+def norm_share(keep, arrived, gain):
+    rows, columns = keep.shape
+    step = columns * PAIR // gain.shape[0]
+
+    def kernel(keep_ref, arrived_ref, gain_ref, resid_ref, norm_ref, turned_ref):
+        resid = keep_ref[...] + arrived_ref[...].astype(F32)
+        resid_ref[...] = resid
+        norm = normed(resid, gain_ref[...])
+        norm_ref[...] = norm
+        for i in range(columns // step):
+            at, source = i * step, (i ^ 1) * step
+            turned_ref[:, at : at + step] = norm[:, source : source + step]
+
+    shapes = [((rows, columns), F32)] + [((rows, columns), BF)] * 2
+    return call(
+        kernel, [], [keep, arrived, gain.reshape(1, columns)], shapes, [], "norm_share", 24
+    )
+
+
+def pick_pages(source, pages):
+    count = source.shape[0]
+
+    def kernel(source_ref, *refs):
+        for p in range(count):
+            for i, ref in enumerate(refs[:-1]):
+
+                @pl.when(source_ref[p] == i)
+                def _(p=p, ref=ref):
+                    refs[-1][p] = ref[...]
+
+    shapes = [((count, *pages[0].shape), BF)]
+    return call(kernel, [source], pages, shapes, [], "pick_pages", 16, 5 * 10**9)[0]
+
+
 def class_rows(place, weight):
     rows, columns = weight.shape
     half = rows // 2
@@ -358,20 +399,25 @@
     return call(kernel, [place], [weight], [((half, columns), BF)] * 2, [], "class_rows")
 
 
-def gated(tokens, weight):
-    rows = tokens.shape[0]
+def gated(tokens, weight, parts=1):
+    rows = tokens.shape[0] // parts
     size = weight.shape[1] // 2
     tile = 256
 
-    def kernel(tokens_ref, weight_ref, out_ref):
-        @pl.loop(0, rows // tile)
-        def _(i):
-            at = pl.ds(pl.multiple_of(i * tile, tile), tile)
-            projected = dot(tokens_ref[at, :], weight_ref[...])
-            gate, up = projected[:, :size], projected[:, size:]
-            out_ref[at, :] = (gate / (1.0 + jnp.exp(-gate)) * up).astype(BF)
-
-    return call(kernel, [], [tokens, weight], [((rows, size), BF)], [], "gated", 24)[0]
+    def kernel(tokens_ref, weight_ref, *outs):
+        for p, out_ref in enumerate(outs):
+
+            @pl.loop(0, rows // tile)
+            def _(i, p=p, out_ref=out_ref):
+                source = pl.ds(pl.multiple_of(p * rows + i * tile, tile), tile)
+                projected = dot(tokens_ref[source, :], weight_ref[...])
+                gate, up = projected[:, :size], projected[:, size:]
+                out_ref[pl.ds(pl.multiple_of(i * tile, tile), tile), :] = (
+                    gate / (1.0 + jnp.exp(-gate)) * up
+                ).astype(BF)
+
+    shapes = [((rows, size), BF)] * parts
+    return call(kernel, [], [tokens, weight], shapes, [], "gated", 24)
 
 
 def body(
@@ -466,9 +512,12 @@
     qkv[1] = swap(qkv_own, 1, 0)
     far = list(pack_far(place, gu_own, gu_near, chunks))
     tokens, far = sync((tokens, far))
-    for c in range(len(chunks)):
-        moved = [swap(far[c][f], 0, 2 * f + 2) for f in range(n_tp // 2 - 1)]
-        far[c] = jnp.stack(moved) if len(moved) > 1 else moved[0][None]
+
+    def over_y(value):
+        moved = [swap(value[f], 0, 2 * f + 2) for f in range(n_tp // 2 - 1)]
+        return jnp.stack(moved) if len(moved) > 1 else moved[0][None]
+
+    blocks = [join_gateup(place, gu_own, gu_near, over_y(far[0]), 0)]
     order = jnp.arange(n_req, dtype=jnp.int32) ^ req
     shards = (order[:, None] * n_tp + jnp.arange(n_tp, dtype=jnp.int32)[None, :]).reshape(-1)
     blocks_at = trainer_layout[shards]
@@ -487,7 +536,8 @@
     st = sync(
         dict(
             qkv=qkv,
-            far=far,
+            far=far[1],
+            blocks=blocks,
             gu_own=gu_own,
             gu_near=gu_near,
             x_norm=x_norm,
@@ -502,11 +552,8 @@
 
     qkv, far, x_norm, tokens_in = st["qkv"], st["far"], st["x_norm"], st["tokens_in"]
     columns_at, page_slot = st["onehot_at"], st["page_slot"]
-    blocks = []
-    for c in range(len(chunks)):
-        blocks.append(
-            join_gateup(place, st["gu_own"], st["gu_near"], far[c], 2 * sum(chunks[:c]))
-        )
+    blocks = list(st["blocks"])
+    blocks.append(join_gateup(place, st["gu_own"], st["gu_near"], over_y(far), 2 * chunks[0]))
     spread_z(qkv, doubles)
     for r in singles[::-1]:
         qkv[r ^ 1] = swap(qkv[r], 1, 0)
@@ -517,15 +564,21 @@
     ffn_gain_in = st["ffn_gain"].reshape(devices, rows_each)[blocks_at].reshape(-1)
     n_pages = seq_len // PAGE
     holders = lax.dynamic_slice_in_dim(page_slot, req * n_pages, n_pages, 0) // n_pages
-    page_bits = [bit for bit in zbits if bit != PAIR] + [1, PAIR]
+    page_bits = [PAIR, 1] + [bit for bit in zbits if bit != PAIR]
     at_slot = [
-        sum(bit for k, bit in enumerate(page_bits) if (i >> k) & 1) for i in range(n_req)
+        sum(bit for k, bit in enumerate(reversed(page_bits)) if (i >> k) & 1)
+        for i in range(n_req)
     ]
     relative = jnp.asarray(at_slot, jnp.int32) ^ req
     chosen = jnp.argmax(holders[None, :] == relative[:, None], axis=1)
     targets = req * n_pages + jnp.arange(n_pages, dtype=jnp.int32)
     source = jnp.argmax(page_slot[None, :] == targets[:, None], axis=1) // n_pages
-    source = jnp.argmax(relative[None, :] == source[:, None], axis=1)
+    arrival = [0]
+    for bit in page_bits:
+        arrival = arrival + [r ^ bit for r in arrival]
+    arrival = jnp.asarray(arrival, jnp.int32) ^ req
+    source = jnp.argmax(arrival[None, :] == source[:, None], axis=1)
+    tokens_share = lax.dynamic_slice_in_dim(tokens_in, tp * share, share, 0)
     st = sync(
         dict(
             qkv=qkv,
@@ -536,11 +589,13 @@
             down_rel=down_rel,
             ffn_gain_in=ffn_gain_in,
             pages=(chosen, source),
+            tokens_share=tokens_share,
         )
     )
 
     qkv, gu, blocks, x_norm, out_in = (st[k] for k in ("qkv", "gu", "blocks", "x_norm", "out_in"))
     chosen, source = st["pages"]
+    tokens_share = st["tokens_share"]
     down_rel, ffn_gain_in = st["down_rel"], st["ffn_gain_in"]
     spread_class(gu[0], *blocks[0], [PAIR])
     spread_class(gu[1], *blocks[1], plain)
@@ -569,9 +624,10 @@
     for r in plain:
         gu[0][r ^ 1] = swap(gu[0][r], 1, 0)
     shares = sorted(range(n_tp), key=lambda s: [(s >> k) & 1 for k in range(len(bits))])
-    leaving, staying, cache_rows = attend(
+    leaving, staying, *box = attend(
         place,
         lengths,
+        chosen.astype(jnp.int32),
         st["joined"],
         jnp.concatenate([x_norm[:, r * width : (r + 1) * width] for r in last], axis=1),
         [qkv[r] for r in last],
@@ -580,65 +636,48 @@
         (local_heads, local_kv, head_dim),
         shares,
     )
-    st = sync(
-        dict(gu=gu, blocks=blocks, leaving=leaving, staying=staying, pages=cache_rows, out=out_in)
-    )
-
-    gu, blocks = st["gu"], st["blocks"]
-    tokens_share = lax.dynamic_slice_in_dim(tokens_in, tp * share, share, 0)
+    st = sync(dict(gu=gu, leaving=leaving, staying=staying, box=box))
+
+    gu, box = st["gu"], st["box"]
     keep, send = add_share(st["staying"], swap(st["leaving"], 0, bits[0]), tokens_share)
-    resid_in = keep + swap(send, 0, bits[1]).astype(F32)
+    arrived = swap(send, 0, bits[1])
     spread_class(gu[1], None, None, crossed)
     gu[0][PAIR ^ 1] = swap(gu[0][PAIR], 1, 0)
     for r in plain:
         gu[1][r ^ 1] = swap(gu[1][r], 1, 0)
-    h_share = normed(resid_in, ffn_gain_in)
-
-    def reordered(values):
-        return jnp.concatenate(
-            [values[:, (j ^ PAIR) * width : ((j ^ PAIR) + 1) * width] for j in range(n_req)], axis=1
+
+    def page_parts(box):
+        half = box[0].shape[0] // 2
+        return [pages[:half] for pages in box], jnp.concatenate(
+            [pages[half:] for pages in box], axis=0
         )
 
-    def page_step(box, bit):
-        box = box.reshape((-1, 2) + box.shape[1:])
-        return jnp.concatenate([box[:, 0], swap(box[:, 1], bit, 0)], axis=1)
+    def page_step(parts, bit):
+        kept, leaving = parts
+        half = kept[0].shape[0]
+        moved = swap(leaving, bit, 0)
+        return kept + [moved[at : at + half] for at in range(0, leaving.shape[0], half)]
 
     late = crossed[0]
-    gu[1][late] = hold(gu[1][late], gu[0][PAIR ^ 1], *[gu[1][r ^ 1] for r in plain])
-    st = sync(dict(gu=gu, h=(h_share, reordered(h_share)), resid_in=resid_in, pages=st["pages"]))
+    box = [box[0], swap(box[1], page_bits[0], 0)]
+    gu[1][late] = hold(gu[1][late], box[1], gu[0][PAIR ^ 1], *[gu[1][r ^ 1] for r in plain])
+    resid_in, h_share, h_leaving = norm_share(
+        keep, arrived, ffn_gain_in.reshape(n_req, model_dim // n_req)
+    )
+    st = sync(dict(gu=gu, h=(h_share, h_leaving), resid_in=resid_in, box=box))
 
     gu, resid_in = st["gu"], st["resid_in"]
     h_share, h_leaving = st["h"]
     cross = n_tp // 2
-    h_across = swap(h_share, 0, cross)
-    h_pair = swap(h_leaving, PAIR, 0)
+    own = (h_share, swap(h_share, 0, cross))
+    theirs = (swap(h_leaving, PAIR, 0), swap(h_leaving, PAIR, cross))
     for r in crossed:
         gu[0][r ^ 1] = swap(gu[0][r], 1, 0)
+    gu[1][PAIR ^ 1] = swap(gu[1][PAIR], 1, 0)
     coarse = resid_in.astype(BF)
     fine = (resid_in - coarse.astype(F32)).astype(BF)
     terms = permute_columns(jnp.concatenate([coarse, fine], axis=0), columns_back)
-    cut = share // 2
-    st = sync(
-        dict(
-            gu=gu,
-            own=(h_share, h_across),
-            theirs=h_pair,
-            halves=(h_pair[:cut], reordered(h_across[cut:])),
-            terms=terms,
-            box=st["pages"].reshape(n_pages, PAGE, 2 * k_cols)[chosen][:, None],
-        )
-    )
-
-    gu, box = st["gu"], st["box"]
-    over_y, over_pair = st["halves"]
-    h_diag = [swap(over_y, 0, cross), swap(over_pair, PAIR, 0)]
-    gu[1][PAIR ^ 1] = swap(gu[1][PAIR], 1, 0)
-    for bit in page_bits[:-2]:
-        box = page_step(box, bit)
-    resid = st["terms"][:share] + st["terms"][share:]
-    own = jnp.concatenate(st["own"], axis=0)
-    theirs = jnp.concatenate([st["theirs"]] + h_diag, axis=0)
-    st = sync(dict(gu=gu, h=(own, theirs), resid=resid, box=box))
+    st = sync(dict(gu=gu, own=own, theirs=theirs, terms=terms, box=page_parts(st["box"])))
 
     def whole(rows):
         for bit in bits[:-1]:
@@ -646,38 +685,43 @@
         return rows
 
     gu, box = st["gu"], st["box"]
-    h_own, h_theirs = (whole(rows) for rows in st["h"])
+    resid = st["terms"][:share] + st["terms"][share:]
+    h_own, h_theirs = (whole(jnp.concatenate(st[k], axis=0)) for k in ("own", "theirs"))
     for r in crossed:
         gu[1][r ^ 1] = swap(gu[1][r], 1, 0)
     weight = assemble([gu[0][r] for r in range(n_req)])
-    theirs = gated(h_theirs, weight)
-    kept = [gated(h_own, weight)]
-    st = sync(
-        dict(gu=gu[1], h=(h_own, h_theirs), hidden=(kept, theirs), resid=st["resid"], box=box)
-    )
+    theirs = gated(h_theirs, weight, 2)
+    kept = gated(h_own, weight)
+    st = sync(dict(gu=gu[1], h=(h_own, h_theirs), hidden=(kept, theirs), resid=resid, box=box))
 
     resid, box = st["resid"], st["box"]
     h_own, h_theirs = st["h"]
     kept, theirs = st["hidden"]
-    returned = [swap(theirs, PAIR, 0)]
+    returned = [swap(theirs[0], PAIR, 0)]
+    second, _ = sync((theirs[1], returned[0]))
+    returned.append(swap(second, PAIR, 0))
     weight = assemble([st["gu"][r] for r in range(n_req)])
     theirs = gated(h_theirs, weight)
-    box = page_step(box, page_bits[-2])
     h_own, theirs = sync((h_own, theirs))
-    returned.append(swap(theirs, PAIR, 0))
-    kept.append(gated(h_own, weight))
-    product = rows_product(kept, down_rel[0])
-    returned, box, product = sync((returned, box, product))
+    kept = list(kept) + list(gated(h_own, weight))
     rows = seq_len // 2
-    leaving = rows_product(returned, down_rel[1], rows, rows, product, BF)
+    product = []
+    for i in range(2):
+        part = rows_product([(piece, i * rows) for piece in kept], down_rel[0], 0, rows)
+        product.append(rows_product([(returned[i], 0)], down_rel[1], 0, rows, part))
+    box = page_parts(page_step(box, page_bits[1]))
+    returned, box, product = sync((swap(theirs[0], PAIR, 0), box, product))
+    leaving = rows_product([(returned, rows)], down_rel[1], chunks[0], rows, product[1], BF)
     arrived = swap(leaving, 0, bits[0])
-    staying = rows_product(returned, down_rel[1], 0, rows, product)
+    staying = rows_product([(returned, 0)], down_rel[1], chunks[0], rows, product[0])
     keep, send = add_share(staying, arrived, resid)
-    box = page_step(box, page_bits[-1])
+    box = page_step(box, page_bits[2])
+    for bit in page_bits[3:]:
+        box = page_step(page_parts(box), bit)
     share_slots = tp * share + jnp.arange(share, dtype=jnp.int32)
     live_share = (share_slots < lengths[0]).astype(F32)
     layer_out = ((keep + swap(send, 0, bits[1]).astype(F32)) * live_share[:, None]).astype(BF)
-    kv_cache = box[0][source]
+    kv_cache = pick_pages(source.astype(jnp.int32), box)
     return (layer_out, kv_cache)
 
 

time: 276 us -> 267 us (0.967)
  other arithmetic: 12.2 us -> 6.37 us
    gather x2 -> x0, local copies, waits for them, and re-layouts: 3.75 us -> none  [the longest x1 2.44 us: body(): st['pages'].reshape(n_pages, PAGE, 2 * k_cols)[chosen][:, None]]
    concatenate x6 -> x4, other arithmetic: 3.59 us -> 0.27 us  [the longest x2 0.17 us: body(): jnp.concatenate(st[k], axis=0)]
    unnamed x89 -> x84, local copies, waits for them, and re-layouts: 15.5 us -> 18.4 us
    pallas_call x16 -> x21, Pallas kernels: 76.3 us -> 76.6 us  [call(): pl.pallas_call(kernel, in_specs=[SMEM] * len(smem) + [VMEM] * len(vmem),...]
  transfers between devices with their start and end apart: 42 -> 42, of which waited for: 19 -> 18; matrix products, arithmetic and copies ran while one was open for 11% -> 9% of each run, Pallas kernels for 32% -> 34%
where the time goes in v4:
time: 267 us
  Pallas kernels  93.8 us (35%)
  waiting for transfers between devices  87.2 us (33%)
  starting transfers between devices  44.5 us (17%)
  local copies, waits for them, and re-layouts  29 us (11%)
  other arithmetic  6.37 us (2%)
  matrix products  3.54 us (1%)
    ppermute x42, waiting for transfers between devices, swap(): return lax.ppermute(value, ('req', 'tp'), pairs)  87.2 us
    pallas_call x21, Pallas kernels, call(): pl.pallas_call(kernel, in_specs=[SMEM] * len(smem) + [VMEM] * len(vmem),...  76.6 us
    ppermute x42, starting transfers between devices, swap(): return lax.ppermute(value, ('req', 'tp'), pairs)  44.5 us
    unnamed x84, local copies, waits for them, and re-layouts  18.4 us
    pallas_call x6, Pallas kernels, on_device(): pl.pallas_call(run, in_specs=[pl.BlockSpec(memory_space=pltpu.SMEM)] + [p...  17.2 us
  transfers between devices with their start and end apart: 42, of which 18 were waited for; matrix products, arithmetic and copies ran while one was open for 9% of the time, Pallas kernels for 34%

profile of v4, /device:TPU:0, one launch (start us, length us, event | category | flops | bytes accessed | tf_op | source)
XLA Modules:
  0.0 266.6 jit_solution(9157402379833803026)
XLA Ops:
  1.3 2.5 split_qkv.1
  4.3 2.6 collective-permute-start.1
  7.0 4.3 %split_gateup.1 = (bf16[2,2,80,1728]{3,2,1,0:T(8,128)(2,1)}, bf16[2,2,80,1728]{3,2,1,0:T(8,128)(2,1)}) custom-call(s32[2]{0:T(128)} %pad_add_fusion.place_ref, f32[80,13824]{1,0:T(8,128)} %refs_0_.2), custom_call_target="tpu_custom_call" | custom-call | flops 1 | bytes 1 | tf_op jit(solution)/shard_map/split_gateup/pallas_call | solution.py:40
  12.4 2.9 %collective-permute-done.2.refs_3_ = bf16[80,960]{1,0:T(8,128)(2,1)} collective-permute-done((bf16[80,960]{1,0:T(8,128)(2,1)}, bf16[80,960]{1,0:T(8,128)(2,1)}, u32[]{:S(2)}, u32[]{:S(2)}) %collective-permute-start.2) | collective-permute-done | bytes 153632 | tf_op jit(solution)/shard_map/ppermute | solution.py:454
  15.7 2.1 join_qkv.1
  17.8 1.8 collective-permute-start.5
  21.1 2.6 collective-permute-start.7
  24.4 2.7 %pack_far.1 = (bf16[1,2,2,80,1024]{4,3,2,1,0:T(8,128)(2,1)}, bf16[1,2,2,80,704]{4,3,2,1,0:T(8,128)(2,1)}) custom-call(s32[2]{0:T(128)} %pad_add_fusion.place_ref, bf16[2,2,80,1728]{3,2,1,0:T(8,128)(2,1)} %get-tuple-element.213.refs_0_, bf16[2,2,80,1728]{3,2,1,0:T(8,128)(2,1)} %collective-permute-done.3.refs_1_), custom_call_target="tpu_custom_call" | custom-call | flops 1 | bytes 1 | tf_op jit(solution)/shard_map/pack_far/pallas_call | solution.py:40
  29.7 11.8 %permute_columns.3 = (f32[512,2560]{1,0:T(8,128)}, bf16[512,2560]{1,0:T(8,128)(2,1)S(1)}) custom-call(bf16[512,2560]{1,0:T(8,128)(2,1)S(1)} %copy-done.4, s32[1,2560]{1,0:T(1,128)S(1)} %add.144.at_ref, f32[1,2560]{1,0:T(1,128)S(1)} %broadcast_in_dim_reshape.2.refs_0_), custom_call_target="tpu_custom_call" | custom-call | flops 1 | bytes 1 | tf_op jit(solution)/shard_map/permute_columns/pallas_call | solution.py:146
  43.5 2.9 %join_gateup.2 = (bf16[4,80,1024]{2,1,0:T(8,128)(2,1)}, bf16[4,80,1024]{2,1,0:T(8,128)(2,1)}) custom-call(s32[2]{0:T(128)} %pad_add_fusion.place_ref, bf16[2,2,80,1728]{3,2,1,0:T(8,128)(2,1)} %get-tuple-element.213.refs_0_, bf16[2,2,80,1728]{3,2,1,0:T(8,128)(2,1)} %collective-permute-done.3.refs_1_, bf16[1,2,2,80,1024]{4,3,2,1,0:T(8,128)(2,1)} %bitcast.3.refs_2_), custom_call_target="tpu_custom_call" | custom-call | flops 1 | bytes 1 | tf_op jit(solution)/shard_map/join_gateup/pallas_call | solution.py:40
  46.5 3.9 %collective-permute-done.6 = bf16[320,960]{1,0:T(8,128)(2,1)} collective-permute-done((bf16[320,960]{1,0:T(8,128)(2,1)}, bf16[320,960]{1,0:T(8,128)(2,1)}, u32[]{:S(2)}, u32[]{:S(2)}) %collective-permute-start.6) | collective-permute-done | bytes 614432 | tf_op jit(solution)/shard_map/ppermute | solution.py:454
  50.4 2.4 collective-permute-done.7
  56.7 2.6 collective-permute-start.9
  61.4 6.2 %class_rows.1 = (bf16[864,2560]{1,0:T(8,128)(2,1)S(1)}, bf16[864,2560]{1,0:T(8,128)(2,1)}) custom-call(s32[2]{0:T(128)S(1)} %copy-done.23, bf16[1728,2560]{1,0:T(8,128)(2,1)} %weight_ref), custom_call_target="tpu_custom_call" | custom-call | flops 1 | bytes 1 | tf_op jit(solution)/shard_map/class_rows/pallas_call | solution.py:146
  67.6 2.2 copy-done.2
  69.8 12.1 %permute_columns.4.out_in_ref = bf16[640,2560]{1,0:T(8,128)(2,1)S(1)} custom-call(bf16[640,2560]{1,0:T(8,128)(2,1)} %values_ref.1, s32[1,2560]{1,0:T(1,128)S(1)} %broadcast_in_dim.8.at_ref), custom_call_target="tpu_custom_call" | custom-call | flops 1 | bytes 1 | tf_op jit(solution)/shard_map/permute_columns/pallas_call | solution.py:146
  81.9 1.7 copy-done.3
  85.8 2.8 %join_gateup.3 = (bf16[4,80,704]{2,1,0:T(8,128)(2,1)}, bf16[4,80,704]{2,1,0:T(8,128)(2,1)}) custom-call(s32[2]{0:T(128)} %pad_add_fusion.place_ref, bf16[2,2,80,1728]{3,2,1,0:T(8,128)(2,1)} %get-tuple-element.213.refs_0_, bf16[2,2,80,1728]{3,2,1,0:T(8,128)(2,1)} %collective-permute-done.3.refs_1_, bf16[1,2,2,80,704]{4,3,2,1,0:T(8,128)(2,1)} %bitcast.11.refs_2_), custom_call_target="tpu_custom_call" | custom-call | flops 1 | bytes 1 | tf_op jit(solution)/shard_map/join_gateup/pallas_call | solution.py:40
  89.6 1.7 collective-permute-start.13
  98.6 3.5 %fusion = f32[512,960]{0,1:T(8,128)} fusion(bf16[1920,960]{1,0:T(8,128)(2,1)S(1)} %constant_dynamic-update-slice_fusion, bf16[512,2560]{1,0:T(8,128)(2,1)S(1)} %copy-done.22), kind=kOutput, calls=%fused_computation.3 | convolution fusion | flops 1887436800 | bytes 7864320 | tf_op jit(solution)/shard_map/dot_general | solution.py:26
  103.9 5.4 %collective-permute-done.15.refs_4_ = bf16[320,704]{1,0:T(8,128)(2,1)} collective-permute-done((bf16[320,704]{1,0:T(8,128)(2,1)}, bf16[320,704]{1,0:T(8,128)(2,1)}, u32[]{:S(2)}, u32[]{:S(2)}) %collective-permute-start.15) | collective-permute-done | bytes 450592 | tf_op jit(solution)/shard_map/ppermute | solution.py:454
  109.3 2.1 collective-permute-done.16.refs_1_
  115.2 1.8 collective-permute-start.19
  118.3 2.9 %copy.19.joined_ref = f32[512,960]{1,0:T(8,128)} copy(f32[512,960]{0,1:T(8,128)} %fusion) | data formatting | bytes 3932160 | tf_op jit(solution)/shard_map/optimization_barrier | solution.py:460
  123.5 16.2 %attend.1 = (bf16[256,2560]{1,0:T(8,128)(2,1)}, f32[256,2560]{1,0:T(8,128)}, bf16[512,320]{1,0:T(8,128)(2,1)S(1)}, bf16[512,320]{1,0:T(8,128)(2,1)}) custom-call(s32[2]{0:T(128)S(1)} %copy-done.24, s32[1]{0:T(128)} %copy.31.length_ref, s32[8]{0:T(128)S(1)} %get-tuple-element.234.chosen_ref, f32[512,960]{1,0:T(8,128)} %copy.19.joined_ref, ...), custom_call_target="tpu_custom_call" | custom-call | flops 1 | bytes 1 | tf_op jit(solution)/shard_map/attend/pallas_call | solution.py:146
  140.4 2.1 collective-permute-done.19.refs_6_
  145.3 2.5 collective-permute-start.21
  148.0 1.7 copy-done.5
  152.4 11.7 %collective-permute-done.21.refs_1_ = bf16[512,320]{1,0:T(8,128)(2,1)} collective-permute-done((bf16[512,320]{1,0:T(8,128)(2,1)}, bf16[512,320]{1,0:T(8,128)(2,1)}, u32[]{:S(2)}, u32[]{:S(2)}) %collective-permute-start.21) | collective-permute-done | bytes 327712 | tf_op jit(solution)/shard_map/ppermute | solution.py:454
  164.2 6.3 %collective-permute-done.23.refs_3_.refs_5_ = bf16[320,704]{1,0:T(8,128)(2,1)} collective-permute-done((bf16[320,704]{1,0:T(8,128)(2,1)}, bf16[320,704]{1,0:T(8,128)(2,1)}, u32[]{:S(2)}, u32[]{:S(2)}) %collective-permute-start.23) | collective-permute-done | bytes 450592 | tf_op jit(solution)/shard_map/ppermute | solution.py:454
  171.9 2.0 collective-permute-start.31
  177.7 5.1 %permute_columns.5 = f32[256,2560]{1,0:T(8,128)S(1)} custom-call(bf16[256,2560]{1,0:T(8,128)(2,1)S(1)} %pad_maximum_fusion.values_ref, s32[1,2560]{1,0:T(1,128)S(1)} %add.153.at_ref), custom_call_target="tpu_custom_call" | custom-call | flops 1 | bytes 1 | tf_op jit(solution)/shard_map/permute_columns/pallas_call | solution.py:146
  184.0 16.6 %collective-permute-done.28.refs_3_ = bf16[320,704]{1,0:T(8,128)(2,1)S(1)} collective-permute-done((bf16[320,704]{1,0:T(8,128)(2,1)}, bf16[320,704]{1,0:T(8,128)(2,1)S(1)}, u32[]{:S(2)}, u32[]{:S(2)}) %collective-permute-start.28) | collective-permute-done | bytes 450592 | tf_op jit(solution)/shard_map/ppermute | solution.py:454
  200.6 4.4 %collective-permute-done.29 = bf16[128,2560]{1,0:T(8,128)(2,1)S(1)} collective-permute-done((bf16[128,2560]{1,0:T(8,128)(2,1)S(1)}, bf16[128,2560]{1,0:T(8,128)(2,1)S(1)}, u32[]{:S(2)}, u32[]{:S(2)}) %collective-permute-start.29) | collective-permute-done | bytes 655392 | tf_op jit(solution)/shard_map/ppermute | solution.py:454
  206.5 2.0 assemble.2.weight_ref
  210.4 2.9 %gated.5 = (bf16[256,512]{1,0:T(8,128)(2,1)S(1)}, bf16[256,512]{1,0:T(8,128)(2,1)S(1)}) custom-call(bf16[512,2560]{1,0:T(8,128)(2,1)S(1)} %constant_dynamic-update-slice_fusion.9.tokens_ref, bf16[2560,1024]{1,0:T(8,128)(2,1)S(1)} %assemble.2.weight_ref), custom_call_target="tpu_custom_call" | custom-call | flops 1 | bytes 1 | tf_op jit(solution)/shard_map/gated/pallas_call | solution.py:146
  213.3 3.0 %gated.4.refs_0_ = bf16[512,512]{1,0:T(8,128)(2,1)S(1)} custom-call(bf16[512,2560]{1,0:T(8,128)(2,1)S(1)} %constant_dynamic-update-slice_fusion.6.tokens_ref, bf16[2560,1024]{1,0:T(8,128)(2,1)S(1)} %assemble.2.weight_ref), custom_call_target="tpu_custom_call" | custom-call | flops 1 | bytes 1 | tf_op jit(solution)/shard_map/gated/pallas_call | solution.py:146
  216.3 3.0 %collective-permute-done.32.refs_7_ = bf16[320,704]{1,0:T(8,128)(2,1)S(1)} collective-permute-done((bf16[320,704]{1,0:T(8,128)(2,1)}, bf16[320,704]{1,0:T(8,128)(2,1)S(1)}, u32[]{:S(2)}, u32[]{:S(2)}) %collective-permute-start.32) | collective-permute-done | bytes 450592 | tf_op jit(solution)/shard_map/ppermute | solution.py:454
  220.3 1.9 assemble.3.weight_ref
  222.2 2.6 gated.6
  224.9 1.7 collective-permute-start.35
  226.6 2.6 gated.7.refs_1_
  229.3 1.7 rows_product.8.refs_2_
  231.0 1.7 rows_product.6.refs_2_
  234.3 6.5 %collective-permute-done.38.refs_0_ = bf16[256,512]{1,0:T(8,128)(2,1)S(1)} collective-permute-done((bf16[256,512]{1,0:T(8,128)(2,1)S(1)}, bf16[256,512]{1,0:T(8,128)(2,1)S(1)}, u32[]{:S(2)}, u32[]{:S(2)}) %collective-permute-start.38) | collective-permute-done | bytes 262176 | tf_op jit(solution)/shard_map/ppermute | solution.py:454
  243.0 1.8 collective-permute-start.41
  246.2 1.6 collective-permute-start.40
  247.8 16.0 %collective-permute-done.41 = bf16[512,320]{1,0:T(8,128)(2,1)S(1)} collective-permute-done((bf16[512,320]{1,0:T(8,128)(2,1)S(1)}, bf16[512,320]{1,0:T(8,128)(2,1)S(1)}, u32[]{:S(2)}, u32[]{:S(2)}) %collective-permute-start.41) | collective-permute-done | bytes 327712 | tf_op jit(solution)/shard_map/ppermute | solution.py:454
  (206 shorter events, 59.5 us)
Async XLA Ops:
  0.6 23.1 %copy-start = (s32[32]{0:T(128)S(1)}, s32[32]{0:T(128)}, u32[]{:S(2)}) copy-start(s32[32]{0:T(128)} %param.15) | copy-start | bytes 388
  3.8 8.5 %collective-permute-start = (bf16[80,960]{1,0:T(8,128)(2,1)}, bf16[80,960]{1,0:T(8,128)(2,1)S(1)}, u32[]{:S(2)}, u32[]{:S(2)}) collective-permute-start(bf16[80,960]{1,0:T(8,128)(2,1)} %get-tuple-element.191), channel_id=1, source_target_pairs={{0,1},{1,0},{2,3},{3,2},{4,5},{5,4},{6,7},{7,6},{8,9},{9,8},{10,11... | collective-permute-start | bytes 460808 | tf_op jit(solution)/shard_map/ppermute | solution.py:454
  4.3 8.0 %collective-permute-start.1 = (bf16[80,960]{1,0:T(8,128)(2,1)}, bf16[80,960]{1,0:T(8,128)(2,1)S(1)}, u32[]{:S(2)}, u32[]{:S(2)}) collective-permute-start(bf16[80,960]{1,0:T(8,128)(2,1)} %get-tuple-element.192), channel_id=1, source_target_pairs={{0,2},{1,3},{2,0},{3,1},{4,6},{5,7},{6,4},{7,5},{8,10},{9,11},{10,... | collective-permute-start | bytes 460808 | tf_op jit(solution)/shard_map/ppermute | solution.py:454
  6.9 8.4 %collective-permute-start.2 = (bf16[80,960]{1,0:T(8,128)(2,1)}, bf16[80,960]{1,0:T(8,128)(2,1)}, u32[]{:S(2)}, u32[]{:S(2)}) collective-permute-start(bf16[80,960]{1,0:T(8,128)(2,1)} %get-tuple-element.193), channel_id=1, source_target_pairs={{0,3},{1,2},{2,1},{3,0},{4,7},{5,6},{6,5},{7,4},{8,11},{9,10},{10,... | collective-permute-start | bytes 460808 | tf_op jit(solution)/shard_map/ppermute | solution.py:454
  11.3 18.3 %copy-start.4 = (bf16[512,2560]{1,0:T(8,128)(2,1)S(1)}, bf16[512,2560]{1,0:T(8,128)(2,1)}, u32[]{:S(2)}) copy-start(bf16[512,2560]{1,0:T(8,128)(2,1)} %values_ref) | copy-start | bytes 7864324
  15.3 9.1 %collective-permute-start.3 = (bf16[2,2,80,1728]{3,2,1,0:T(8,128)(2,1)}, bf16[2,2,80,1728]{3,2,1,0:T(8,128)(2,1)}, u32[]{:S(2)}, u32[]{:S(2)}) collective-permute-start(bf16[2,2,80,1728]{3,2,1,0:T(8,128)(2,1)} %get-tuple-element.195), channel_id=1, source_target_pairs={{0,1},{1,0},{2,3},{3,2},{4,5},{5,4},{6,7},{7,6},{8,9},{9,8},{10,11... | collective-permute-start | bytes 3317768 | tf_op jit(solution)/shard_map/ppermute | solution.py:454
  17.8 28.7 %collective-permute-start.5 = (bf16[320,960]{1,0:T(8,128)(2,1)}, bf16[320,960]{1,0:T(8,128)(2,1)}, u32[]{:S(2)}, u32[]{:S(2)}) collective-permute-start(bf16[320,960]{1,0:T(8,128)(2,1)} %bitcast.30), channel_id=1, source_target_pairs={{0,4},{1,5},{2,6},{3,7},{4,0},{5,1},{6,2},{7,3},{8,12},{9,13},{10,... | collective-permute-start | bytes 1843208 | tf_op jit(solution)/shard_map/ppermute | solution.py:454
  19.6 30.8 %collective-permute-start.6 = (bf16[320,960]{1,0:T(8,128)(2,1)}, bf16[320,960]{1,0:T(8,128)(2,1)}, u32[]{:S(2)}, u32[]{:S(2)}) collective-permute-start(bf16[320,960]{1,0:T(8,128)(2,1)} %bitcast.31), channel_id=1, source_target_pairs={{0,8},{1,9},{2,10},{3,11},{4,12},{5,13},{6,14},{7,15},{8,0},{9,1},... | collective-permute-start | bytes 1843208 | tf_op jit(solution)/shard_map/ppermute | solution.py:454
  21.1 31.6 %collective-permute-start.7 = (bf16[320,960]{1,0:T(8,128)(2,1)}, bf16[320,960]{1,0:T(8,128)(2,1)}, u32[]{:S(2)}, u32[]{:S(2)}) collective-permute-start(bf16[320,960]{1,0:T(8,128)(2,1)} %bitcast.32), channel_id=1, source_target_pairs={{0,16},{1,17},{2,18},{3,19},{4,20},{5,21},{6,22},{7,23},{8,24},{9,... | collective-permute-start | bytes 1843208 | tf_op jit(solution)/shard_map/ppermute | solution.py:454
  27.1 16.4 %collective-permute-start.4 = (bf16[2,2,80,1024]{3,2,1,0:T(8,128)(2,1)}, bf16[2,2,80,1024]{3,2,1,0:T(8,128)(2,1)}, u32[]{:S(2)}, u32[]{:S(2)}) collective-permute-start(bf16[2,2,80,1024]{3,2,1,0:T(8,128)(2,1)} %bitcast.35), channel_id=1, source_target_pairs={{0,2},{1,3},{2,0},{3,1},{4,6},{5,7},{6,4},{7,5},{8,10},{9,11},{10,... | collective-permute-start | bytes 1966088 | tf_op jit(solution)/shard_map/ppermute | solution.py:454
  29.6 29.7 %copy-start.30 = (s32[32]{0:T(128)S(1)}, s32[32]{0:T(128)}, u32[]{:S(2)}) copy-start(s32[32]{0:T(128)} %param.14) | copy-start | bytes 388
  29.7 31.8 %copy-start.23 = (s32[2]{0:T(128)S(1)}, s32[2]{0:T(128)}, u32[]{:S(2)}) copy-start(s32[2]{0:T(128)} %pad_add_fusion.place_ref) | copy-start | bytes 28
  52.8 35.8 %collective-permute-start.11 = (bf16[320,960]{1,0:T(8,128)(2,1)}, bf16[320,960]{1,0:T(8,128)(2,1)}, u32[]{:S(2)}, u32[]{:S(2)}) collective-permute-start(bf16[320,960]{1,0:T(8,128)(2,1)} %collective-permute-done.7), channel_id=1, source_target_pairs={{0,4},{1,5},{2,6},{3,7},{4,0},{5,1},{6,2},{7,3},{8,12},{9,13},{10,... | collective-permute-start | bytes 1843208 | tf_op jit(solution)/shard_map/ppermute | solution.py:454
  53.3 35.3 %collective-permute-start.12 = (bf16[320,960]{1,0:T(8,128)(2,1)}, bf16[320,960]{1,0:T(8,128)(2,1)}, u32[]{:S(2)}, u32[]{:S(2)}) collective-permute-start(bf16[320,960]{1,0:T(8,128)(2,1)} %collective-permute-done.7), channel_id=1, source_target_pairs={{0,8},{1,9},{2,10},{3,11},{4,12},{5,13},{6,14},{7,15},{8,0},{9,1},... | collective-permute-start | bytes 1843208 | tf_op jit(solution)/shard_map/ppermute | solution.py:454
  53.7 32.1 %collective-permute-start.8 = (bf16[2,2,80,704]{3,2,1,0:T(8,128)(2,1)}, bf16[2,2,80,704]{3,2,1,0:T(8,128)(2,1)}, u32[]{:S(2)}, u32[]{:S(2)}) collective-permute-start(bf16[2,2,80,704]{3,2,1,0:T(8,128)(2,1)} %bitcast.10), channel_id=1, source_target_pairs={{0,2},{1,3},{2,0},{3,1},{4,6},{5,7},{6,4},{7,5},{8,10},{9,11},{10,... | collective-permute-start | bytes 1351688 | tf_op jit(solution)/shard_map/ppermute | solution.py:454
  55.3 33.4 %collective-permute-start.10 = (bf16[320,960]{1,0:T(8,128)(2,1)}, bf16[320,960]{1,0:T(8,128)(2,1)}, u32[]{:S(2)}, u32[]{:S(2)}) collective-permute-start(bf16[320,960]{1,0:T(8,128)(2,1)} %collective-permute-done.6), channel_id=1, source_target_pairs={{0,4},{1,5},{2,6},{3,7},{4,0},{5,1},{6,2},{7,3},{8,12},{9,13},{10,... | collective-permute-start | bytes 1843208 | tf_op jit(solution)/shard_map/ppermute | solution.py:454
  56.7 31.9 %collective-permute-start.9 = (bf16[320,1024]{1,0:T(8,128)(2,1)}, bf16[320,1024]{1,0:T(8,128)(2,1)S(1)}, u32[]{:S(2)}, u32[]{:S(2)}) collective-permute-start(bf16[320,1024]{1,0:T(8,128)(2,1)} %bitcast.24), channel_id=1, source_target_pairs={{0,16},{1,17},{2,18},{3,19},{4,20},{5,21},{6,22},{7,23},{8,24},{9,... | collective-permute-start | bytes 1966088 | tf_op jit(solution)/shard_map/ppermute | solution.py:454
  88.6 26.0 %copy-start.10 = (bf16[320,1024]{1,0:T(8,128)(2,1)}, bf16[320,1024]{1,0:T(8,128)(2,1)S(1)}, u32[]{:S(2)}) copy-start(bf16[320,1024]{1,0:T(8,128)(2,1)S(1)} %collective-permute-done.9.refs_4_) | copy-start | bytes 1966084
  88.7 14.4 %collective-permute-start.14 = (bf16[320,704]{1,0:T(8,128)(2,1)}, bf16[320,704]{1,0:T(8,128)(2,1)S(1)}, u32[]{:S(2)}, u32[]{:S(2)}) collective-permute-start(bf16[320,704]{1,0:T(8,128)(2,1)} %bitcast.27), channel_id=1, source_target_pairs={{0,4},{1,5},{2,6},{3,7},{4,0},{5,1},{6,2},{7,3},{8,12},{9,13},{10,... | collective-permute-start | bytes 1351688 | tf_op jit(solution)/shard_map/ppermute | solution.py:454
  89.3 20.1 %collective-permute-start.15 = (bf16[320,704]{1,0:T(8,128)(2,1)}, bf16[320,704]{1,0:T(8,128)(2,1)}, u32[]{:S(2)}, u32[]{:S(2)}) collective-permute-start(bf16[320,704]{1,0:T(8,128)(2,1)} %bitcast.28), channel_id=1, source_target_pairs={{0,16},{1,17},{2,18},{3,19},{4,20},{5,21},{6,22},{7,23},{8,24},{9,... | collective-permute-start | bytes 1351688 | tf_op jit(solution)/shard_map/ppermute | solution.py:454
  89.6 23.5 %collective-permute-start.13 = (bf16[320,1024]{1,0:T(8,128)(2,1)}, bf16[320,1024]{1,0:T(8,128)(2,1)}, u32[]{:S(2)}, u32[]{:S(2)}) collective-permute-start(bf16[320,1024]{1,0:T(8,128)(2,1)} %bitcast.34), channel_id=1, source_target_pairs={{0,8},{1,9},{2,10},{3,11},{4,12},{5,13},{6,14},{7,15},{8,0},{9,1},... | collective-permute-start | bytes 1966088 | tf_op jit(solution)/shard_map/ppermute | solution.py:454
  91.3 20.1 %collective-permute-start.16 = (bf16[320,960]{1,0:T(8,128)(2,1)}, bf16[320,960]{1,0:T(8,128)(2,1)S(1)}, u32[]{:S(2)}, u32[]{:S(2)}) collective-permute-start(bf16[320,960]{1,0:T(8,128)(2,1)} %collective-permute-done.12.refs_0_), channel_id=1, source_target_pairs={{0,4},{1,5},{2,6},{3,7},{4,0},{5,1},{6,2},{7,3},{8,12},{9,13},{10,... | collective-permute-start | bytes 1843208 | tf_op jit(solution)/shard_map/ppermute | solution.py:454
  113.1 27.3 %collective-permute-start.17 = (bf16[320,1024]{1,0:T(8,128)(2,1)S(1)}, bf16[320,1024]{1,0:T(8,128)(2,1)}, u32[]{:S(2)}, u32[]{:S(2)}) collective-permute-start(bf16[320,1024]{1,0:T(8,128)(2,1)S(1)} %bitcast.25), channel_id=1, source_target_pairs={{0,4},{1,5},{2,6},{3,7},{4,0},{5,1},{6,2},{7,3},{8,12},{9,13},{10,... | collective-permute-start | bytes 1966088 | tf_op jit(solution)/shard_map/ppermute | solution.py:454
  114.6 25.8 %collective-permute-start.18 = (bf16[320,1024]{1,0:T(8,128)(2,1)S(1)}, bf16[320,1024]{1,0:T(8,128)(2,1)}, u32[]{:S(2)}, u32[]{:S(2)}) collective-permute-start(bf16[320,1024]{1,0:T(8,128)(2,1)S(1)} %collective-permute-done.9.refs_4_), channel_id=1, source_target_pairs={{0,4},{1,5},{2,6},{3,7},{4,0},{5,1},{6,2},{7,3},{8,12},{9,13},{10,... | collective-permute-start | bytes 1966088 | tf_op jit(solution)/shard_map/ppermute | solution.py:454
  115.2 27.3 %collective-permute-start.19 = (bf16[320,1024]{1,0:T(8,128)(2,1)}, bf16[320,1024]{1,0:T(8,128)(2,1)}, u32[]{:S(2)}, u32[]{:S(2)}) collective-permute-start(bf16[320,1024]{1,0:T(8,128)(2,1)} %collective-permute-done.13.refs_2_), channel_id=1, source_target_pairs={{0,16},{1,17},{2,18},{3,19},{4,20},{5,21},{6,22},{7,23},{8,24},{9,... | collective-permute-start | bytes 1966088 | tf_op jit(solution)/shard_map/ppermute | solution.py:454
  117.0 23.5 %collective-permute-start.20 = (bf16[320,704]{1,0:T(8,128)(2,1)}, bf16[320,704]{1,0:T(8,128)(2,1)}, u32[]{:S(2)}, u32[]{:S(2)}) collective-permute-start(bf16[320,704]{1,0:T(8,128)(2,1)} %bitcast.13), channel_id=1, source_target_pairs={{0,8},{1,9},{2,10},{3,11},{4,12},{5,13},{6,14},{7,15},{8,0},{9,1},... | collective-permute-start | bytes 1351688 | tf_op jit(solution)/shard_map/ppermute | solution.py:454
  142.5 5.5 %collective-permute-start.25 = (bf16[256,2560]{1,0:T(8,128)(2,1)}, bf16[256,2560]{1,0:T(8,128)(2,1)S(1)}, u32[]{:S(2)}, u32[]{:S(2)}) collective-permute-start(bf16[256,2560]{1,0:T(8,128)(2,1)} %get-tuple-element.279), channel_id=1, source_target_pairs={{0,1},{1,0},{2,3},{3,2},{4,5},{5,4},{6,7},{7,6},{8,9},{9,8},{10,11... | collective-permute-start | bytes 3932168 | tf_op jit(solution)/shard_map/ppermute | solution.py:454
  142.5 28.0 %collective-permute-start.22 = (bf16[320,1024]{1,0:T(8,128)(2,1)}, bf16[320,1024]{1,0:T(8,128)(2,1)S(1)}, u32[]{:S(2)}, u32[]{:S(2)}) collective-permute-start(bf16[320,1024]{1,0:T(8,128)(2,1)} %collective-permute-done.13.refs_2_), channel_id=1, source_target_pairs={{0,4},{1,5},{2,6},{3,7},{4,0},{5,1},{6,2},{7,3},{8,12},{9,13},{10,... | collective-permute-start | bytes 1966088 | tf_op jit(solution)/shard_map/ppermute | solution.py:454
  143.9 26.6 %collective-permute-start.23 = (bf16[320,704]{1,0:T(8,128)(2,1)}, bf16[320,704]{1,0:T(8,128)(2,1)}, u32[]{:S(2)}, u32[]{:S(2)}) collective-permute-start(bf16[320,704]{1,0:T(8,128)(2,1)} %collective-permute-done.15.refs_4_), channel_id=1, source_target_pairs={{0,4},{1,5},{2,6},{3,7},{4,0},{5,1},{6,2},{7,3},{8,12},{9,13},{10,... | collective-permute-start | bytes 1351688 | tf_op jit(solution)/shard_map/ppermute | solution.py:454
  144.5 26.0 %collective-permute-start.24 = (bf16[320,704]{1,0:T(8,128)(2,1)}, bf16[320,704]{1,0:T(8,128)(2,1)}, u32[]{:S(2)}, u32[]{:S(2)}) collective-permute-start(bf16[320,704]{1,0:T(8,128)(2,1)} %collective-permute-done.20.refs_2_), channel_id=1, source_target_pairs={{0,16},{1,17},{2,18},{3,19},{4,20},{5,21},{6,22},{7,23},{8,24},{9,... | collective-permute-start | bytes 1351688 | tf_op jit(solution)/shard_map/ppermute | solution.py:454
  145.3 18.8 %collective-permute-start.21 = (bf16[512,320]{1,0:T(8,128)(2,1)}, bf16[512,320]{1,0:T(8,128)(2,1)}, u32[]{:S(2)}, u32[]{:S(2)}) collective-permute-start(bf16[512,320]{1,0:T(8,128)(2,1)} %get-tuple-element.267), channel_id=1, source_target_pairs={{0,8},{1,9},{2,10},{3,11},{4,12},{5,13},{6,14},{7,15},{8,0},{9,1},... | collective-permute-start | bytes 983048 | tf_op jit(solution)/shard_map/ppermute | solution.py:454
  151.9 19.4 %copy-start.7 = (f32[128,2560]{1,0:T(8,128)S(1)}, f32[128,2560]{1,0:T(8,128)}, u32[]{:S(2)}) copy-start(f32[128,2560]{1,0:T(8,128)} %copy-done.6) | copy-start | bytes 3932164
  151.9 19.4 %collective-permute-start.26 = (bf16[128,2560]{1,0:T(8,128)(2,1)}, bf16[128,2560]{1,0:T(8,128)(2,1)S(1)}, u32[]{:S(2)}, u32[]{:S(2)}) collective-permute-start(bf16[128,2560]{1,0:T(8,128)(2,1)} %get-tuple-element.282), channel_id=1, source_target_pairs={{0,2},{1,3},{2,0},{3,1},{4,6},{5,7},{6,4},{7,5},{8,10},{9,11},{10,... | collective-permute-start | bytes 1966088 | tf_op jit(solution)/shard_map/ppermute | solution.py:454
  171.8 33.2 %collective-permute-start.30 = (bf16[128,2560]{1,0:T(8,128)(2,1)S(1)}, bf16[128,2560]{1,0:T(8,128)(2,1)S(1)}, u32[]{:S(2)}, u32[]{:S(2)}) collective-permute-start(bf16[128,2560]{1,0:T(8,128)(2,1)S(1)} %get-tuple-element.305), channel_id=1, source_target_pairs={{0,8},{1,9},{2,10},{3,11},{4,12},{5,13},{6,14},{7,15},{8,0},{9,1},... | collective-permute-start | bytes 1966088 | tf_op jit(solution)/shard_map/ppermute | solution.py:454
  171.9 33.1 %collective-permute-start.31 = (bf16[128,2560]{1,0:T(8,128)(2,1)S(1)}, bf16[128,2560]{1,0:T(8,128)(2,1)S(1)}, u32[]{:S(2)}, u32[]{:S(2)}) collective-permute-start(bf16[128,2560]{1,0:T(8,128)(2,1)S(1)} %get-tuple-element.305), channel_id=1, source_target_pairs={{0,10},{1,11},{2,8},{3,9},{4,14},{5,15},{6,12},{7,13},{8,2},{9,3},... | collective-permute-start | bytes 1966088 | tf_op jit(solution)/shard_map/ppermute | solution.py:454
  174.0 26.6 %collective-permute-start.27 = (bf16[320,1024]{1,0:T(8,128)(2,1)}, bf16[320,1024]{1,0:T(8,128)(2,1)S(1)}, u32[]{:S(2)}, u32[]{:S(2)}) collective-permute-start(bf16[320,1024]{1,0:T(8,128)(2,1)} %collective-permute-done.19.refs_6_), channel_id=1, source_target_pairs={{0,4},{1,5},{2,6},{3,7},{4,0},{5,1},{6,2},{7,3},{8,12},{9,13},{10,... | collective-permute-start | bytes 1966088 | tf_op jit(solution)/shard_map/ppermute | solution.py:454
  175.5 29.6 %collective-permute-start.29 = (bf16[128,2560]{1,0:T(8,128)(2,1)S(1)}, bf16[128,2560]{1,0:T(8,128)(2,1)S(1)}, u32[]{:S(2)}, u32[]{:S(2)}) collective-permute-start(bf16[128,2560]{1,0:T(8,128)(2,1)S(1)} %get-tuple-element.316), channel_id=1, source_target_pairs={{0,2},{1,3},{2,0},{3,1},{4,6},{5,7},{6,4},{7,5},{8,10},{9,11},{10,... | collective-permute-start | bytes 1966088 | tf_op jit(solution)/shard_map/ppermute | solution.py:454
  177.0 23.6 %collective-permute-start.28 = (bf16[320,704]{1,0:T(8,128)(2,1)}, bf16[320,704]{1,0:T(8,128)(2,1)S(1)}, u32[]{:S(2)}, u32[]{:S(2)}) collective-permute-start(bf16[320,704]{1,0:T(8,128)(2,1)} %collective-permute-done.20.refs_2_), channel_id=1, source_target_pairs={{0,4},{1,5},{2,6},{3,7},{4,0},{5,1},{6,2},{7,3},{8,12},{9,13},{10,... | collective-permute-start | bytes 1351688 | tf_op jit(solution)/shard_map/ppermute | solution.py:454
  205.2 3.6 %collective-permute-start.34 = (bf16[256,2560]{1,0:T(8,128)(2,1)S(1)}, bf16[256,2560]{1,0:T(8,128)(2,1)S(1)}, u32[]{:S(2)}, u32[]{:S(2)}) collective-permute-start(bf16[256,2560]{1,0:T(8,128)(2,1)S(1)} %pad_maximum_fusion.2), channel_id=1, source_target_pairs={{0,1},{1,0},{2,3},{3,2},{4,5},{5,4},{6,7},{7,6},{8,9},{9,8},{10,11... | collective-permute-start | bytes 3932168 | tf_op jit(solution)/shard_map/ppermute | solution.py:454
  205.3 4.8 %collective-permute-start.33 = (bf16[256,2560]{1,0:T(8,128)(2,1)S(1)}, bf16[256,2560]{1,0:T(8,128)(2,1)S(1)}, u32[]{:S(2)}, u32[]{:S(2)}) collective-permute-start(bf16[256,2560]{1,0:T(8,128)(2,1)S(1)} %pad_maximum_fusion.1), channel_id=1, source_target_pairs={{0,1},{1,0},{2,3},{3,2},{4,5},{5,4},{6,7},{7,6},{8,9},{9,8},{10,11... | collective-permute-start | bytes 3932168 | tf_op jit(solution)/shard_map/ppermute | solution.py:454
  205.9 13.4 %collective-permute-start.32 = (bf16[320,704]{1,0:T(8,128)(2,1)}, bf16[320,704]{1,0:T(8,128)(2,1)S(1)}, u32[]{:S(2)}, u32[]{:S(2)}) collective-permute-start(bf16[320,704]{1,0:T(8,128)(2,1)} %hold.1.refs_6_), channel_id=1, source_target_pairs={{0,4},{1,5},{2,6},{3,7},{4,0},{5,1},{6,2},{7,3},{8,12},{9,13},{10,... | collective-permute-start | bytes 1351688 | tf_op jit(solution)/shard_map/ppermute | solution.py:454
  219.3 13.4 %collective-permute-start.37 = (bf16[256,512]{1,0:T(8,128)(2,1)S(1)}, bf16[256,512]{1,0:T(8,128)(2,1)S(1)}, u32[]{:S(2)}, u32[]{:S(2)}) collective-permute-start(bf16[256,512]{1,0:T(8,128)(2,1)S(1)} %get-tuple-element.345), channel_id=1, source_target_pairs={{0,8},{1,9},{2,10},{3,11},{4,12},{5,13},{6,14},{7,15},{8,0},{9,1},... | collective-permute-start | bytes 786440 | tf_op jit(solution)/shard_map/ppermute | solution.py:454
  219.7 14.5 %collective-permute-start.36 = (bf16[512,320]{1,0:T(8,128)(2,1)S(1)}, bf16[512,320]{1,0:T(8,128)(2,1)S(1)}, u32[]{:S(2)}, u32[]{:S(2)}) collective-permute-start(bf16[512,320]{1,0:T(8,128)(2,1)S(1)} %pad_maximum_fusion.3), channel_id=1, source_target_pairs={{0,4},{1,5},{2,6},{3,7},{4,0},{5,1},{6,2},{7,3},{8,12},{9,13},{10,... | collective-permute-start | bytes 983048 | tf_op jit(solution)/shard_map/ppermute | solution.py:454
  224.9 17.0 %collective-permute-start.35 = (bf16[512,352]{1,0:T(8,128)(2,1)S(1)}, bf16[512,352]{1,0:T(8,128)(2,1)S(1)}, u32[]{:S(2)}, u32[]{:S(2)}) collective-permute-start(bf16[512,352]{1,0:T(8,128)(2,1)S(1)} %gated.6), channel_id=1, source_target_pairs={{0,8},{1,9},{2,10},{3,11},{4,12},{5,13},{6,14},{7,15},{8,0},{9,1},... | collective-permute-start | bytes 1081352 | tf_op jit(solution)/shard_map/ppermute | solution.py:454
  232.7 8.1 %collective-permute-start.38 = (bf16[256,512]{1,0:T(8,128)(2,1)S(1)}, bf16[256,512]{1,0:T(8,128)(2,1)S(1)}, u32[]{:S(2)}, u32[]{:S(2)}) collective-permute-start(bf16[256,512]{1,0:T(8,128)(2,1)S(1)} %get-tuple-element.351), channel_id=1, source_target_pairs={{0,8},{1,9},{2,10},{3,11},{4,12},{5,13},{6,14},{7,15},{8,0},{9,1},... | collective-permute-start | bytes 786440 | tf_op jit(solution)/shard_map/ppermute | solution.py:454
  242.9 3.1 %collective-permute-start.39 = (bf16[256,2560]{1,0:T(8,128)(2,1)S(1)}, bf16[256,2560]{1,0:T(8,128)(2,1)S(1)}, u32[]{:S(2)}, u32[]{:S(2)}) collective-permute-start(bf16[256,2560]{1,0:T(8,128)(2,1)S(1)} %rows_product.11), channel_id=1, source_target_pairs={{0,1},{1,0},{2,3},{3,2},{4,5},{5,4},{6,7},{7,6},{8,9},{9,8},{10,11... | collective-permute-start | bytes 3932168 | tf_op jit(solution)/shard_map/ppermute | solution.py:454
  243.0 20.9 %collective-permute-start.41 = (bf16[512,320]{1,0:T(8,128)(2,1)S(1)}, bf16[512,320]{1,0:T(8,128)(2,1)S(1)}, u32[]{:S(2)}, u32[]{:S(2)}) collective-permute-start(bf16[512,320]{1,0:T(8,128)(2,1)S(1)} %pad_maximum_fusion.4), channel_id=1, source_target_pairs={{0,16},{1,17},{2,18},{3,19},{4,20},{5,21},{6,22},{7,23},{8,24},{9,... | collective-permute-start | bytes 983048 | tf_op jit(solution)/shard_map/ppermute | solution.py:454
  246.2 19.4 %collective-permute-start.40 = (bf16[128,2560]{1,0:T(8,128)(2,1)S(1)}, bf16[128,2560]{1,0:T(8,128)(2,1)S(1)}, u32[]{:S(2)}, u32[]{:S(2)}) collective-permute-start(bf16[128,2560]{1,0:T(8,128)(2,1)S(1)} %get-tuple-element.357), channel_id=1, source_target_pairs={{0,2},{1,3},{2,0},{3,1},{4,6},{5,7},{6,4},{7,5},{8,10},{9,11},{10,... | collective-permute-start | bytes 1966088 | tf_op jit(solution)/shard_map/ppermute | solution.py:454
  (31 other events, 146.0 us)

commit v5 on v4

--- a/solution.py
+++ b/solution.py
@@ -239,7 +239,8 @@
             cache_ref[at, k_cols:] = (rows[:, q_cols + k_cols :] * live).astype(BF)
         for i in range(chosen.shape[0]):
             page = cache_ref[pl.ds(pl.multiple_of(chosen_ref[i] * PAGE, PAGE), PAGE), :]
-            boxes[i // slots][i % slots * PAGE : (i % slots + 1) * PAGE, :] = page
+            at, side = i % slots // 2 * PAGE, i % 2 * 2 * k_cols
+            boxes[i // slots][at : at + PAGE, side : side + 2 * k_cols] = page
         for k in range(kv_heads):
             key_at = q_cols + k * head_dim
             for t in range(seq_len // tile):
@@ -292,13 +293,13 @@
             ((seq_len // 2, model_dim), BF),
             ((seq_len // 2, model_dim), F32),
         ]
-        + [((slots * PAGE, 2 * k_cols), BF)] * 2,
+        + [((slots // 2 * PAGE, 4 * k_cols), BF)] * 2,
         [((seq_len, 2 * k_cols), BF), ((seq_len, wide), BF), ((seq_len, k_cols), BF), ((seq_len, q_cols), BF)],
         "attend",
     )
 
 
-def assemble(blocks):
+def assemble(blocks, flops=1):
     each, columns = blocks[0].shape
     count = len(blocks)
 
@@ -306,7 +307,8 @@
         for i in range(count):
             refs[count][i * each : (i + 1) * each, :] = refs[i][...]
 
-    return call(kernel, [], blocks, [((count * each, columns), BF)], [], "assemble", 24)[0]
+    shapes = [((count * each, columns), BF)]
+    return call(kernel, [], blocks, shapes, [], "assemble", 24, flops)[0]
 
 
 def rows_product(pieces, weight, at, count, base=None, dtype=F32):
@@ -372,19 +374,35 @@
     )
 
 
-def pick_pages(source, pages):
-    count = source.shape[0]
+def pack_pages(pairs):
+    width = pairs[0].shape[1] // 2
+
+    def kernel(*refs):
+        for j, ref in enumerate(refs[:-1]):
+            at, side = j // 2 * PAGE, j % 2 * width
+            refs[-1][at : at + PAGE, side : side + width] = ref[:, width:]
+
+    shapes = [((len(pairs) // 2 * PAGE, 2 * width), BF)]
+    return call(kernel, [], pairs, shapes, [], "pack_pages", 16)[0]
+
+
+def pick_pages(source, pairs, arrived, count):
+    width = arrived.shape[1] // 2
 
     def kernel(source_ref, *refs):
+        pages = [ref[:, :width] for ref in refs[: len(pairs)]]
+        for j in range(len(pairs)):
+            at, side = j // 2 * PAGE, j % 2 * width
+            pages.append(refs[len(pairs)][at : at + PAGE, side : side + width])
         for p in range(count):
-            for i, ref in enumerate(refs[:-1]):
+            for i, page in enumerate(pages):
 
                 @pl.when(source_ref[p] == i)
-                def _(p=p, ref=ref):
-                    refs[-1][p] = ref[...]
-
-    shapes = [((count, *pages[0].shape), BF)]
-    return call(kernel, [source], pages, shapes, [], "pick_pages", 16, 5 * 10**9)[0]
+                def _(p=p, page=page):
+                    refs[-1][p] = page
+
+    shapes = [((count, PAGE, width), BF)]
+    return call(kernel, [source], [*pairs, arrived], shapes, [], "pick_pages", 16, 5 * 10**9)[0]
 
 
 def class_rows(place, weight):
@@ -554,11 +572,11 @@
     columns_at, page_slot = st["onehot_at"], st["page_slot"]
     blocks = list(st["blocks"])
     blocks.append(join_gateup(place, st["gu_own"], st["gu_near"], over_y(far), 2 * chunks[0]))
+    gu = [dict() for _ in chunks]
+    spread_class(gu[0], *blocks[0], plain)
     spread_z(qkv, doubles)
     for r in singles[::-1]:
         qkv[r ^ 1] = swap(qkv[r], 1, 0)
-    gu = [dict() for _ in chunks]
-    spread_class(gu[0], *blocks[0], plain)
     out_in = permute_columns(st["out_proj"], columns_at, dtype=BF)
     down_rel = class_rows(place, st["down_proj"])
     ffn_gain_in = st["ffn_gain"].reshape(devices, rows_each)[blocks_at].reshape(-1)
@@ -679,49 +697,57 @@
     terms = permute_columns(jnp.concatenate([coarse, fine], axis=0), columns_back)
     st = sync(dict(gu=gu, own=own, theirs=theirs, terms=terms, box=page_parts(st["box"])))
 
-    def whole(rows):
-        for bit in bits[:-1]:
-            rows = jnp.concatenate([rows, swap(rows, 0, bit)], axis=0)
-        return rows
-
     gu, box = st["gu"], st["box"]
     resid = st["terms"][:share] + st["terms"][share:]
-    h_own, h_theirs = (whole(jnp.concatenate(st[k], axis=0)) for k in ("own", "theirs"))
+    own, theirs = (jnp.concatenate(st[k], axis=0) for k in ("own", "theirs"))
+    weight = assemble([gu[0][r] for r in range(n_req)])
+    hidden = gated(theirs, weight)[0]
+    returned = [swap(hidden, PAIR, 0)]
+    own_next, theirs_next = swap(own, 0, bits[0]), swap(theirs, 0, bits[0])
     for r in crossed:
         gu[1][r ^ 1] = swap(gu[1][r], 1, 0)
-    weight = assemble([gu[0][r] for r in range(n_req)])
-    theirs = gated(h_theirs, weight, 2)
-    kept = gated(h_own, weight)
-    st = sync(dict(gu=gu[1], h=(h_own, h_theirs), hidden=(kept, theirs), resid=resid, box=box))
+    hidden = gated(theirs_next, weight)[0]
+    h_own = jnp.concatenate([own, own_next], axis=0)
+    h_theirs = jnp.concatenate([theirs, theirs_next], axis=0)
+    weights = [weight, assemble([gu[1][r] for r in range(n_req)], 4 * 10**9)]
+    st = sync(
+        dict(
+            weights=weights,
+            h=(h_own, h_theirs),
+            hidden=(hidden, returned),
+            resid=resid,
+            box=box,
+        )
+    )
 
     resid, box = st["resid"], st["box"]
     h_own, h_theirs = st["h"]
-    kept, theirs = st["hidden"]
-    returned = [swap(theirs[0], PAIR, 0)]
-    second, _ = sync((theirs[1], returned[0]))
-    returned.append(swap(second, PAIR, 0))
-    weight = assemble([st["gu"][r] for r in range(n_req)])
-    theirs = gated(h_theirs, weight)
+    hidden, returned = st["hidden"]
+    returned = list(returned) + [swap(hidden, PAIR, 0)]
+    weights = st["weights"]
+    theirs = gated(h_theirs, weights[1])
     h_own, theirs = sync((h_own, theirs))
-    kept = list(kept) + list(gated(h_own, weight))
+    kept = [gated(h_own, weight)[0] for weight in weights]
     rows = seq_len // 2
     product = []
     for i in range(2):
         part = rows_product([(piece, i * rows) for piece in kept], down_rel[0], 0, rows)
         product.append(rows_product([(returned[i], 0)], down_rel[1], 0, rows, part))
-    box = page_parts(page_step(box, page_bits[1]))
-    returned, box, product = sync((swap(theirs[0], PAIR, 0), box, product))
+    for bit in page_bits[1:-1]:
+        box = page_step(box if bit == page_bits[1] else page_parts(box), bit)
+    leaving_pages = pack_pages(box)
+    returned, box, leaving_pages, product = sync(
+        (swap(theirs[0], PAIR, 0), box, leaving_pages, product)
+    )
     leaving = rows_product([(returned, rows)], down_rel[1], chunks[0], rows, product[1], BF)
     arrived = swap(leaving, 0, bits[0])
     staying = rows_product([(returned, 0)], down_rel[1], chunks[0], rows, product[0])
     keep, send = add_share(staying, arrived, resid)
-    box = page_step(box, page_bits[2])
-    for bit in page_bits[3:]:
-        box = page_step(page_parts(box), bit)
+    arrived_pages = swap(leaving_pages, page_bits[-1], 0)
     share_slots = tp * share + jnp.arange(share, dtype=jnp.int32)
     live_share = (share_slots < lengths[0]).astype(F32)
     layer_out = ((keep + swap(send, 0, bits[1]).astype(F32)) * live_share[:, None]).astype(BF)
-    kv_cache = pick_pages(source.astype(jnp.int32), box)
+    kv_cache = pick_pages(source.astype(jnp.int32), box, arrived_pages, n_pages)
     return (layer_out, kv_cache)
 
 

time: 267 us -> 260 us (0.974)
  waiting for transfers between devices: 87.2 us -> 79.4 us
    ppermute x42, waiting for transfers between devices: 87.2 us -> 79.4 us  [swap(): return lax.ppermute(value, ('req', 'tp'), pairs)]
    pallas_call x21 -> x23, Pallas kernels: 76.6 us -> 77.4 us  [call(): pl.pallas_call(kernel, in_specs=[SMEM] * len(smem) + [VMEM] * len(vmem),...]
    unnamed x84 -> x81, local copies, waits for them, and re-layouts: 18.4 us -> 18.3 us
  transfers between devices with their start and end apart: 42 -> 42, of which waited for: 18 -> 17; matrix products, arithmetic and copies ran while one was open for 9% -> 9% of each run, Pallas kernels for 34% -> 35%
where the time goes in v5:
time: 260 us; the launch traced here: 259 us
  Pallas kernels  94.6 us (36%)
  waiting for transfers between devices  79.4 us (31%)
  starting transfers between devices  44 us (17%)
  local copies, waits for them, and re-layouts  28.7 us (11%)
  other arithmetic  6.36 us (2%)
  matrix products  3.54 us (1%)
    ppermute x42, waiting for transfers between devices, swap(): return lax.ppermute(value, ('req', 'tp'), pairs)  79.4 us
    pallas_call x23, Pallas kernels, call(): pl.pallas_call(kernel, in_specs=[SMEM] * len(smem) + [VMEM] * len(vmem),...  77.4 us
    ppermute x42, starting transfers between devices, swap(): return lax.ppermute(value, ('req', 'tp'), pairs)  44 us
    unnamed x81, local copies, waits for them, and re-layouts  18.3 us
    pallas_call x6, Pallas kernels, on_device(): pl.pallas_call(run, in_specs=[pl.BlockSpec(memory_space=pltpu.SMEM)] + [p...  17.2 us
  transfers between devices with their start and end apart: 42, of which 17 were waited for; matrix products, arithmetic and copies ran while one was open for 9% of the time, Pallas kernels for 35%

profile of v5, /device:TPU:0, one launch (start us, length us, event | category | flops | bytes accessed | tf_op | source)
XLA Modules:
  0.0 258.9 jit_solution(5472853653365636006)
XLA Ops:
  1.3 2.5 split_qkv.1
  4.3 2.6 %collective-permute-start.1 = (bf16[80,960]{1,0:T(8,128)(2,1)}, bf16[80,960]{1,0:T(8,128)(2,1)S(1)}, u32[]{:S(2)}, u32[]{:S(2)}) collective-permute-start(bf16[80,960]{1,0:T(8,128)(2,1)} %get-tuple-element.182), channel_id=1, source_target_pairs={{0,2},{1,3},{2,0},{3,1},{4,6},{5,7},{6,4},{7,5},{8,10},{9,11},{10,... | collective-permute-start | bytes 460808 | tf_op jit(solution)/shard_map/ppermute | solution.py:472
  7.0 4.3 %split_gateup.1 = (bf16[2,2,80,1728]{3,2,1,0:T(8,128)(2,1)}, bf16[2,2,80,1728]{3,2,1,0:T(8,128)(2,1)}) custom-call(s32[2]{0:T(128)} %pad_add_fusion.place_ref, f32[80,13824]{1,0:T(8,128)} %refs_0_.2), custom_call_target="tpu_custom_call" | custom-call | flops 1 | bytes 1 | tf_op jit(solution)/shard_map/split_gateup/pallas_call | solution.py:40
  12.3 2.9 %collective-permute-done.2.refs_3_ = bf16[80,960]{1,0:T(8,128)(2,1)} collective-permute-done((bf16[80,960]{1,0:T(8,128)(2,1)}, bf16[80,960]{1,0:T(8,128)(2,1)}, u32[]{:S(2)}, u32[]{:S(2)}) %collective-permute-start.2) | collective-permute-done | bytes 153632 | tf_op jit(solution)/shard_map/ppermute | solution.py:472
  15.7 2.1 join_qkv.1
  17.7 1.8 collective-permute-start.5
  19.5 1.6 collective-permute-start.6
  21.1 2.6 %collective-permute-start.7 = (bf16[320,960]{1,0:T(8,128)(2,1)}, bf16[320,960]{1,0:T(8,128)(2,1)}, u32[]{:S(2)}, u32[]{:S(2)}) collective-permute-start(bf16[320,960]{1,0:T(8,128)(2,1)} %bitcast.32), channel_id=1, source_target_pairs={{0,16},{1,17},{2,18},{3,19},{4,20},{5,21},{6,22},{7,23},{8,24},{9,... | collective-permute-start | bytes 1843208 | tf_op jit(solution)/shard_map/ppermute | solution.py:472
  24.4 2.7 %pack_far.1 = (bf16[1,2,2,80,1024]{4,3,2,1,0:T(8,128)(2,1)}, bf16[1,2,2,80,704]{4,3,2,1,0:T(8,128)(2,1)}) custom-call(s32[2]{0:T(128)} %pad_add_fusion.place_ref, bf16[2,2,80,1728]{3,2,1,0:T(8,128)(2,1)} %get-tuple-element.203.refs_0_, bf16[2,2,80,1728]{3,2,1,0:T(8,128)(2,1)} %collective-permute-done.3.refs_1_), custom_call_target="tpu_custom_call" | custom-call | flops 1 | bytes 1 | tf_op jit(solution)/shard_map/pack_far/pallas_call | solution.py:40
  27.1 1.6 collective-permute-start.4
  29.6 11.8 %permute_columns.3 = (f32[512,2560]{1,0:T(8,128)}, bf16[512,2560]{1,0:T(8,128)(2,1)S(1)}) custom-call(bf16[512,2560]{1,0:T(8,128)(2,1)S(1)} %copy-done.4, s32[1,2560]{1,0:T(1,128)S(1)} %add.144.at_ref, f32[1,2560]{1,0:T(1,128)S(1)} %broadcast_in_dim_reshape.2.refs_0_), custom_call_target="tpu_custom_call" | custom-call | flops 1 | bytes 1 | tf_op jit(solution)/shard_map/permute_columns/pallas_call | solution.py:146
  43.5 2.9 %join_gateup.2 = (bf16[4,80,1024]{2,1,0:T(8,128)(2,1)}, bf16[4,80,1024]{2,1,0:T(8,128)(2,1)}) custom-call(s32[2]{0:T(128)} %pad_add_fusion.place_ref, bf16[2,2,80,1728]{3,2,1,0:T(8,128)(2,1)} %get-tuple-element.203.refs_0_, bf16[2,2,80,1728]{3,2,1,0:T(8,128)(2,1)} %collective-permute-done.3.refs_1_, bf16[1,2,2,80,1024]{4,3,2,1,0:T(8,128)(2,1)} %bitcast.3.refs_2_), custom_call_target="tpu_custom_call" | custom-call | flops 1 | bytes 1 | tf_op jit(solution)/shard_map/join_gateup/pallas_call | solution.py:40
  46.4 3.9 %collective-permute-done.6 = bf16[320,960]{1,0:T(8,128)(2,1)} collective-permute-done((bf16[320,960]{1,0:T(8,128)(2,1)}, bf16[320,960]{1,0:T(8,128)(2,1)}, u32[]{:S(2)}, u32[]{:S(2)}) %collective-permute-start.6) | collective-permute-done | bytes 614432 | tf_op jit(solution)/shard_map/ppermute | solution.py:472
  50.3 2.4 collective-permute-done.7
  56.7 2.6 %collective-permute-start.9 = (bf16[320,1024]{1,0:T(8,128)(2,1)}, bf16[320,1024]{1,0:T(8,128)(2,1)S(1)}, u32[]{:S(2)}, u32[]{:S(2)}) collective-permute-start(bf16[320,1024]{1,0:T(8,128)(2,1)} %bitcast.24), channel_id=1, source_target_pairs={{0,16},{1,17},{2,18},{3,19},{4,20},{5,21},{6,22},{7,23},{8,24},{9,... | collective-permute-start | bytes 1966088 | tf_op jit(solution)/shard_map/ppermute | solution.py:472
  61.4 6.2 %class_rows.1 = (bf16[864,2560]{1,0:T(8,128)(2,1)S(1)}, bf16[864,2560]{1,0:T(8,128)(2,1)}) custom-call(s32[2]{0:T(128)S(1)} %copy-done.20, bf16[1728,2560]{1,0:T(8,128)(2,1)} %weight_ref), custom_call_target="tpu_custom_call" | custom-call | flops 1 | bytes 1 | tf_op jit(solution)/shard_map/class_rows/pallas_call | solution.py:146
  67.6 2.2 copy-done.2
  69.7 12.1 %permute_columns.4.out_in_ref = bf16[640,2560]{1,0:T(8,128)(2,1)S(1)} custom-call(bf16[640,2560]{1,0:T(8,128)(2,1)} %values_ref.1, s32[1,2560]{1,0:T(1,128)S(1)} %broadcast_in_dim.8.at_ref), custom_call_target="tpu_custom_call" | custom-call | flops 1 | bytes 1 | tf_op jit(solution)/shard_map/permute_columns/pallas_call | solution.py:146
  81.9 1.7 copy-done.3
  85.8 2.8 %join_gateup.3 = (bf16[4,80,704]{2,1,0:T(8,128)(2,1)}, bf16[4,80,704]{2,1,0:T(8,128)(2,1)}) custom-call(s32[2]{0:T(128)} %pad_add_fusion.place_ref, bf16[2,2,80,1728]{3,2,1,0:T(8,128)(2,1)} %get-tuple-element.203.refs_0_, bf16[2,2,80,1728]{3,2,1,0:T(8,128)(2,1)} %collective-permute-done.3.refs_1_, bf16[1,2,2,80,704]{4,3,2,1,0:T(8,128)(2,1)} %bitcast.11.refs_2_), custom_call_target="tpu_custom_call" | custom-call | flops 1 | bytes 1 | tf_op jit(solution)/shard_map/join_gateup/pallas_call | solution.py:40
  89.6 1.7 collective-permute-start.13
  98.6 3.5 %fusion = f32[512,960]{0,1:T(8,128)} fusion(bf16[1920,960]{1,0:T(8,128)(2,1)S(1)} %constant_dynamic-update-slice_fusion, bf16[512,2560]{1,0:T(8,128)(2,1)S(1)} %copy-done.19), kind=kOutput, calls=%fused_computation.5 | convolution fusion | flops 1887436800 | bytes 7864320 | tf_op jit(solution)/shard_map/dot_general | solution.py:26
  103.9 5.4 %collective-permute-done.15.refs_4_ = bf16[320,704]{1,0:T(8,128)(2,1)} collective-permute-done((bf16[320,704]{1,0:T(8,128)(2,1)}, bf16[320,704]{1,0:T(8,128)(2,1)}, u32[]{:S(2)}, u32[]{:S(2)}) %collective-permute-start.15) | collective-permute-done | bytes 450592 | tf_op jit(solution)/shard_map/ppermute | solution.py:472
  109.3 2.1 collective-permute-done.16.refs_1_
  115.1 1.8 collective-permute-start.19
  118.3 2.9 %copy.19.joined_ref = f32[512,960]{1,0:T(8,128)} copy(f32[512,960]{0,1:T(8,128)} %fusion) | data formatting | bytes 3932160 | tf_op jit(solution)/shard_map/optimization_barrier | solution.py:478
  123.4 16.5 %attend.1 = (bf16[256,2560]{1,0:T(8,128)(2,1)}, f32[256,2560]{1,0:T(8,128)}, bf16[256,640]{1,0:T(8,128)(2,1)S(1)}, bf16[256,640]{1,0:T(8,128)(2,1)}) custom-call(s32[2]{0:T(128)S(1)} %copy-done.21, s32[1]{0:T(128)} %copy.28.length_ref, s32[8]{0:T(128)S(1)} %get-tuple-element.224.chosen_ref, f32[512,960]{1,0:T(8,128)} %copy.19.joined_ref, ...), custom_call_target="tpu_custom_call" | custom-call | flops 1 | bytes 1 | tf_op jit(solution)/shard_map/attend/pallas_call | solution.py:146
  140.7 1.7 collective-permute-done.19.refs_6_
  145.3 2.4 collective-permute-start.21
  147.9 1.7 copy-done.5
  152.4 10.3 %collective-permute-done.21.refs_1_ = bf16[256,640]{1,0:T(8,128)(2,1)} collective-permute-done((bf16[256,640]{1,0:T(8,128)(2,1)}, bf16[256,640]{1,0:T(8,128)(2,1)}, u32[]{:S(2)}, u32[]{:S(2)}) %collective-permute-start.21) | collective-permute-done | bytes 327712 | tf_op jit(solution)/shard_map/ppermute | solution.py:472
  162.7 7.7 %collective-permute-done.23.refs_3_.refs_5_ = bf16[320,704]{1,0:T(8,128)(2,1)} collective-permute-done((bf16[320,704]{1,0:T(8,128)(2,1)}, bf16[320,704]{1,0:T(8,128)(2,1)}, u32[]{:S(2)}, u32[]{:S(2)}) %collective-permute-start.23) | collective-permute-done | bytes 450592 | tf_op jit(solution)/shard_map/ppermute | solution.py:472
  171.9 2.0 collective-permute-start.31
  177.7 5.1 %permute_columns.5 = f32[256,2560]{1,0:T(8,128)S(1)} custom-call(bf16[256,2560]{1,0:T(8,128)(2,1)S(1)} %pad_maximum_fusion.2.values_ref, s32[1,2560]{1,0:T(1,128)S(1)} %add.153.at_ref), custom_call_target="tpu_custom_call" | custom-call | flops 1 | bytes 1 | tf_op jit(solution)/shard_map/permute_columns/pallas_call | solution.py:146
  184.1 16.5 %collective-permute-done.28.refs_3_ = bf16[320,704]{1,0:T(8,128)(2,1)S(1)} collective-permute-done((bf16[320,704]{1,0:T(8,128)(2,1)}, bf16[320,704]{1,0:T(8,128)(2,1)S(1)}, u32[]{:S(2)}, u32[]{:S(2)}) %collective-permute-start.28) | collective-permute-done | bytes 450592 | tf_op jit(solution)/shard_map/ppermute | solution.py:472
  200.6 4.4 %collective-permute-done.29 = bf16[128,2560]{1,0:T(8,128)(2,1)S(1)} collective-permute-done((bf16[128,2560]{1,0:T(8,128)(2,1)S(1)}, bf16[128,2560]{1,0:T(8,128)(2,1)S(1)}, u32[]{:S(2)}, u32[]{:S(2)}) %collective-permute-start.29) | collective-permute-done | bytes 655392 | tf_op jit(solution)/shard_map/ppermute | solution.py:472
  205.7 2.0 assemble.2.weight_ref
  207.8 1.5 gated.6
  210.3 6.0 %collective-permute-done.35.refs_7_ = bf16[320,704]{1,0:T(8,128)(2,1)S(1)} collective-permute-done((bf16[320,704]{1,0:T(8,128)(2,1)}, bf16[320,704]{1,0:T(8,128)(2,1)S(1)}, u32[]{:S(2)}, u32[]{:S(2)}) %collective-permute-start.35) | collective-permute-done | bytes 450592 | tf_op jit(solution)/shard_map/ppermute | solution.py:472
  216.3 1.7 assemble.3.weight_ref
  221.3 2.6 %gated.7 = bf16[512,352]{1,0:T(8,128)(2,1)S(1)} custom-call(bf16[512,2560]{1,0:T(8,128)(2,1)S(1)} %pad_maximum_fusion.1.tokens_ref, bf16[2560,704]{1,0:T(8,128)(2,1)S(1)} %assemble.3.weight_ref), custom_call_target="tpu_custom_call" | custom-call | flops 1 | bytes 1 | tf_op jit(solution)/shard_map/gated/pallas_call | solution.py:146
  225.0 2.6 %gated.9.refs_1_ = bf16[512,352]{1,0:T(8,128)(2,1)S(1)} custom-call(bf16[512,2560]{1,0:T(8,128)(2,1)S(1)} %pad_maximum_fusion.tokens_ref, bf16[2560,704]{1,0:T(8,128)(2,1)S(1)} %assemble.3.weight_ref), custom_call_target="tpu_custom_call" | custom-call | flops 1 | bytes 1 | tf_op jit(solution)/shard_map/gated/pallas_call | solution.py:146
  227.7 3.0 %gated.8.refs_0_ = bf16[512,512]{1,0:T(8,128)(2,1)S(1)} custom-call(bf16[512,2560]{1,0:T(8,128)(2,1)S(1)} %pad_maximum_fusion.tokens_ref, bf16[2560,1024]{1,0:T(8,128)(2,1)S(1)} %assemble.2.weight_ref), custom_call_target="tpu_custom_call" | custom-call | flops 1 | bytes 1 | tf_op jit(solution)/shard_map/gated/pallas_call | solution.py:146
  230.8 1.7 rows_product.8.refs_2_
  232.5 1.7 rows_product.6.refs_2_
  237.7 1.7 collective-permute-start.41
  241.0 1.6 collective-permute-start.40
  242.6 13.1 %collective-permute-done.41.refs_4_ = bf16[256,640]{1,0:T(8,128)(2,1)S(1)} collective-permute-done((bf16[256,640]{1,0:T(8,128)(2,1)S(1)}, bf16[256,640]{1,0:T(8,128)(2,1)S(1)}, u32[]{:S(2)}, u32[]{:S(2)}) %collective-permute-start.41) | collective-permute-done | bytes 327712 | tf_op jit(solution)/shard_map/ppermute | solution.py:472
  (201 shorter events, 58.4 us)
Async XLA Ops:
  0.6 23.1 %copy-start = (s32[32]{0:T(128)S(1)}, s32[32]{0:T(128)}, u32[]{:S(2)}) copy-start(s32[32]{0:T(128)} %param.15) | copy-start | bytes 388
  3.8 8.5 %collective-permute-start = (bf16[80,960]{1,0:T(8,128)(2,1)}, bf16[80,960]{1,0:T(8,128)(2,1)S(1)}, u32[]{:S(2)}, u32[]{:S(2)}) collective-permute-start(bf16[80,960]{1,0:T(8,128)(2,1)} %get-tuple-element.181), channel_id=1, source_target_pairs={{0,1},{1,0},{2,3},{3,2},{4,5},{5,4},{6,7},{7,6},{8,9},{9,8},{10,11... | collective-permute-start | bytes 460808 | tf_op jit(solution)/shard_map/ppermute | solution.py:472
  4.3 8.0 %collective-permute-start.1 = (bf16[80,960]{1,0:T(8,128)(2,1)}, bf16[80,960]{1,0:T(8,128)(2,1)S(1)}, u32[]{:S(2)}, u32[]{:S(2)}) collective-permute-start(bf16[80,960]{1,0:T(8,128)(2,1)} %get-tuple-element.182), channel_id=1, source_target_pairs={{0,2},{1,3},{2,0},{3,1},{4,6},{5,7},{6,4},{7,5},{8,10},{9,11},{10,... | collective-permute-start | bytes 460808 | tf_op jit(solution)/shard_map/ppermute | solution.py:472
  6.9 8.4 %collective-permute-start.2 = (bf16[80,960]{1,0:T(8,128)(2,1)}, bf16[80,960]{1,0:T(8,128)(2,1)}, u32[]{:S(2)}, u32[]{:S(2)}) collective-permute-start(bf16[80,960]{1,0:T(8,128)(2,1)} %get-tuple-element.183), channel_id=1, source_target_pairs={{0,3},{1,2},{2,1},{3,0},{4,7},{5,6},{6,5},{7,4},{8,11},{9,10},{10,... | collective-permute-start | bytes 460808 | tf_op jit(solution)/shard_map/ppermute | solution.py:472
  15.2 9.1 %collective-permute-start.3 = (bf16[2,2,80,1728]{3,2,1,0:T(8,128)(2,1)}, bf16[2,2,80,1728]{3,2,1,0:T(8,128)(2,1)}, u32[]{:S(2)}, u32[]{:S(2)}) collective-permute-start(bf16[2,2,80,1728]{3,2,1,0:T(8,128)(2,1)} %get-tuple-element.185), channel_id=1, source_target_pairs={{0,1},{1,0},{2,3},{3,2},{4,5},{5,4},{6,7},{7,6},{8,9},{9,8},{10,11... | collective-permute-start | bytes 3317768 | tf_op jit(solution)/shard_map/ppermute | solution.py:472
  17.7 28.7 %collective-permute-start.5 = (bf16[320,960]{1,0:T(8,128)(2,1)}, bf16[320,960]{1,0:T(8,128)(2,1)}, u32[]{:S(2)}, u32[]{:S(2)}) collective-permute-start(bf16[320,960]{1,0:T(8,128)(2,1)} %bitcast.30), channel_id=1, source_target_pairs={{0,4},{1,5},{2,6},{3,7},{4,0},{5,1},{6,2},{7,3},{8,12},{9,13},{10,... | collective-permute-start | bytes 1843208 | tf_op jit(solution)/shard_map/ppermute | solution.py:472
  19.5 30.8 %collective-permute-start.6 = (bf16[320,960]{1,0:T(8,128)(2,1)}, bf16[320,960]{1,0:T(8,128)(2,1)}, u32[]{:S(2)}, u32[]{:S(2)}) collective-permute-start(bf16[320,960]{1,0:T(8,128)(2,1)} %bitcast.31), channel_id=1, source_target_pairs={{0,8},{1,9},{2,10},{3,11},{4,12},{5,13},{6,14},{7,15},{8,0},{9,1},... | collective-permute-start | bytes 1843208 | tf_op jit(solution)/shard_map/ppermute | solution.py:472
  21.1 31.6 %collective-permute-start.7 = (bf16[320,960]{1,0:T(8,128)(2,1)}, bf16[320,960]{1,0:T(8,128)(2,1)}, u32[]{:S(2)}, u32[]{:S(2)}) collective-permute-start(bf16[320,960]{1,0:T(8,128)(2,1)} %bitcast.32), channel_id=1, source_target_pairs={{0,16},{1,17},{2,18},{3,19},{4,20},{5,21},{6,22},{7,23},{8,24},{9,... | collective-permute-start | bytes 1843208 | tf_op jit(solution)/shard_map/ppermute | solution.py:472
  27.1 16.4 %collective-permute-start.4 = (bf16[2,2,80,1024]{3,2,1,0:T(8,128)(2,1)}, bf16[2,2,80,1024]{3,2,1,0:T(8,128)(2,1)}, u32[]{:S(2)}, u32[]{:S(2)}) collective-permute-start(bf16[2,2,80,1024]{3,2,1,0:T(8,128)(2,1)} %bitcast.35), channel_id=1, source_target_pairs={{0,2},{1,3},{2,0},{3,1},{4,6},{5,7},{6,4},{7,5},{8,10},{9,11},{10,... | collective-permute-start | bytes 1966088 | tf_op jit(solution)/shard_map/ppermute | solution.py:472
  29.6 29.7 %copy-start.30 = (s32[32]{0:T(128)S(1)}, s32[32]{0:T(128)}, u32[]{:S(2)}) copy-start(s32[32]{0:T(128)} %param.14) | copy-start | bytes 388
  29.6 31.8 %copy-start.20 = (s32[2]{0:T(128)S(1)}, s32[2]{0:T(128)}, u32[]{:S(2)}) copy-start(s32[2]{0:T(128)} %pad_add_fusion.place_ref) | copy-start | bytes 28
  52.7 35.8 %collective-permute-start.11 = (bf16[320,960]{1,0:T(8,128)(2,1)}, bf16[320,960]{1,0:T(8,128)(2,1)}, u32[]{:S(2)}, u32[]{:S(2)}) collective-permute-start(bf16[320,960]{1,0:T(8,128)(2,1)} %collective-permute-done.7), channel_id=1, source_target_pairs={{0,4},{1,5},{2,6},{3,7},{4,0},{5,1},{6,2},{7,3},{8,12},{9,13},{10,... | collective-permute-start | bytes 1843208 | tf_op jit(solution)/shard_map/ppermute | solution.py:472
  53.3 35.3 %collective-permute-start.12 = (bf16[320,960]{1,0:T(8,128)(2,1)}, bf16[320,960]{1,0:T(8,128)(2,1)}, u32[]{:S(2)}, u32[]{:S(2)}) collective-permute-start(bf16[320,960]{1,0:T(8,128)(2,1)} %collective-permute-done.7), channel_id=1, source_target_pairs={{0,8},{1,9},{2,10},{3,11},{4,12},{5,13},{6,14},{7,15},{8,0},{9,1},... | collective-permute-start | bytes 1843208 | tf_op jit(solution)/shard_map/ppermute | solution.py:472
  53.7 32.1 %collective-permute-start.8 = (bf16[2,2,80,704]{3,2,1,0:T(8,128)(2,1)}, bf16[2,2,80,704]{3,2,1,0:T(8,128)(2,1)}, u32[]{:S(2)}, u32[]{:S(2)}) collective-permute-start(bf16[2,2,80,704]{3,2,1,0:T(8,128)(2,1)} %bitcast.10), channel_id=1, source_target_pairs={{0,2},{1,3},{2,0},{3,1},{4,6},{5,7},{6,4},{7,5},{8,10},{9,11},{10,... | collective-permute-start | bytes 1351688 | tf_op jit(solution)/shard_map/ppermute | solution.py:472
  55.2 33.4 %collective-permute-start.10 = (bf16[320,960]{1,0:T(8,128)(2,1)}, bf16[320,960]{1,0:T(8,128)(2,1)}, u32[]{:S(2)}, u32[]{:S(2)}) collective-permute-start(bf16[320,960]{1,0:T(8,128)(2,1)} %collective-permute-done.6), channel_id=1, source_target_pairs={{0,4},{1,5},{2,6},{3,7},{4,0},{5,1},{6,2},{7,3},{8,12},{9,13},{10,... | collective-permute-start | bytes 1843208 | tf_op jit(solution)/shard_map/ppermute | solution.py:472
  56.7 31.9 %collective-permute-start.9 = (bf16[320,1024]{1,0:T(8,128)(2,1)}, bf16[320,1024]{1,0:T(8,128)(2,1)S(1)}, u32[]{:S(2)}, u32[]{:S(2)}) collective-permute-start(bf16[320,1024]{1,0:T(8,128)(2,1)} %bitcast.24), channel_id=1, source_target_pairs={{0,16},{1,17},{2,18},{3,19},{4,20},{5,21},{6,22},{7,23},{8,24},{9,... | collective-permute-start | bytes 1966088 | tf_op jit(solution)/shard_map/ppermute | solution.py:472
  88.6 26.0 %copy-start.10 = (bf16[320,1024]{1,0:T(8,128)(2,1)}, bf16[320,1024]{1,0:T(8,128)(2,1)S(1)}, u32[]{:S(2)}) copy-start(bf16[320,1024]{1,0:T(8,128)(2,1)S(1)} %collective-permute-done.9.refs_4_) | copy-start | bytes 1966084
  88.6 14.4 %collective-permute-start.14 = (bf16[320,704]{1,0:T(8,128)(2,1)}, bf16[320,704]{1,0:T(8,128)(2,1)S(1)}, u32[]{:S(2)}, u32[]{:S(2)}) collective-permute-start(bf16[320,704]{1,0:T(8,128)(2,1)} %bitcast.27), channel_id=1, source_target_pairs={{0,4},{1,5},{2,6},{3,7},{4,0},{5,1},{6,2},{7,3},{8,12},{9,13},{10,... | collective-permute-start | bytes 1351688 | tf_op jit(solution)/shard_map/ppermute | solution.py:472
  89.2 20.1 %collective-permute-start.15 = (bf16[320,704]{1,0:T(8,128)(2,1)}, bf16[320,704]{1,0:T(8,128)(2,1)}, u32[]{:S(2)}, u32[]{:S(2)}) collective-permute-start(bf16[320,704]{1,0:T(8,128)(2,1)} %bitcast.28), channel_id=1, source_target_pairs={{0,16},{1,17},{2,18},{3,19},{4,20},{5,21},{6,22},{7,23},{8,24},{9,... | collective-permute-start | bytes 1351688 | tf_op jit(solution)/shard_map/ppermute | solution.py:472
  89.6 23.5 %collective-permute-start.13 = (bf16[320,1024]{1,0:T(8,128)(2,1)}, bf16[320,1024]{1,0:T(8,128)(2,1)}, u32[]{:S(2)}, u32[]{:S(2)}) collective-permute-start(bf16[320,1024]{1,0:T(8,128)(2,1)} %bitcast.34), channel_id=1, source_target_pairs={{0,8},{1,9},{2,10},{3,11},{4,12},{5,13},{6,14},{7,15},{8,0},{9,1},... | collective-permute-start | bytes 1966088 | tf_op jit(solution)/shard_map/ppermute | solution.py:472
  91.3 20.1 %collective-permute-start.16 = (bf16[320,960]{1,0:T(8,128)(2,1)}, bf16[320,960]{1,0:T(8,128)(2,1)S(1)}, u32[]{:S(2)}, u32[]{:S(2)}) collective-permute-start(bf16[320,960]{1,0:T(8,128)(2,1)} %collective-permute-done.12.refs_0_), channel_id=1, source_target_pairs={{0,4},{1,5},{2,6},{3,7},{4,0},{5,1},{6,2},{7,3},{8,12},{9,13},{10,... | collective-permute-start | bytes 1843208 | tf_op jit(solution)/shard_map/ppermute | solution.py:472
  113.1 27.6 %collective-permute-start.17 = (bf16[320,1024]{1,0:T(8,128)(2,1)S(1)}, bf16[320,1024]{1,0:T(8,128)(2,1)}, u32[]{:S(2)}, u32[]{:S(2)}) collective-permute-start(bf16[320,1024]{1,0:T(8,128)(2,1)S(1)} %bitcast.25), channel_id=1, source_target_pairs={{0,4},{1,5},{2,6},{3,7},{4,0},{5,1},{6,2},{7,3},{8,12},{9,13},{10,... | collective-permute-start | bytes 1966088 | tf_op jit(solution)/shard_map/ppermute | solution.py:472
  114.6 26.1 %collective-permute-start.18 = (bf16[320,1024]{1,0:T(8,128)(2,1)S(1)}, bf16[320,1024]{1,0:T(8,128)(2,1)}, u32[]{:S(2)}, u32[]{:S(2)}) collective-permute-start(bf16[320,1024]{1,0:T(8,128)(2,1)S(1)} %collective-permute-done.9.refs_4_), channel_id=1, source_target_pairs={{0,4},{1,5},{2,6},{3,7},{4,0},{5,1},{6,2},{7,3},{8,12},{9,13},{10,... | collective-permute-start | bytes 1966088 | tf_op jit(solution)/shard_map/ppermute | solution.py:472
  115.1 27.3 %collective-permute-start.19 = (bf16[320,1024]{1,0:T(8,128)(2,1)}, bf16[320,1024]{1,0:T(8,128)(2,1)}, u32[]{:S(2)}, u32[]{:S(2)}) collective-permute-start(bf16[320,1024]{1,0:T(8,128)(2,1)} %collective-permute-done.13.refs_2_), channel_id=1, source_target_pairs={{0,16},{1,17},{2,18},{3,19},{4,20},{5,21},{6,22},{7,23},{8,24},{9,... | collective-permute-start | bytes 1966088 | tf_op jit(solution)/shard_map/ppermute | solution.py:472
  116.9 23.8 %collective-permute-start.20 = (bf16[320,704]{1,0:T(8,128)(2,1)}, bf16[320,704]{1,0:T(8,128)(2,1)}, u32[]{:S(2)}, u32[]{:S(2)}) collective-permute-start(bf16[320,704]{1,0:T(8,128)(2,1)} %bitcast.13), channel_id=1, source_target_pairs={{0,8},{1,9},{2,10},{3,11},{4,12},{5,13},{6,14},{7,15},{8,0},{9,1},... | collective-permute-start | bytes 1351688 | tf_op jit(solution)/shard_map/ppermute | solution.py:472
  142.4 5.5 %collective-permute-start.25 = (bf16[256,2560]{1,0:T(8,128)(2,1)}, bf16[256,2560]{1,0:T(8,128)(2,1)S(1)}, u32[]{:S(2)}, u32[]{:S(2)}) collective-permute-start(bf16[256,2560]{1,0:T(8,128)(2,1)} %get-tuple-element.269), channel_id=1, source_target_pairs={{0,1},{1,0},{2,3},{3,2},{4,5},{5,4},{6,7},{7,6},{8,9},{9,8},{10,11... | collective-permute-start | bytes 3932168 | tf_op jit(solution)/shard_map/ppermute | solution.py:472
  142.4 28.0 %collective-permute-start.22 = (bf16[320,1024]{1,0:T(8,128)(2,1)}, bf16[320,1024]{1,0:T(8,128)(2,1)S(1)}, u32[]{:S(2)}, u32[]{:S(2)}) collective-permute-start(bf16[320,1024]{1,0:T(8,128)(2,1)} %collective-permute-done.13.refs_2_), channel_id=1, source_target_pairs={{0,4},{1,5},{2,6},{3,7},{4,0},{5,1},{6,2},{7,3},{8,12},{9,13},{10,... | collective-permute-start | bytes 1966088 | tf_op jit(solution)/shard_map/ppermute | solution.py:472
  143.8 26.6 %collective-permute-start.23 = (bf16[320,704]{1,0:T(8,128)(2,1)}, bf16[320,704]{1,0:T(8,128)(2,1)}, u32[]{:S(2)}, u32[]{:S(2)}) collective-permute-start(bf16[320,704]{1,0:T(8,128)(2,1)} %collective-permute-done.15.refs_4_), channel_id=1, source_target_pairs={{0,4},{1,5},{2,6},{3,7},{4,0},{5,1},{6,2},{7,3},{8,12},{9,13},{10,... | collective-permute-start | bytes 1351688 | tf_op jit(solution)/shard_map/ppermute | solution.py:472
  144.4 26.0 %collective-permute-start.24 = (bf16[320,704]{1,0:T(8,128)(2,1)}, bf16[320,704]{1,0:T(8,128)(2,1)}, u32[]{:S(2)}, u32[]{:S(2)}) collective-permute-start(bf16[320,704]{1,0:T(8,128)(2,1)} %collective-permute-done.20.refs_2_), channel_id=1, source_target_pairs={{0,16},{1,17},{2,18},{3,19},{4,20},{5,21},{6,22},{7,23},{8,24},{9,... | collective-permute-start | bytes 1351688 | tf_op jit(solution)/shard_map/ppermute | solution.py:472
  145.3 17.4 %collective-permute-start.21 = (bf16[256,640]{1,0:T(8,128)(2,1)}, bf16[256,640]{1,0:T(8,128)(2,1)}, u32[]{:S(2)}, u32[]{:S(2)}) collective-permute-start(bf16[256,640]{1,0:T(8,128)(2,1)} %get-tuple-element.257), channel_id=1, source_target_pairs={{0,8},{1,9},{2,10},{3,11},{4,12},{5,13},{6,14},{7,15},{8,0},{9,1},... | collective-permute-start | bytes 983048 | tf_op jit(solution)/shard_map/ppermute | solution.py:472
  151.9 19.4 %collective-permute-start.26 = (bf16[128,2560]{1,0:T(8,128)(2,1)}, bf16[128,2560]{1,0:T(8,128)(2,1)S(1)}, u32[]{:S(2)}, u32[]{:S(2)}) collective-permute-start(bf16[128,2560]{1,0:T(8,128)(2,1)} %get-tuple-element.272), channel_id=1, source_target_pairs={{0,2},{1,3},{2,0},{3,1},{4,6},{5,7},{6,4},{7,5},{8,10},{9,11},{10,... | collective-permute-start | bytes 1966088 | tf_op jit(solution)/shard_map/ppermute | solution.py:472
  171.8 33.2 %collective-permute-start.30 = (bf16[128,2560]{1,0:T(8,128)(2,1)S(1)}, bf16[128,2560]{1,0:T(8,128)(2,1)S(1)}, u32[]{:S(2)}, u32[]{:S(2)}) collective-permute-start(bf16[128,2560]{1,0:T(8,128)(2,1)S(1)} %get-tuple-element.295), channel_id=1, source_target_pairs={{0,8},{1,9},{2,10},{3,11},{4,12},{5,13},{6,14},{7,15},{8,0},{9,1},... | collective-permute-start | bytes 1966088 | tf_op jit(solution)/shard_map/ppermute | solution.py:472
  171.9 33.1 %collective-permute-start.31 = (bf16[128,2560]{1,0:T(8,128)(2,1)S(1)}, bf16[128,2560]{1,0:T(8,128)(2,1)S(1)}, u32[]{:S(2)}, u32[]{:S(2)}) collective-permute-start(bf16[128,2560]{1,0:T(8,128)(2,1)S(1)} %get-tuple-element.295), channel_id=1, source_target_pairs={{0,10},{1,11},{2,8},{3,9},{4,14},{5,15},{6,12},{7,13},{8,2},{9,3},... | collective-permute-start | bytes 1966088 | tf_op jit(solution)/shard_map/ppermute | solution.py:472
  173.9 26.6 %collective-permute-start.27 = (bf16[320,1024]{1,0:T(8,128)(2,1)}, bf16[320,1024]{1,0:T(8,128)(2,1)S(1)}, u32[]{:S(2)}, u32[]{:S(2)}) collective-permute-start(bf16[320,1024]{1,0:T(8,128)(2,1)} %collective-permute-done.19.refs_6_), channel_id=1, source_target_pairs={{0,4},{1,5},{2,6},{3,7},{4,0},{5,1},{6,2},{7,3},{8,12},{9,13},{10,... | collective-permute-start | bytes 1966088 | tf_op jit(solution)/shard_map/ppermute | solution.py:472
  175.4 29.6 %collective-permute-start.29 = (bf16[128,2560]{1,0:T(8,128)(2,1)S(1)}, bf16[128,2560]{1,0:T(8,128)(2,1)S(1)}, u32[]{:S(2)}, u32[]{:S(2)}) collective-permute-start(bf16[128,2560]{1,0:T(8,128)(2,1)S(1)} %get-tuple-element.299), channel_id=1, source_target_pairs={{0,2},{1,3},{2,0},{3,1},{4,6},{5,7},{6,4},{7,5},{8,10},{9,11},{10,... | collective-permute-start | bytes 1966088 | tf_op jit(solution)/shard_map/ppermute | solution.py:472
  176.9 23.6 %collective-permute-start.28 = (bf16[320,704]{1,0:T(8,128)(2,1)}, bf16[320,704]{1,0:T(8,128)(2,1)S(1)}, u32[]{:S(2)}, u32[]{:S(2)}) collective-permute-start(bf16[320,704]{1,0:T(8,128)(2,1)} %collective-permute-done.20.refs_2_), channel_id=1, source_target_pairs={{0,4},{1,5},{2,6},{3,7},{4,0},{5,1},{6,2},{7,3},{8,12},{9,13},{10,... | collective-permute-start | bytes 1351688 | tf_op jit(solution)/shard_map/ppermute | solution.py:472
  182.8 22.9 %copy-start.9 = (bf16[4,80,1024]{2,1,0:T(8,128)(2,1)S(1)}, bf16[4,80,1024]{2,1,0:T(8,128)(2,1)}, u32[]{:S(2)}) copy-start(bf16[4,80,1024]{2,1,0:T(8,128)(2,1)} %get-tuple-element.190) | copy-start | bytes 1966084
  182.8 22.9 %copy-start.11 = (bf16[320,1024]{1,0:T(8,128)(2,1)S(1)}, bf16[320,1024]{1,0:T(8,128)(2,1)}, u32[]{:S(2)}) copy-start(bf16[320,1024]{1,0:T(8,128)(2,1)} %copy-done.10) | copy-start | bytes 1966084
  205.0 11.3 %collective-permute-start.35 = (bf16[320,704]{1,0:T(8,128)(2,1)}, bf16[320,704]{1,0:T(8,128)(2,1)S(1)}, u32[]{:S(2)}, u32[]{:S(2)}) collective-permute-start(bf16[320,704]{1,0:T(8,128)(2,1)} %hold.1.refs_6_), channel_id=1, source_target_pairs={{0,4},{1,5},{2,6},{3,7},{4,0},{5,1},{6,2},{7,3},{8,12},{9,13},{10,... | collective-permute-start | bytes 1351688 | tf_op jit(solution)/shard_map/ppermute | solution.py:472
  207.8 10.3 %collective-permute-start.33 = (bf16[256,2560]{1,0:T(8,128)(2,1)S(1)}, bf16[256,2560]{1,0:T(8,128)(2,1)S(1)}, u32[]{:S(2)}, u32[]{:S(2)}) collective-permute-start(bf16[256,2560]{1,0:T(8,128)(2,1)S(1)} %constant_dynamic-update-slice_fusion.6.tokens_ref), channel_id=1, source_target_pairs={{0,1},{1,0},{2,3},{3,2},{4,5},{5,4},{6,7},{7,6},{8,9},{9,8},{10,11... | collective-permute-start | bytes 3932168 | tf_op jit(solution)/shard_map/ppermute | solution.py:472
  209.4 10.6 %collective-permute-start.34 = (bf16[256,512]{1,0:T(8,128)(2,1)S(1)}, bf16[256,512]{1,0:T(8,128)(2,1)S(1)}, u32[]{:S(2)}, u32[]{:S(2)}) collective-permute-start(bf16[256,512]{1,0:T(8,128)(2,1)S(1)} %gated.6), channel_id=1, source_target_pairs={{0,8},{1,9},{2,10},{3,11},{4,12},{5,13},{6,14},{7,15},{8,0},{9,1},... | collective-permute-start | bytes 786440 | tf_op jit(solution)/shard_map/ppermute | solution.py:472
  209.9 9.9 %collective-permute-start.32 = (bf16[256,2560]{1,0:T(8,128)(2,1)S(1)}, bf16[256,2560]{1,0:T(8,128)(2,1)S(1)}, u32[]{:S(2)}, u32[]{:S(2)}) collective-permute-start(bf16[256,2560]{1,0:T(8,128)(2,1)S(1)} %pad_maximum_fusion.3), channel_id=1, source_target_pairs={{0,1},{1,0},{2,3},{3,2},{4,5},{5,4},{6,7},{7,6},{8,9},{9,8},{10,11... | collective-permute-start | bytes 3932168 | tf_op jit(solution)/shard_map/ppermute | solution.py:472
  220.0 16.4 %collective-permute-start.37 = (bf16[256,640]{1,0:T(8,128)(2,1)S(1)}, bf16[256,640]{1,0:T(8,128)(2,1)S(1)}, u32[]{:S(2)}, u32[]{:S(2)}) collective-permute-start(bf16[256,640]{1,0:T(8,128)(2,1)S(1)} %pad_maximum_fusion.4), channel_id=1, source_target_pairs={{0,4},{1,5},{2,6},{3,7},{4,0},{5,1},{6,2},{7,3},{8,12},{9,13},{10,... | collective-permute-start | bytes 983048 | tf_op jit(solution)/shard_map/ppermute | solution.py:472
  220.3 15.0 %collective-permute-start.38 = (bf16[256,512]{1,0:T(8,128)(2,1)S(1)}, bf16[256,512]{1,0:T(8,128)(2,1)S(1)}, u32[]{:S(2)}, u32[]{:S(2)}) collective-permute-start(bf16[256,512]{1,0:T(8,128)(2,1)S(1)} %gated.5), channel_id=1, source_target_pairs={{0,8},{1,9},{2,10},{3,11},{4,12},{5,13},{6,14},{7,15},{8,0},{9,1},... | collective-permute-start | bytes 786440 | tf_op jit(solution)/shard_map/ppermute | solution.py:472
  223.9 12.7 %collective-permute-start.36 = (bf16[512,352]{1,0:T(8,128)(2,1)S(1)}, bf16[512,352]{1,0:T(8,128)(2,1)S(1)}, u32[]{:S(2)}, u32[]{:S(2)}) collective-permute-start(bf16[512,352]{1,0:T(8,128)(2,1)S(1)} %gated.7), channel_id=1, source_target_pairs={{0,8},{1,9},{2,10},{3,11},{4,12},{5,13},{6,14},{7,15},{8,0},{9,1},... | collective-permute-start | bytes 1081352 | tf_op jit(solution)/shard_map/ppermute | solution.py:472
  237.6 3.1 %collective-permute-start.39 = (bf16[256,2560]{1,0:T(8,128)(2,1)S(1)}, bf16[256,2560]{1,0:T(8,128)(2,1)S(1)}, u32[]{:S(2)}, u32[]{:S(2)}) collective-permute-start(bf16[256,2560]{1,0:T(8,128)(2,1)S(1)} %rows_product.11), channel_id=1, source_target_pairs={{0,1},{1,0},{2,3},{3,2},{4,5},{5,4},{6,7},{7,6},{8,9},{9,8},{10,11... | collective-permute-start | bytes 3932168 | tf_op jit(solution)/shard_map/ppermute | solution.py:472
  237.7 18.0 %collective-permute-start.41 = (bf16[256,640]{1,0:T(8,128)(2,1)S(1)}, bf16[256,640]{1,0:T(8,128)(2,1)S(1)}, u32[]{:S(2)}, u32[]{:S(2)}) collective-permute-start(bf16[256,640]{1,0:T(8,128)(2,1)S(1)} %pack_pages.1), channel_id=1, source_target_pairs={{0,16},{1,17},{2,18},{3,19},{4,20},{5,21},{6,22},{7,23},{8,24},{9,... | collective-permute-start | bytes 983048 | tf_op jit(solution)/shard_map/ppermute | solution.py:472
  241.0 16.8 %collective-permute-start.40 = (bf16[128,2560]{1,0:T(8,128)(2,1)S(1)}, bf16[128,2560]{1,0:T(8,128)(2,1)S(1)}, u32[]{:S(2)}, u32[]{:S(2)}) collective-permute-start(bf16[128,2560]{1,0:T(8,128)(2,1)S(1)} %get-tuple-element.337), channel_id=1, source_target_pairs={{0,2},{1,3},{2,0},{3,1},{4,6},{5,7},{6,4},{7,5},{8,10},{9,11},{10,... | collective-permute-start | bytes 1966088 | tf_op jit(solution)/shard_map/ppermute | solution.py:472
  (31 other events, 193.1 us)
